TPU v7x, 32 devices: a whole 2x2x4 slice. The times are simulated.
32 devices in a mesh: section: 2 (over y), fsdp: 4 (over x, core), dp: 4 (over z).
Axes of the slice: x: 2, y: 2, z: 4, core: 2. Of those that a mesh axis runs over, the one named last changes fastest.
Arguments:
- images: bfloat16 [32, 65, 384], P(('fsdp', 'dp')), may hold values from -6 to 6
- slot_image: int32 [16, 2], P(('fsdp', 'dp')), may hold values from 0 to 1, each once within a row
- cotangent: bfloat16 [32, 65, 384], P(('fsdp', 'dp')), may hold values from -6 to 6
- pre_gain: bfloat16 [2, 384], P('section', 'fsdp'), may hold values from 0.099609375 to 1.8984375
- pre_shift: bfloat16 [2, 384], P('section', 'fsdp'), may hold values from -1.5 to 1.5
- heads_weight: bfloat16 [2, 384, 1152], P('section', 'fsdp'), may hold values from -0.4375 to 0.4375
- query_bias: bfloat16 [2, 384], P('section', 'fsdp'), may hold values from -1.5 to 1.5
- value_bias: bfloat16 [2, 384], P('section', 'fsdp'), may hold values from -1.5 to 1.5
- merge_weight: bfloat16 [2, 384, 384], P('section', 'fsdp'), may hold values from -0.875 to 0.875
- merge_bias: bfloat16 [2, 384], P('section', 'fsdp'), may hold values from -1.5 to 1.5
- mid_gain: bfloat16 [2, 384], P('section', 'fsdp'), may hold values from 0.099609375 to 1.8984375
- mid_shift: bfloat16 [2, 384], P('section', 'fsdp'), may hold values from -1.5 to 1.5
- up_weight: bfloat16 [2, 384, 1536], P('section', 'fsdp'), may hold values from -0.3125 to 0.3125
- up_bias: bfloat16 [2, 1536], P('section', 'fsdp'), may hold values from -1.5 to 1.5
- down_weight: bfloat16 [2, 1536, 384], P('section', 'fsdp'), may hold values from -0.21875 to 0.21875
- down_bias: bfloat16 [2, 384], P('section', 'fsdp'), may hold values from -1.5 to 1.5
Outputs:
- layer_outputs: bfloat16 [2, 32, 65, 384], P('section', ('fsdp', 'dp'))
- input_grads: float32 [2, 32, 65, 384], P('section', ('fsdp', 'dp'))
- grad_pre_gain: float32 [2, 384], P('section', 'fsdp')
- grad_pre_shift: float32 [2, 384], P('section', 'fsdp')
- grad_heads_weight: float32 [2, 384, 1152], P('section', 'fsdp')
- grad_query_bias: float32 [2, 384], P('section', 'fsdp')
- grad_value_bias: float32 [2, 384], P('section', 'fsdp')
- grad_merge_weight: float32 [2, 384, 384], P('section', 'fsdp')
- grad_merge_bias: float32 [2, 384], P('section', 'fsdp')
- grad_mid_gain: float32 [2, 384], P('section', 'fsdp')
- grad_mid_shift: float32 [2, 384], P('section', 'fsdp')
- grad_up_weight: float32 [2, 384, 1536], P('section', 'fsdp')
- grad_up_bias: float32 [2, 1536], P('section', 'fsdp')
- grad_down_weight: float32 [2, 1536, 384], P('section', 'fsdp')
- grad_down_bias: float32 [2, 384], P('section', 'fsdp')
All inputs are finite; a program needn't handle non-finite values.
Results may differ from a plain program's by a relative error of at most 0.024.
Values may be sent and summed in bfloat16 or wider, within the bound.
No kernel may reach another device: no remote copies, remote signals or barrier semaphores. Data moves between devices by JAX's collectives and lax.ppermute only.
A program may use at most 64 MiB of HBM per device.

v0:
```python
import jax
import jax.numpy as jnp
from jax import lax
from jax.sharding import PartitionSpec as P

HD = 64


EPS = 1e-06
SQRT_HALF = 0.7071067811865476
INV_ROOT_TAU = 0.3989422804014327


def from_behind(block, axis, distance):
    devices = range(lax.axis_size(axis))
    route = [(i - distance, i) for i in devices if i - distance in devices]
    return lax.ppermute(block, axis, route)


def as_sent(value):
    return jax.tree.map(lambda a: a.astype(jnp.bfloat16) if a.dtype == jnp.float32 else a, value)


def norm_forward(rows_in, gain_vec, shift_vec):
    row_mean = jnp.mean(rows_in, axis=-1, keepdims=True)
    centered = rows_in - row_mean
    row_var = jnp.mean(centered * centered, axis=-1, keepdims=True)
    inverse = lax.rsqrt(row_var + EPS)
    normed = centered * inverse
    return (normed * gain_vec + shift_vec, normed, inverse)


def norm_backward(grad_rows, normed, inverse, gain_vec):
    scaled = grad_rows * gain_vec
    mean_one = jnp.mean(scaled, axis=-1, keepdims=True)
    mean_two = jnp.mean(scaled * normed, axis=-1, keepdims=True)
    back_rows = inverse * (scaled - mean_one - normed * mean_two)
    return (back_rows, jnp.sum(grad_rows * normed, axis=0), jnp.sum(grad_rows, axis=0))


def gelu_slope(hidden):
    return (
        0.5 * (1.0 + lax.erf(hidden * SQRT_HALF))
        + hidden * jnp.exp(-0.5 * hidden * hidden) * INV_ROOT_TAU
    )


def attention_scores(queries, key_rows):
    return jnp.einsum(
        "qhd,khd->hqk", queries, key_rows, preferred_element_type=jnp.float32
    ) * HD ** (-0.5)


def layer_forward(inputs, weights):
    (
        pre_gain,
        pre_shift,
        heads_weight,
        query_bias,
        value_bias,
        merge_weight,
        merge_bias,
        mid_gain,
        mid_shift,
        up_weight,
        up_bias,
        down_weight,
        down_bias,
    ) = weights
    length, model_width = inputs.shape
    head_count = model_width // HD
    start_rows = inputs.astype(jnp.float32)
    normed_in, unit_one, inverse_one = norm_forward(
        start_rows, pre_gain.astype(jnp.float32), pre_shift.astype(jnp.float32)
    )
    entry_rows = normed_in.astype(jnp.bfloat16)
    bias_all = jnp.concatenate([query_bias, jnp.zeros_like(query_bias), value_bias]).astype(
        jnp.float32
    )
    packed = (
        jnp.dot(entry_rows, heads_weight, preferred_element_type=jnp.float32) + bias_all
    ).astype(jnp.bfloat16)
    split_heads = packed.reshape(length, 3, head_count, HD)
    scores = attention_scores(split_heads[:, 0], split_heads[:, 1])
    row_top = jnp.max(scores, axis=-1, keepdims=True)
    log_total = jnp.log(jnp.sum(jnp.exp(scores - row_top), axis=-1, keepdims=True)) + row_top
    attn_probs = jnp.exp(scores - log_total).astype(jnp.bfloat16)
    mixed_heads = jnp.einsum(
        "hqk,khd->qhd", attn_probs, split_heads[:, 2], preferred_element_type=jnp.float32
    )
    mixed_heads = mixed_heads.reshape(length, model_width).astype(jnp.bfloat16)
    middle = (
        start_rows
        + jnp.dot(mixed_heads, merge_weight, preferred_element_type=jnp.float32)
        + merge_bias.astype(jnp.float32)
    )
    normed_mid, unit_two, inverse_two = norm_forward(
        middle, mid_gain.astype(jnp.float32), mid_shift.astype(jnp.float32)
    )
    mid_rows = normed_mid.astype(jnp.bfloat16)
    hidden = jnp.dot(mid_rows, up_weight, preferred_element_type=jnp.float32) + up_bias.astype(
        jnp.float32
    )
    activated = jax.nn.gelu(hidden, approximate=False).astype(jnp.bfloat16)
    result = (
        middle
        + jnp.dot(activated, down_weight, preferred_element_type=jnp.float32)
        + down_bias.astype(jnp.float32)
    )
    stashed = (
        entry_rows,
        unit_one,
        inverse_one,
        packed,
        log_total,
        mixed_heads,
        unit_two,
        inverse_two,
        mid_rows,
        hidden,
        activated,
    )
    return (result.astype(jnp.bfloat16), stashed)


def layer_backward(incoming, stashed, weights):
    (
        pre_gain,
        pre_shift,
        heads_weight,
        query_bias,
        value_bias,
        merge_weight,
        merge_bias,
        mid_gain,
        mid_shift,
        up_weight,
        up_bias,
        down_weight,
        down_bias,
    ) = weights
    (
        entry_rows,
        unit_one,
        inverse_one,
        packed,
        log_total,
        mixed_heads,
        unit_two,
        inverse_two,
        mid_rows,
        hidden,
        activated,
    ) = stashed
    length, model_width = incoming.shape
    head_count = model_width // HD
    grad_out = incoming.astype(jnp.float32)
    grad_down_bias = jnp.sum(grad_out, axis=0)
    grad_down = jnp.einsum("sf,sd->fd", activated, incoming, preferred_element_type=jnp.float32)
    grad_act = jnp.einsum("sd,fd->sf", incoming, down_weight, preferred_element_type=jnp.float32)
    grad_hidden = (grad_act * gelu_slope(hidden)).astype(jnp.bfloat16)
    grad_up_bias = jnp.sum(grad_hidden.astype(jnp.float32), axis=0)
    grad_up = jnp.einsum("sd,sf->df", mid_rows, grad_hidden, preferred_element_type=jnp.float32)
    grad_mid_rows = jnp.einsum(
        "sf,df->sd", grad_hidden, up_weight, preferred_element_type=jnp.float32
    )
    back_mid, grad_mid_gain, grad_mid_shift = norm_backward(
        grad_mid_rows, unit_two, inverse_two, mid_gain.astype(jnp.float32)
    )
    grad_middle = grad_out + back_mid
    grad_branch = grad_middle.astype(jnp.bfloat16)
    grad_merge_bias = jnp.sum(grad_branch.astype(jnp.float32), axis=0)
    grad_merge = jnp.einsum(
        "sd,se->de", mixed_heads, grad_branch, preferred_element_type=jnp.float32
    )
    grad_mixed = jnp.einsum(
        "se,de->sd", grad_branch, merge_weight, preferred_element_type=jnp.float32
    )
    grad_mixed = grad_mixed.astype(jnp.bfloat16).reshape(length, head_count, HD)
    split_heads = packed.reshape(length, 3, head_count, HD)
    queries = split_heads[:, 0]
    key_rows = split_heads[:, 1]
    values = split_heads[:, 2]
    exact_probs = jnp.exp(attention_scores(queries, key_rows) - log_total)
    attn_probs = exact_probs.astype(jnp.bfloat16)
    grad_probs = jnp.einsum("qhd,khd->hqk", grad_mixed, values, preferred_element_type=jnp.float32)
    grad_values = jnp.einsum(
        "hqk,qhd->khd", attn_probs, grad_mixed, preferred_element_type=jnp.float32
    )
    inner_sum = jnp.sum(exact_probs * grad_probs, axis=-1, keepdims=True)
    grad_scores = (exact_probs * (grad_probs - inner_sum)).astype(jnp.bfloat16)
    grad_queries = jnp.einsum(
        "hqk,khd->qhd", grad_scores, key_rows, preferred_element_type=jnp.float32
    ) * HD ** (-0.5)
    grad_keys = jnp.einsum(
        "hqk,qhd->khd", grad_scores, queries, preferred_element_type=jnp.float32
    ) * HD ** (-0.5)
    grad_packed = (
        jnp.stack([grad_queries, grad_keys, grad_values], axis=1)
        .reshape(length, 3 * model_width)
        .astype(jnp.bfloat16)
    )
    packed_sums = jnp.sum(grad_packed.astype(jnp.float32), axis=0)
    grad_query_bias = packed_sums[:model_width]
    grad_value_bias = packed_sums[2 * model_width :]
    grad_heads = jnp.einsum(
        "sd,se->de", entry_rows, grad_packed, preferred_element_type=jnp.float32
    )
    grad_entry = jnp.einsum(
        "se,de->sd", grad_packed, heads_weight, preferred_element_type=jnp.float32
    )
    back_in, grad_pre_gain, grad_pre_shift = norm_backward(
        grad_entry, unit_one, inverse_one, pre_gain.astype(jnp.float32)
    )
    grad_input = grad_middle + back_in
    weight_grads = (
        grad_pre_gain,
        grad_pre_shift,
        grad_heads,
        grad_query_bias,
        grad_value_bias,
        grad_merge,
        grad_merge_bias,
        grad_mid_gain,
        grad_mid_shift,
        grad_up,
        grad_up_bias,
        grad_down,
        grad_down_bias,
    )
    return (weight_grads, grad_input)


def choose_side(leading, when_true, when_false):
    return jax.tree.map(
        lambda left_side, right_side: jnp.where(leading, left_side, right_side),
        when_true,
        when_false,
    )


def local(
    images,
    slot_image,
    cotangent,
    pre_gain,
    pre_shift,
    heads_weight,
    query_bias,
    value_bias,
    merge_weight,
    merge_bias,
    mid_gain,
    mid_shift,
    up_weight,
    up_bias,
    down_weight,
    down_bias,
):
    shards = (
        pre_gain,
        pre_shift,
        heads_weight,
        query_bias,
        value_bias,
        merge_weight,
        merge_bias,
        mid_gain,
        mid_shift,
        up_weight,
        up_bias,
        down_weight,
        down_bias,
    )
    leading = lax.axis_index("section") == 0
    micro_count, length, model_width = images.shape
    gathered = (
        lax.all_gather(shards[0], "fsdp", axis=1, tiled=True),
        lax.all_gather(shards[1], "fsdp", axis=1, tiled=True),
        lax.all_gather(shards[2], "fsdp", axis=1, tiled=True),
        lax.all_gather(shards[3], "fsdp", axis=1, tiled=True),
        lax.all_gather(shards[4], "fsdp", axis=1, tiled=True),
        lax.all_gather(shards[5], "fsdp", axis=1, tiled=True),
        lax.all_gather(shards[6], "fsdp", axis=1, tiled=True),
        lax.all_gather(shards[7], "fsdp", axis=1, tiled=True),
        lax.all_gather(shards[8], "fsdp", axis=1, tiled=True),
        lax.all_gather(shards[9], "fsdp", axis=1, tiled=True),
        lax.all_gather(shards[10], "fsdp", axis=1, tiled=True),
        lax.all_gather(shards[11], "fsdp", axis=1, tiled=True),
        lax.all_gather(shards[12], "fsdp", axis=1, tiled=True),
    )
    full_weights = tuple((member[0] for member in gathered))
    pick_matrix = (
        slot_image[0][:, None] == jnp.arange(micro_count, dtype=jnp.int32)[None, :]
    ).astype(jnp.bfloat16)
    ordered = jnp.einsum(
        "mj,jsd->msd", pick_matrix, images, preferred_element_type=jnp.float32
    ).astype(jnp.bfloat16)
    blank_rows = jnp.zeros((length, model_width), jnp.bfloat16)
    arrived = blank_rows
    produced = []
    stash_list = []
    for timestep in range(micro_count + 1):
        own_image = ordered[min(timestep, micro_count - 1)]
        source = jnp.where(leading, own_image, arrived)
        result, stashed = layer_forward(source, full_weights)
        produced.append(result)
        stash_list.append(stashed)
        if timestep < micro_count:
            arrived = from_behind(result, "section", 1)
    layer_outputs = jnp.stack(
        [
            jnp.where(leading, produced[index_m], produced[index_m + 1])
            for index_m in range(micro_count)
        ]
    )
    regathered = (
        lax.all_gather(shards[0], "fsdp", axis=1, tiled=True),
        lax.all_gather(shards[1], "fsdp", axis=1, tiled=True),
        lax.all_gather(shards[2], "fsdp", axis=1, tiled=True),
        lax.all_gather(shards[3], "fsdp", axis=1, tiled=True),
        lax.all_gather(shards[4], "fsdp", axis=1, tiled=True),
        lax.all_gather(shards[5], "fsdp", axis=1, tiled=True),
        lax.all_gather(shards[6], "fsdp", axis=1, tiled=True),
        lax.all_gather(shards[7], "fsdp", axis=1, tiled=True),
        lax.all_gather(shards[8], "fsdp", axis=1, tiled=True),
        lax.all_gather(shards[9], "fsdp", axis=1, tiled=True),
        lax.all_gather(shards[10], "fsdp", axis=1, tiled=True),
        lax.all_gather(shards[11], "fsdp", axis=1, tiled=True),
        lax.all_gather(shards[12], "fsdp", axis=1, tiled=True),
    )
    back_weights = tuple((member[0] for member in regathered))
    returned = blank_rows
    grad_sums = None
    backs = []
    for timestep in range(micro_count + 1):
        before = stash_list[max(timestep - 1, 0)]
        behind = stash_list[min(timestep + 1, micro_count)]
        stashed = choose_side(leading, before, behind)
        low_part = returned if timestep > 0 else blank_rows
        high_part = cotangent[timestep] if timestep < micro_count else blank_rows
        incoming = jnp.where(leading, low_part, high_part)
        weight_grads, grad_input = layer_backward(incoming, stashed, back_weights)
        backs.append(grad_input)
        if timestep < micro_count:
            sent_back = grad_input.astype(jnp.bfloat16)
            returned = from_behind(sent_back, "section", -1)
        grad_sums = (
            weight_grads
            if grad_sums is None
            else tuple((old + new for old, new in zip(grad_sums, weight_grads)))
        )
    grad_sums = jax.tree.map(
        lambda part: part.astype(jnp.float32),
        lax.psum_scatter(
            as_sent(tuple((member[None] for member in grad_sums))),
            "fsdp",
            scatter_dimension=1,
            tiled=True,
        ),
    )
    totals = jax.tree.map(lambda part: part.astype(jnp.float32), lax.psum(as_sent(grad_sums), "dp"))
    input_grads = jnp.stack(
        [
            jnp.where(
                leading, backs[index_m + 1], backs[index_m].astype(jnp.bfloat16).astype(jnp.float32)
            )
            for index_m in range(micro_count)
        ]
    )
    return (
        layer_outputs[None],
        input_grads[None],
        totals[0],
        totals[1],
        totals[2],
        totals[3],
        totals[4],
        totals[5],
        totals[6],
        totals[7],
        totals[8],
        totals[9],
        totals[10],
        totals[11],
        totals[12],
    )


def solution(mesh):
    return jax.shard_map(
        local,
        mesh=mesh,
        in_specs=(
            P(("fsdp", "dp"), None, None),
            P(("fsdp", "dp"), None),
            P(("fsdp", "dp"), None, None),
            P("section", "fsdp"),
            P("section", "fsdp"),
            P("section", "fsdp", None),
            P("section", "fsdp"),
            P("section", "fsdp"),
            P("section", "fsdp", None),
            P("section", "fsdp"),
            P("section", "fsdp"),
            P("section", "fsdp"),
            P("section", "fsdp", None),
            P("section", "fsdp"),
            P("section", "fsdp", None),
            P("section", "fsdp"),
        ),
        out_specs=(
            P("section", ("fsdp", "dp"), None, None),
            P("section", ("fsdp", "dp"), None, None),
            P("section", "fsdp"),
            P("section", "fsdp"),
            P("section", "fsdp", None),
            P("section", "fsdp"),
            P("section", "fsdp"),
            P("section", "fsdp", None),
            P("section", "fsdp"),
            P("section", "fsdp"),
            P("section", "fsdp"),
            P("section", "fsdp", None),
            P("section", "fsdp"),
            P("section", "fsdp", None),
            P("section", "fsdp"),
        ),
        check_vma=False,
    )
```

profile of v0, /device:TPU:0, one launch (start us, length us, event | category | flops | bytes accessed | tf_op | source)
XLA Modules:
  0.0 500.4 jit_solution(1832048927789654863)
XLA Ops:
  17.4 8.9 %all-reduce.10 = (bf16[384]{0:T(512)(128)(2,1)S(1)}, bf16[384]{0:T(512)(128)(2,1)S(1)}, bf16[384]{0:T(512)(128)(2,1)S(1)}, bf16[384]{0:T(512)(128)(2,1)S(1)}, bf...) all-reduce(bf16[384]{0:T(512)(128)(2,1)S(1)} %dynamic-update-slice., ...), channel_id=1, replica_groups=mesh['section'=2,'fsdp'=4,'dp'=4] {'fsdp'}, use_global_device_ids=true, to_apply=%add.3 | all-reduce | flops 3072 | bytes 12288 | tf_op jit(solution)/shard_map/concatenate | solution.py:77
  26.3 8.2 %all_gather.47 = bf16[1,384,1152]{2,1,0:T(8,128)(2,1)S(1)} all-gather(bf16[1,96,1152]{2,1,0:T(8,128)(2,1)} %param.21), channel_id=1, replica_groups=mesh['section'=2,'fsdp'=4,'dp'=4] {'fsdp'}, dimensions={1}, use_global_device_ids=true | all-gather | bytes 1105920 | tf_op jit(solution)/shard_map/all_gather | solution.py:280
  36.9 5.2 %all_gather.55 = bf16[1,1536]{1,0:T(2,128)(2,1)S(1)} all-gather(bf16[1,384]{1,0:T(2,128)(2,1)S(1)} %copy-done.152), channel_id=1, replica_groups=mesh['section'=2,'fsdp'=4,'dp'=4] {'fsdp'}, dimensions={1}, use_global_device_ids=true | all-gather | bytes 3840 | tf_op jit(solution)/shard_map/all_gather | solution.py:288
  42.1 7.8 %all_gather.50 = bf16[1,384,384]{2,1,0:T(8,128)(2,1)S(1)} all-gather(bf16[1,96,384]{2,1,0:T(8,128)(2,1)S(1)} %copy-done.78), channel_id=1, replica_groups=mesh['section'=2,'fsdp'=4,'dp'=4] {'fsdp'}, dimensions={1}, use_global_device_ids=true | all-gather | bytes 368640 | tf_op jit(solution)/shard_map/all_gather | solution.py:283
  51.5 3.2 fusion.91
  56.5 3.5 collective-permute-start
  67.7 4.6 collective-permute-start.1
  107.7 2.4 convert_reduce_fusion.4
  126.9 2.4 collective-permute-done.3
  145.4 2.4 fusion.4
  158.6 22.6 %reduce-scatter.32.cloned.1.call-done = bf16[1,96,1152]{2,1,0:T(8,128)(2,1)} async-done(((bf16[1,384,1152]{2,1,0:T(8,128)(2,1)}), bf16[1,96,1152]{2,1,0:T(8,128)(2,1)}) %reduce-scatter.32.cloned.1.call-update) | async-done | bytes 221200 | tf_op jit(solution)/shard_map/reduce_scatter | solution.py:355
  181.2 28.2 %reduce-scatter.36.cloned.1.call-done = bf16[1,96,1536]{2,1,0:T(8,128)(2,1)} async-done(((bf16[1,384,1536]{2,1,0:T(8,128)(2,1)}), bf16[1,96,1536]{2,1,0:T(8,128)(2,1)}) %reduce-scatter.36.cloned.1.call-update) | async-done | bytes 294928 | tf_op jit(solution)/shard_map/reduce_scatter | solution.py:355
  209.4 28.3 %reduce-scatter.38.cloned.1.call-done = bf16[1,384,384]{2,1,0:T(8,128)(2,1)} async-done(((bf16[1,1536,384]{2,1,0:T(8,128)(2,1)}), bf16[1,384,384]{2,1,0:T(8,128)(2,1)}) %reduce-scatter.38.cloned.1.call-update) | async-done | bytes 294928 | tf_op jit(solution)/shard_map/reduce_scatter | solution.py:355
  239.5 20.8 %reduce-scatter.40.cloned.1.call-done = bf16[96,1]{1,0:T(8,128)(2,1)} async-done(((bf16[384,1]{1,0:T(8,128)(2,1)}), bf16[96,1]{1,0:T(8,128)(2,1)}) %reduce-scatter.40.cloned.1.call-update) | async-done | bytes 208
  261.1 21.2 %reduce-scatter.42.cloned.1.call-done = bf16[96,1]{1,0:T(8,128)(2,1)} async-done(((bf16[384,1]{1,0:T(8,128)(2,1)}), bf16[96,1]{1,0:T(8,128)(2,1)}) %reduce-scatter.42.cloned.1.call-update) | async-done | bytes 208
  283.0 21.2 %reduce-scatter.44.cloned.1.call-done = bf16[96,1]{1,0:T(8,128)(2,1)} async-done(((bf16[384,1]{1,0:T(8,128)(2,1)}), bf16[96,1]{1,0:T(8,128)(2,1)}) %reduce-scatter.44.cloned.1.call-update) | async-done | bytes 208
  305.0 21.0 %reduce-scatter.46.cloned.1.call-done = bf16[96,1]{1,0:T(8,128)(2,1)} async-done(((bf16[384,1]{1,0:T(8,128)(2,1)}), bf16[96,1]{1,0:T(8,128)(2,1)}) %reduce-scatter.46.cloned.1.call-update) | async-done | bytes 208
  326.9 21.2 %reduce-scatter.48.cloned.1.call-done = bf16[96,1]{1,0:T(8,128)(2,1)} async-done(((bf16[384,1]{1,0:T(8,128)(2,1)}), bf16[96,1]{1,0:T(8,128)(2,1)}) %reduce-scatter.48.cloned.1.call-update) | async-done | bytes 208
  348.9 21.1 %reduce-scatter.50.cloned.1.call-done = bf16[96,1]{1,0:T(8,128)(2,1)} async-done(((bf16[384,1]{1,0:T(8,128)(2,1)}), bf16[96,1]{1,0:T(8,128)(2,1)}) %reduce-scatter.50.cloned.1.call-update) | async-done | bytes 208
  370.7 21.2 %reduce-scatter.52.cloned.1.call-done = bf16[96,1]{1,0:T(8,128)(2,1)} async-done(((bf16[384,1]{1,0:T(8,128)(2,1)}), bf16[96,1]{1,0:T(8,128)(2,1)}) %reduce-scatter.52.cloned.1.call-update) | async-done | bytes 208
  392.7 21.0 %reduce-scatter.56.cloned.1.call-done = bf16[96,1]{1,0:T(8,128)(2,1)} async-done(((bf16[384,1]{1,0:T(8,128)(2,1)}), bf16[96,1]{1,0:T(8,128)(2,1)}) %reduce-scatter.56.cloned.1.call-update) | async-done | bytes 208
  414.5 22.9 %reduce-scatter.54.cloned.1.call-done = bf16[384,1]{1,0:T(8,128)(2,1)} async-done(((bf16[1536,1]{1,0:T(8,128)(2,1)}), bf16[384,1]{1,0:T(8,128)(2,1)}) %reduce-scatter.54.cloned.1.call-update) | async-done | bytes 784
  438.5 11.9 %all-reduce.8 = (bf16[1,96]{1,0:T(2,128)(2,1)S(1)}, bf16[1,96]{1,0:T(2,128)(2,1)S(1)}, bf16[1,96]{1,0:T(2,128)(2,1)S(1)}, bf16[1,96]{1,0:T(2,128)(2,1)S(1)}, bf1...) all-reduce(bf16[1,96]{1,0:T(2,128)(2,1)S(1)} %copy.211, ...), channel_id=1, replica_groups=mesh['section'=2,'fsdp'=4,'dp'=4] {'dp'}, use_global_device_ids=true, to_apply=%region_37.38 | all-reduce | flops 1152 | bytes 4608 | tf_op jit(solution)/shard_map/psum | solution.py:362
  455.0 32.9 %all-reduce.13.cloned.1.call-done = (bf16[1,96,1152]{2,1,0:T(8,128)(2,1)}, bf16[1,96,384]{2,1,0:T(8,128)(2,1)}, bf16[1,96,1536]{2,1,0:T(8,128)(2,1)}, bf16[1,384,384]{2,1,0:T(8,128)(2,1)}) async-done(((bf16[1,96,1152]{2,1,0:T(8,128)(2,1)}, bf16[1,96,384]{2,1,0:T(8,128)(2,1)}, bf16[1,96,1536]{2,1,0:T(8,128)(2,1)}, bf16[1,384,384]{2,1,0:T(8,128)(2,1)}), (bf16[1,96,1152]{2,1,0:T(8,128)(2,1)}, ...) | async-done | bytes 884752 | tf_op jit(solution)/shard_map/psum | solution.py:362
  (538 shorter events, 119.5 us)
Async XLA Ops:
  7.2 44.3 %all-gather.3.cloned.1.call-start = ((), (), s32[]{:S(2)}) async-start(), calls=%async_computation.13 | async-start | bytes 1474560 | tf_op jit(solution)/shard_map/all_gather | solution.py:287
  7.9 46.9 %all-gather.5.cloned.1.call-start = ((), (), s32[]{:S(2)}) async-start(), calls=%async_computation.14 | async-start | bytes 1474560 | tf_op jit(solution)/shard_map/all_gather | solution.py:289
  8.7 149.9 %reduce-scatter.34.cloned.1.call-start = ((), (), s32[]{:S(2)}) async-start(), calls=%async_computation.16 | async-start | bytes 368640 | tf_op jit(solution)/shard_map/reduce_scatter | solution.py:355
  56.5 5.3 %collective-permute-start = (bf16[65,384]{1,0:T(8,128)(2,1)S(1)}, bf16[65,384]{1,0:T(8,128)(2,1)S(1)}, u32[]{:S(2)}, u32[]{:S(2)}) collective-permute-start(bf16[65,384]{1,0:T(8,128)(2,1)S(1)} %fusion.65), channel_id=1, source_target_pairs={{0,16},{1,17},{2,18},{3,19},{4,20},{5,21},{6,22},{7,23},{8,24},{9,... | collective-permute-start | bytes 149768 | tf_op jit(solution)/shard_map/ppermute | solution.py:17
  67.7 8.2 %collective-permute-start.1 = (bf16[65,384]{1,0:T(8,128)(2,1)S(1)}, bf16[65,384]{1,0:T(8,128)(2,1)S(1)}, u32[]{:S(2)}, u32[]{:S(2)}) collective-permute-start(bf16[65,384]{1,0:T(8,128)(2,1)S(1)} %fusion.68), channel_id=1, source_target_pairs={{0,16},{1,17},{2,18},{3,19},{4,20},{5,21},{6,22},{7,23},{8,24},{9,... | collective-permute-start | bytes 149768 | tf_op jit(solution)/shard_map/ppermute | solution.py:17
  99.0 7.1 %collective-permute-start.2 = (bf16[65,384]{1,0:T(8,128)(2,1)}, bf16[65,384]{1,0:T(8,128)(2,1)}, u32[]{:S(2)}, u32[]{:S(2)}) collective-permute-start(bf16[65,384]{1,0:T(8,128)(2,1)} %add_convert_fusion.1), channel_id=1, source_target_pairs={{16,0},{17,1},{18,2},{19,3},{20,4},{21,5},{22,6},{23,7},{24,8},{25... | collective-permute-start | bytes 149768 | tf_op jit(solution)/shard_map/ppermute | solution.py:17
  122.6 6.8 %collective-permute-start.3 = (bf16[65,384]{1,0:T(8,128)(2,1)S(1)}, bf16[65,384]{1,0:T(8,128)(2,1)S(1)}, u32[]{:S(2)}, u32[]{:S(2)}) collective-permute-start(bf16[65,384]{1,0:T(8,128)(2,1)S(1)} %get-tuple-element.137), channel_id=1, source_target_pairs={{16,0},{17,1},{18,2},{19,3},{20,4},{21,5},{22,6},{23,7},{24,8},{25... | collective-permute-start | bytes 149768 | tf_op jit(solution)/shard_map/ppermute | solution.py:17
  134.8 46.4 %reduce-scatter.32.cloned.1.call-start = ((), (), s32[]{:S(2)}) async-start(), calls=%async_computation.15 | async-start | bytes 1105920 | tf_op jit(solution)/shard_map/reduce_scatter | solution.py:355
  138.9 70.4 %reduce-scatter.36.cloned.1.call-start = ((), (), s32[]{:S(2)}) async-start(), calls=%async_computation.17 | async-start | bytes 1474560 | tf_op jit(solution)/shard_map/reduce_scatter | solution.py:355
  142.5 95.3 %reduce-scatter.38.cloned.1.call-start = ((), (), s32[]{:S(2)}) async-start(), calls=%async_computation.18 | async-start | bytes 1474560 | tf_op jit(solution)/shard_map/reduce_scatter | solution.py:355
  148.0 112.3 %reduce-scatter.40.cloned.1.call-start = ((), (), s32[]{:S(2)}) async-start(), calls=%async_computation.19 | async-start | bytes 122880
  149.9 132.3 %reduce-scatter.42.cloned.1.call-start = ((), (), s32[]{:S(2)}) async-start(), calls=%async_computation.20 | async-start | bytes 122880
  150.8 153.5 %reduce-scatter.44.cloned.1.call-start = ((), (), s32[]{:S(2)}) async-start(), calls=%async_computation.21 | async-start | bytes 122880
  151.7 174.3 %reduce-scatter.46.cloned.1.call-start = ((), (), s32[]{:S(2)}) async-start(), calls=%async_computation.22 | async-start | bytes 122880
  152.7 195.4 %reduce-scatter.48.cloned.1.call-start = ((), (), s32[]{:S(2)}) async-start(), calls=%async_computation.23 | async-start | bytes 122880
  153.5 216.4 %reduce-scatter.50.cloned.1.call-start = ((), (), s32[]{:S(2)}) async-start(), calls=%async_computation.24 | async-start | bytes 122880
  154.4 237.5 %reduce-scatter.52.cloned.1.call-start = ((), (), s32[]{:S(2)}) async-start(), calls=%async_computation.25 | async-start | bytes 122880
  155.3 258.4 %reduce-scatter.56.cloned.1.call-start = ((), (), s32[]{:S(2)}) async-start(), calls=%async_computation.27 | async-start | bytes 122880
  156.2 281.3 %reduce-scatter.54.cloned.1.call-start = ((), (), s32[]{:S(2)}) async-start(), calls=%async_computation.26 | async-start | bytes 491520
  157.3 330.5 %all-reduce.13.cloned.1.call-start = ((), (), s32[]{:S(2)}) async-start(), calls=%async_computation.28 | async-start | bytes 1769472 | tf_op jit(solution)/shard_map/psum | solution.py:362
  158.5 80.0 %copy-start.77 = (bf16[65,384]{1,0:T(8,128)(2,1)S(1)}, bf16[65,384]{1,0:T(8,128)(2,1)}, u32[]{:S(2)}) copy-start(bf16[65,384]{1,0:T(8,128)(2,1)} %copy-done.76) | copy-start | bytes 149764
  158.5 80.0 %copy-start.88 = (f32[65]{0:T(128)S(1)}, f32[65]{0:T(128)}, u32[]{:S(2)}) copy-start(f32[65]{0:T(128)} %copy-done.86) | copy-start | bytes 784
  158.5 80.0 %copy-start.150 = (f32[65]{0:T(128)S(1)}, f32[65]{0:T(128)}, u32[]{:S(2)}) copy-start(f32[65]{0:T(128)} %get-tuple-element.163) | copy-start | bytes 784
  158.5 80.1 %copy-start.63 = (f32[1,65,384]{2,1,0:T(8,128)S(1)}, f32[1,65,384]{2,1,0:T(8,128)}, u32[]{:S(2)}) copy-start(f32[1,65,384]{2,1,0:T(8,128)} %get-tuple-element.136) | copy-start | bytes 299524
  (150 other events, 625.5 us)
Sparse Core Ops, SparseCore 0:
  9.6 20.4 all-gather.2
  31.6 19.1 all-gather.4
  135.0 19.7 reduce-scatter.33
  157.3 23.8 reduce-scatter.31
  183.6 25.7 reduce-scatter.35
  212.0 25.7 reduce-scatter.37
  240.7 19.4 reduce-scatter.39
  262.7 19.5 reduce-scatter.41
  284.7 19.5 reduce-scatter.43
  306.5 19.5 reduce-scatter.45
  328.5 19.5 reduce-scatter.47
  350.3 19.5 reduce-scatter.49
  372.3 19.5 reduce-scatter.51
  394.2 19.5 reduce-scatter.55
  416.6 20.7 reduce-scatter.53
  440.0 47.8 all-reduce.12
where the time goes:
time: 502 us; the launch traced here: 500 us
  waiting for transfers between devices  308 us (61%)
  matrix products  55.2 us (11%)
  blocking collectives  41.9 us (8%)
  local copies, waits for them, and re-layouts  41.4 us (8%)
  other arithmetic  25.4 us (5%)
  between operations  16.9 us (3%)
  starting transfers between devices  11.6 us (2%)
    unnamed x25, waiting for transfers between devices  193 us
    reduce_scatter x4, waiting for transfers between devices, local(): lax.psum_scatter(as_sent(tuple((member[None] for member in grad_sums))),...  79.2 us
    psum x1, waiting for transfers between devices, local(): lax.psum(as_sent(grad_sums), 'dp')  32.9 us
    unnamed x344, local copies, waits for them, and re-layouts  27.7 us
    psum x1, blocking collectives, local(): lax.psum(as_sent(grad_sums), 'dp')  11.9 us
    ppermute x4, starting transfers between devices, from_behind(): return lax.ppermute(block, axis, route)  10.7 us
    convert_element_type x13, other arithmetic, local(): part.astype(jnp.float32)  10.7 us
  transfers between devices with their start and end apart: 20, of which 15 were waited for; matrix products, arithmetic and copies ran while one was open for 12% of the time, Pallas kernels for 0%

commit v1 on v0

v1 whole, which is shorter than its diff:
```python
import functools

import jax
import jax.numpy as jnp
from jax import lax
from jax.experimental import pallas as pl
from jax.experimental.pallas import tpu as pltpu
from jax.sharding import PartitionSpec as P

HD = 64
PAIR = 2 * HD
EPS = 1e-06
SQRT_HALF = 0.7071067811865476
INV_ROOT_TAU = 0.3989422804014327
BF = jnp.bfloat16
F32 = jnp.float32
VMEM_BYTES = 28 * 1024 * 1024

PRE_GAIN, PRE_SHIFT, QUERY_BIAS, VALUE_BIAS, MERGE_BIAS, MID_GAIN, MID_SHIFT, DOWN_BIAS = range(8)


def padded_length(length):
    return -(-length // 16) * 16


def dot(a, b):
    return jnp.dot(a, b, preferred_element_type=F32)


def dot_nt(a, b):
    return lax.dot_general(a, b, (((1,), (1,)), ((), ())), preferred_element_type=F32)


def dot_tn(a, b):
    return lax.dot_general(a, b, (((0,), (0,)), ((), ())), preferred_element_type=F32)


def fetch(pieces, dest, sems, first, me):
    copies = []
    for k, piece in enumerate(pieces):
        rows = piece.shape[0]
        start = pl.multiple_of(jnp.bitwise_xor(me, k) * rows, rows)
        copies.append(pltpu.make_async_copy(piece, dest.at[pl.ds(start, rows)], sems.at[first + k]))
    for copy in copies:
        copy.start()
    return copies


def arrive(copies):
    for copy in copies:
        copy.wait()


def pad_images(images, scratch):
    length = images[0].shape[0]
    step = padded_length(length)
    scratch[...] = jnp.zeros_like(scratch)
    for n, image in enumerate(images):
        scratch[n * step : n * step + length, :] = image.astype(F32)
    return scratch[...]


def unpad(ref, rows, kind):
    count, length, _ = ref.shape
    step = padded_length(length)
    for n in range(count):
        ref[n] = rows[n * step : n * step + length, :].astype(kind)


def norm_parts(rows):
    mean = jnp.mean(rows, axis=-1, keepdims=True)
    centered = rows - mean
    inverse = lax.rsqrt(jnp.mean(centered * centered, axis=-1, keepdims=True) + EPS)
    return centered * inverse, inverse


def norm_backward(grad_rows, normed, inverse, gain):
    scaled = grad_rows * gain
    mean_one = jnp.mean(scaled, axis=-1, keepdims=True)
    mean_two = jnp.mean(scaled * normed, axis=-1, keepdims=True)
    return inverse * (scaled - mean_one - normed * mean_two)


def column_sum(rows):
    return jnp.sum(rows, axis=0, keepdims=True)


def half_masks():
    lane = lax.broadcasted_iota(jnp.int32, (1, PAIR), 1)
    low = (lane < HD).astype(F32)
    return low.astype(BF), (1.0 - low).astype(BF)


def both_heads(rows):
    low, high = half_masks()
    return jnp.concatenate([rows * low, rows * high], axis=0)


def beside(stacked):
    half = stacked.shape[0] // 2
    lane = lax.broadcasted_iota(jnp.int32, (half, PAIR), 1)
    return jnp.where(lane < HD, stacked[:half], stacked[half:])


def qkv(packed, n, pair, step, width):
    rows = slice(n * step, (n + 1) * step)
    return tuple(packed[rows, part * width + pair * PAIR : part * width + (pair + 1) * PAIR] for part in range(3))


def head_probs(queries, keys, length):
    stacked = both_heads(queries)
    scores = dot_nt(stacked, keys) * HD**-0.5
    lane = lax.broadcasted_iota(jnp.int32, scores.shape, 1)
    scores = jnp.where(lane < length, scores, -1e30)
    grown = jnp.exp(scores - jnp.max(scores, axis=-1, keepdims=True))
    return grown * (1.0 / jnp.sum(grown, axis=-1, keepdims=True)), stacked


def attention_forward(packed, mixed, count, length, width):
    step = padded_length(length)
    for n in range(count):
        for pair in range(width // PAIR):
            queries, keys, values = qkv(packed, n, pair, step, width)
            probs, _ = head_probs(queries, keys, length)
            out = beside(dot(probs.astype(BF), values)).astype(BF)
            mixed[n * step : (n + 1) * step, pair * PAIR : (pair + 1) * PAIR] = out


def attention_backward(packed, grad_mixed, grad_packed, count, length, width):
    step = padded_length(length)
    for n in range(count):
        for pair in range(width // PAIR):
            queries, keys, values = qkv(packed, n, pair, step, width)
            probs, stacked = head_probs(queries, keys, length)
            rows = slice(n * step, (n + 1) * step)
            incoming = both_heads(grad_mixed[rows, pair * PAIR : (pair + 1) * PAIR])
            grad_probs = dot_nt(incoming, values)
            inner = jnp.sum(probs * grad_probs, axis=-1, keepdims=True)
            grad_scores = (probs * (grad_probs - inner)).astype(BF)
            parts = (
                beside(dot(grad_scores, keys)) * HD**-0.5,
                dot_tn(grad_scores, stacked) * HD**-0.5,
                dot_tn(probs.astype(BF), incoming),
            )
            for part, value in enumerate(parts):
                column = part * width + pair * PAIR
                grad_packed[rows, column : column + PAIR] = value.astype(BF)


def entry_rows(rows, small):
    normed, inverse = norm_parts(rows)
    return (normed * small[PRE_GAIN : PRE_GAIN + 1] + small[PRE_SHIFT : PRE_SHIFT + 1]).astype(BF), normed, inverse


def mid_rows(middle, small):
    normed, inverse = norm_parts(middle)
    return (normed * small[MID_GAIN : MID_GAIN + 1] + small[MID_SHIFT : MID_SHIFT + 1]).astype(BF), normed, inverse


def packed_bias(small):
    query = small[QUERY_BIAS : QUERY_BIAS + 1]
    return jnp.concatenate([query, jnp.zeros_like(query), small[VALUE_BIAS : VALUE_BIAS + 1]], axis=1)


def attention_half(rows, small, heads, merge, packed, mixed, count, length, waits):
    width = rows.shape[1]
    entry, _, _ = entry_rows(rows, small)
    arrive(waits[0])
    packed[...] = (dot(entry, heads[...]) + packed_bias(small)).astype(BF)
    attention_forward(packed, mixed, count, length, width)
    arrive(waits[1])
    return rows + dot(mixed[...], merge[...]) + small[MERGE_BIAS : MERGE_BIAS + 1]


def gelu_parts(hidden):
    bell = 0.5 * (1.0 + lax.erf(hidden * SQRT_HALF))
    return hidden * bell, bell


def gelu_slope(hidden, bell):
    return bell + hidden * jnp.exp(-0.5 * hidden * hidden) * INV_ROOT_TAU


def picked_images(info, images):
    return [
        jnp.where(info[2 + n] == 0, images[0], images[1]) for n in range(images.shape[0])
    ]


def attend_kernel(shards, info, images, small, *refs):
    heads_pieces, merge_pieces = refs[:shards], refs[shards : 2 * shards]
    middle_ref, mid_ref, heads, merge, rows_ref, packed, mixed, sems = refs[2 * shards :]
    me = info[0]
    waits = (fetch(heads_pieces, heads, sems, 0, me), fetch(merge_pieces, merge, sems, shards, me))
    count, length, _ = images.shape
    rows = pad_images(picked_images(info, images), rows_ref)
    middle = attention_half(rows, small, heads, merge, packed, mixed, count, length, waits)
    middle_ref[...] = middle
    mid_ref[...] = mid_rows(middle, small)[0]


def widen_kernel(shards, info, mid_ref, up_bias, *refs):
    act_ref, up, sems = refs[shards:]
    arrive(fetch(refs[:shards], up, sems, 0, info[0]))
    hidden = dot(mid_ref[...], up[...]) + up_bias[...]
    act_ref[...] = gelu_parts(hidden)[0].astype(BF)


def narrow_kernel(shards, info, act_ref, middle_ref, small, *refs):
    out_ref, down, sems = refs[shards:]
    arrive(fetch(refs[:shards], down, sems, 0, info[0]))
    out = middle_ref[...] + dot(act_ref[...], down[...]) + small[DOWN_BIAS : DOWN_BIAS + 1]
    unpad(out_ref, out, BF)


def both_ways_kernel(shards, info, images, arrived, cotangent, small, up_bias, *refs):
    pieces = [refs[n * shards : (n + 1) * shards] for n in range(4)]
    out_ref, sent_ref, packed, mixed, middle_ref, act_ref = refs[4 * shards : 4 * shards + 6]
    heads, merge, up, down, rows_ref, grad_ref, grad_packed, sems = refs[4 * shards + 6 :]
    me, leading = info[0], info[1] == 0
    waits = [
        fetch(piece, dest, sems, n * shards, me) for n, (piece, dest) in enumerate(zip(pieces, (heads, merge, up, down)))
    ]
    count, length, width = images.shape
    source = [jnp.where(leading, image, arrived[n]) for n, image in enumerate(picked_images(info, images))]
    rows = pad_images(source, rows_ref)
    middle = attention_half(rows, small, heads, merge, packed, mixed, count, length, waits)
    middle_ref[...] = middle
    mid, unit_two, inverse_two = mid_rows(middle, small)
    arrive(waits[2])
    hidden = dot(mid, up[...]) + up_bias[...]
    act, bell = gelu_parts(hidden)
    slope = gelu_slope(hidden, bell)
    act_ref[...] = act.astype(BF)
    arrive(waits[3])
    out = middle + dot(act_ref[...], down[...]) + small[DOWN_BIAS : DOWN_BIAS + 1]
    unpad(out_ref, out, BF)
    incoming = pad_images([cotangent[n] for n in range(count)], grad_ref)
    grad_hidden = (dot_nt(incoming.astype(BF), down[...]) * slope).astype(BF)
    grad_mid = dot_nt(grad_hidden, up[...])
    grad_middle = incoming + norm_backward(grad_mid, unit_two, inverse_two, small[MID_GAIN : MID_GAIN + 1])
    grad_mixed = dot_nt(grad_middle.astype(BF), merge[...]).astype(BF)
    attention_backward(packed, grad_mixed, grad_packed, count, length, width)
    grad_entry = dot_nt(grad_packed[...], heads[...])
    _, unit_one, inverse_one = entry_rows(rows, small)
    grad_in = grad_middle + norm_backward(grad_entry, unit_one, inverse_one, small[PRE_GAIN : PRE_GAIN + 1])
    unpad(sent_ref, grad_in, BF)


def own_gradient(info, returned, cotangent, scratch):
    leading = info[1] == 0
    return pad_images(
        [jnp.where(leading, returned[n], cotangent[n]) for n in range(cotangent.shape[0])], scratch
    )


def down_grad_kernel(shards, info, returned, cotangent, act_ref, *refs):
    outs, grad_ref = refs[:shards], refs[shards]
    incoming = own_gradient(info, returned, cotangent, grad_ref).astype(BF)
    rows = outs[0].shape[0]
    for k in range(shards):
        start = pl.multiple_of(jnp.bitwise_xor(info[0], k) * rows, rows)
        outs[k][...] = dot_tn(act_ref[:, pl.ds(start, rows)], incoming).astype(BF)


def up_grad_kernel(shards, info, returned, cotangent, middle_ref, small, up_bias, *refs):
    pieces = (refs[:shards], refs[shards : 2 * shards])
    outs = refs[2 * shards : 3 * shards]
    hidden_ref, up, down, grad_ref, whole, sems = refs[3 * shards :]
    me = info[0]
    waits = [fetch(piece, dest, sems, n * shards, me) for n, (piece, dest) in enumerate(zip(pieces, (up, down)))]
    incoming = own_gradient(info, returned, cotangent, grad_ref).astype(BF)
    mid, _, _ = mid_rows(middle_ref[...], small)
    arrive(waits[0])
    hidden = dot(mid, up[...]) + up_bias[...]
    slope = gelu_slope(hidden, gelu_parts(hidden)[1])
    arrive(waits[1])
    hidden_ref[...] = (dot_nt(incoming, down[...]) * slope).astype(BF)
    whole[...] = dot_tn(mid, hidden_ref[...]).astype(BF)
    rows = outs[0].shape[0]
    for k in range(shards):
        start = pl.multiple_of(jnp.bitwise_xor(me, k) * rows, rows)
        outs[k][...] = whole[pl.ds(start, rows), :]


def rest_grad_kernel(
    shards, info, returned, cotangent, images, arrived, middle_ref, grad_hidden, packed, mixed, small, *refs
):
    pieces = [refs[n * shards : (n + 1) * shards] for n in range(3)]
    outs = refs[3 * shards : 4 * shards]
    grad_in_ref, heads, merge, up, rows_ref, grad_ref, grad_packed, whole_heads, whole_merge, extra, sems = refs[4 * shards :]
    me, leading = info[0], info[1] == 0
    waits = [
        fetch(piece, dest, sems, n * shards, me) for n, (piece, dest) in enumerate(zip(pieces, (heads, merge, up)))
    ]
    count, length, width = images.shape
    incoming = own_gradient(info, returned, cotangent, grad_ref)
    extra[...] = jnp.zeros_like(extra)
    extra[DOWN_BIAS : DOWN_BIAS + 1, :] = column_sum(incoming)
    wide_sum = column_sum(grad_hidden[...].astype(F32))
    for n in range(wide_sum.shape[1] // width):
        extra[8 + n : 9 + n, :] = wide_sum[:, n * width : (n + 1) * width]
    _, unit_two, inverse_two = mid_rows(middle_ref[...], small)
    arrive(waits[2])
    grad_mid = dot_nt(grad_hidden[...], up[...])
    extra[MID_GAIN : MID_GAIN + 1, :] = column_sum(grad_mid * unit_two)
    extra[MID_SHIFT : MID_SHIFT + 1, :] = column_sum(grad_mid)
    grad_middle = incoming + norm_backward(grad_mid, unit_two, inverse_two, small[MID_GAIN : MID_GAIN + 1])
    grad_branch = grad_middle.astype(BF)
    extra[MERGE_BIAS : MERGE_BIAS + 1, :] = column_sum(grad_branch.astype(F32))
    whole_merge[...] = dot_tn(mixed[...], grad_branch).astype(BF)
    arrive(waits[1])
    grad_mixed = dot_nt(grad_branch, merge[...]).astype(BF)
    attention_backward(packed, grad_mixed, grad_packed, count, length, width)
    packed_sum = column_sum(grad_packed[...].astype(F32))
    extra[QUERY_BIAS : QUERY_BIAS + 1, :] = packed_sum[:, :width]
    extra[VALUE_BIAS : VALUE_BIAS + 1, :] = packed_sum[:, 2 * width :]
    source = [jnp.where(leading, image, arrived[n]) for n, image in enumerate(picked_images(info, images))]
    entry, unit_one, inverse_one = entry_rows(pad_images(source, rows_ref), small)
    whole_heads[...] = dot_tn(entry, grad_packed[...]).astype(BF)
    arrive(waits[0])
    grad_entry = dot_nt(grad_packed[...], heads[...])
    extra[PRE_GAIN : PRE_GAIN + 1, :] = column_sum(grad_entry * unit_one)
    extra[PRE_SHIFT : PRE_SHIFT + 1, :] = column_sum(grad_entry)
    grad_in = grad_middle + norm_backward(grad_entry, unit_one, inverse_one, small[PRE_GAIN : PRE_GAIN + 1])
    rounded = grad_in.astype(BF).astype(F32)
    unpad(grad_in_ref, jnp.where(leading, grad_in, rounded), F32)
    rows = pieces[0][0].shape[0]
    wide = whole_heads.shape[1]
    for k in range(shards):
        start = pl.multiple_of(jnp.bitwise_xor(me, k) * rows, rows)
        outs[k][:rows, :wide] = whole_heads[pl.ds(start, rows), :]
        outs[k][:rows, wide:] = whole_merge[pl.ds(start, rows), :]
        outs[k][rows:, :wide] = jnp.zeros((16, wide), BF)
        outs[k][rows:, wide:] = extra[...].astype(BF)


def call(kernel, name, info, blocks, pieces, outs, scratch, flops):
    space = lambda kind, many: [pl.BlockSpec(memory_space=kind)] * many
    nbytes = sum(a.size * a.dtype.itemsize for a in (*blocks, *pieces, *outs))
    return pl.pallas_call(
        kernel,
        out_shape=outs,
        in_specs=space(pltpu.SMEM, 1) + space(pltpu.VMEM, len(blocks)) + space(pl.ANY, len(pieces)),
        out_specs=space(pltpu.VMEM, len(outs)),
        scratch_shapes=scratch,
        compiler_params=pltpu.CompilerParams(vmem_limit_bytes=VMEM_BYTES),
        cost_estimate=pl.CostEstimate(flops=flops, bytes_accessed=nbytes, transcendentals=0),
        name=name,
    )(info, *blocks, *pieces)


def swapped(block, axis, bit):
    return lax.ppermute(block, axis, [(i, i ^ bit) for i in range(lax.axis_size(axis))])


def bits_of(size):
    return [1 << n for n in range(size.bit_length() - 1)]


def gather_pieces(shard, axis):
    pieces = {0: shard}
    for bit in reversed(bits_of(lax.axis_size(axis))):
        pieces.update({k ^ bit: swapped(piece, axis, bit) for k, piece in list(pieces.items())})
    return [pieces[k] for k in range(len(pieces))]


def in_order(pieces, me):
    stacked = jnp.stack(pieces)
    for bit in bits_of(len(pieces)):
        split = stacked.reshape(-1, 2, bit, *stacked.shape[1:])
        stacked = jnp.where((me & bit) != 0, split[:, ::-1], split).reshape(stacked.shape)
    return stacked


def added(*terms):
    return sum(term.astype(F32) for term in terms).astype(BF)


def scatter_pieces(pieces, axis):
    for bit in bits_of(lax.axis_size(axis)):
        kept = [k for k in range(len(pieces)) if pieces[k] is not None and not k & bit]
        for k in sorted(kept, reverse=True):
            pieces[k] = added(pieces[k], swapped(pieces[k ^ bit], axis, bit))
            pieces[k ^ bit] = None
    return pieces[0]


def total_over(shard, axis):
    if lax.axis_size(axis) != 4:
        return lax.psum(shard, axis).astype(F32)
    at = lax.axis_index(axis)
    inward = added(shard, lax.ppermute(shard, axis, [(0, 1), (3, 2)]))
    across = inward.astype(F32) + lax.ppermute(inward, axis, [(1, 2), (2, 1)]).astype(F32)
    across = lax.reduce_precision(across, 8, 7).astype(BF)
    outward = lax.ppermute(across, axis, [(1, 0), (2, 3)])
    return jnp.where((at == 0) | (at == 3), outward, across).astype(F32)


def local(
    images,
    slot_image,
    cotangent,
    pre_gain,
    pre_shift,
    heads_weight,
    query_bias,
    value_bias,
    merge_weight,
    merge_bias,
    mid_gain,
    mid_shift,
    up_weight,
    up_bias,
    down_weight,
    down_bias,
):
    me = lax.axis_index("fsdp").astype(jnp.int32)
    section = lax.axis_index("section").astype(jnp.int32)
    shards = lax.axis_size("fsdp")
    info = jnp.concatenate([jnp.stack([me, section]), slot_image[0]])
    count, length, width = images.shape
    tall = count * padded_length(length)
    part = width // shards
    wide = heads_weight.shape[2]
    hidden_width = up_weight.shape[2]

    vectors = jnp.concatenate(
        [pre_gain, pre_shift, query_bias, value_bias, merge_bias, mid_gain, mid_shift, down_bias, up_bias.reshape(-1, part)]
    )
    vector_pieces = gather_pieces(vectors, "fsdp")
    heads_pieces = gather_pieces(heads_weight[0], "fsdp")
    merge_pieces = gather_pieces(merge_weight[0], "fsdp")
    up_pieces = gather_pieces(up_weight[0], "fsdp")
    down_pieces = gather_pieces(down_weight[0], "fsdp")
    ordered = in_order(vector_pieces, me).astype(F32)
    small = ordered[:, :8].transpose(1, 0, 2).reshape(8, width)
    wide_bias = ordered[:, 8:].reshape(1, hidden_width)

    shape = jax.ShapeDtypeStruct
    scratch_heads = pltpu.VMEM((width, wide), BF)
    scratch_merge = pltpu.VMEM((width, width), BF)
    scratch_up = pltpu.VMEM((width, hidden_width), BF)
    scratch_down = pltpu.VMEM((hidden_width, width), BF)
    scratch_rows = pltpu.VMEM((tall, width), F32)
    scratch_packed = pltpu.VMEM((tall, wide), BF)
    scratch_mixed = pltpu.VMEM((tall, width), BF)
    sems = lambda many: pltpu.SemaphoreType.DMA((many * shards,))
    bind = lambda kernel: functools.partial(kernel, shards)
    work = 2 * tall * width

    middle, mid = call(
        bind(attend_kernel),
        "attend",
        info,
        (images, small),
        (*heads_pieces, *merge_pieces),
        (shape((tall, width), F32), shape((tall, width), BF)),
        [scratch_heads, scratch_merge, scratch_rows, scratch_packed, scratch_mixed, sems(2)],
        work * (wide + width),
    )
    (act,) = call(
        bind(widen_kernel),
        "widen",
        info,
        (mid, wide_bias),
        up_pieces,
        (shape((tall, hidden_width), BF),),
        [scratch_up, sems(1)],
        work * hidden_width,
    )
    (first_out,) = call(
        bind(narrow_kernel),
        "narrow",
        info,
        (act, middle, small),
        down_pieces,
        (shape(images.shape, BF),),
        [scratch_down, sems(1)],
        work * hidden_width,
    )
    arrived = lax.ppermute(first_out, "section", [(0, 1)])

    layer_out, sent, packed, mixed, middle, act = call(
        bind(both_ways_kernel),
        "both_ways",
        info,
        (images, arrived, cotangent, small, wide_bias),
        (*heads_pieces, *merge_pieces, *up_pieces, *down_pieces),
        (
            shape(images.shape, BF),
            shape(images.shape, BF),
            shape((tall, wide), BF),
            shape((tall, width), BF),
            shape((tall, width), F32),
            shape((tall, hidden_width), BF),
        ),
        [scratch_heads, scratch_merge, scratch_up, scratch_down, scratch_rows, scratch_rows, scratch_packed, sems(4)],
        2 * work * (wide + width + 2 * hidden_width),
    )
    returned = lax.ppermute(sent, "section", [(1, 0)])

    down_grads = call(
        bind(down_grad_kernel),
        "down_grad",
        info,
        (returned, cotangent, act),
        (),
        (shape((hidden_width // shards, width), BF),) * shards,
        [scratch_rows],
        work * hidden_width,
    )
    *up_grads, grad_hidden = call(
        bind(up_grad_kernel),
        "up_grad",
        info,
        (returned, cotangent, middle, small, wide_bias),
        (*up_pieces, *down_pieces),
        (shape((part, hidden_width), BF),) * shards + (shape((tall, hidden_width), BF),),
        [scratch_up, scratch_down, scratch_rows, scratch_up, sems(2)],
        3 * work * hidden_width,
    )
    *rest_grads, grad_in = call(
        bind(rest_grad_kernel),
        "rest_grad",
        info,
        (returned, cotangent, images, arrived, middle, grad_hidden, packed, mixed, small),
        (*heads_pieces, *merge_pieces, *up_pieces),
        (shape((part + 16, wide + width), BF),) * shards + (shape(images.shape, F32),),
        [
            scratch_heads,
            scratch_merge,
            scratch_up,
            scratch_rows,
            scratch_rows,
            scratch_packed,
            scratch_heads,
            scratch_merge,
            pltpu.VMEM((16, width), F32),
            sems(3),
        ],
        work * (2 * wide + 2 * width + hidden_width),
    )
    down_total = total_over(scatter_pieces(list(down_grads), "fsdp"), "dp")
    up_total = total_over(scatter_pieces(list(up_grads), "fsdp"), "dp")
    rest_total = total_over(scatter_pieces(list(rest_grads), "fsdp"), "dp")

    heads_total = rest_total[:part, :wide]
    merge_total = rest_total[:part, wide:]
    vector_total = lax.dynamic_slice(rest_total, (part, wide + me * part), (8, part))
    up_bias_total = lax.dynamic_slice(rest_total, (part + 8 + me, wide), (1, width))
    row = lambda n: vector_total[n : n + 1]
    return (
        layer_out[None],
        grad_in[None],
        row(PRE_GAIN),
        row(PRE_SHIFT),
        heads_total[None],
        row(QUERY_BIAS),
        row(VALUE_BIAS),
        merge_total[None],
        row(MERGE_BIAS),
        row(MID_GAIN),
        row(MID_SHIFT),
        up_total[None],
        up_bias_total,
        down_total[None],
        row(DOWN_BIAS),
    )


def solution(mesh):
    vector, matrix = P("section", "fsdp"), P("section", "fsdp", None)
    rows = P("section", ("fsdp", "dp"), None, None)
    weights = (
        vector,
        vector,
        matrix,
        vector,
        vector,
        matrix,
        vector,
        vector,
        vector,
        matrix,
        vector,
        matrix,
        vector,
    )
    blocks = P(("fsdp", "dp"), None, None)
    return jax.shard_map(
        local,
        mesh=mesh,
        in_specs=(blocks, P(("fsdp", "dp"), None), blocks, *weights),
        out_specs=(rows, rows, *weights),
        check_vma=False,
    )
```

time: 502 us -> 143 us (0.28)
  waiting for transfers between devices: 308 us -> 61.5 us
  matrix products: 55.2 us -> 0 us
  blocking collectives: 41.9 us -> 0 us
  local copies, waits for them, and re-layouts: 41.4 us -> 10.9 us
  Pallas kernels: 0 us -> 28.9 us
  starting transfers between devices: 11.6 us -> 34.6 us
  other arithmetic: 25.4 us -> 5.32 us
  between operations: 16.9 us -> 1.3 us
    unnamed x25 -> x0, waiting for transfers between devices: 193 us -> none
    reduce_scatter x4 -> x0, waiting for transfers between devices: 79.2 us -> none  [local(): lax.psum_scatter(as_sent(tuple((member[None] for member in grad_sums))),...]
    ppermute x4 -> x35, waiting for transfers between devices: 2.89 us -> 61.5 us  [the longest x24 28.9 us: swapped(): lax.ppermute(block, axis, [(i, i ^ bit) for i in range(lax.axis_size(axis...]
    dot_general x58 -> x0, matrix products: 55.2 us -> none  [the longest x3 5.54 us: layer_forward(): jnp.dot(mid_rows, up_weight, preferred_element_type=jnp.float32)]
    psum x1 -> x0, waiting for transfers between devices: 32.9 us -> none  [local(): lax.psum(as_sent(grad_sums), 'dp')]
    pallas_call x0 -> x7, Pallas kernels: none -> 28.9 us  [call(): pl.pallas_call(kernel, out_shape=outs, in_specs=space(pltpu.SMEM, 1) + sp...]
    ppermute x4 -> x35, starting transfers between devices: 10.7 us -> 34.6 us  [the longest x24 13.1 us: swapped(): lax.ppermute(block, axis, [(i, i ^ bit) for i in range(lax.axis_size(axis...]
    all_gather x3 -> x0, blocking collectives: 21.2 us -> none  [the longest x1 8.21 us: local(): lax.all_gather(shards[2], 'fsdp', axis=1, tiled=True)]
  transfers between devices with their start and end apart: 20 -> 35, of which waited for: 15 -> 13; matrix products, arithmetic and copies ran while one was open for 12% -> 6% of each run, Pallas kernels for 0% -> 11%
where the time goes in v1:
time: 143 us
  waiting for transfers between devices  61.5 us (43%)
  starting transfers between devices  34.6 us (24%)
  Pallas kernels  28.9 us (20%)
  local copies, waits for them, and re-layouts  10.9 us (8%)
  other arithmetic  5.32 us (4%)
    pallas_call x7, Pallas kernels, call(): pl.pallas_call(kernel, out_shape=outs, in_specs=space(pltpu.SMEM, 1) + sp...  28.9 us
    ppermute x24, waiting for transfers between devices, swapped(): lax.ppermute(block, axis, [(i, i ^ bit) for i in range(lax.axis_size(axis...  28.9 us
    ppermute x3, waiting for transfers between devices, total_over(): outward = lax.ppermute(across, axis, [(1, 0), (2, 3)])  19.7 us
    ppermute x24, starting transfers between devices, swapped(): lax.ppermute(block, axis, [(i, i ^ bit) for i in range(lax.axis_size(axis...  13.1 us
    ppermute x3, starting transfers between devices, total_over(): inward = added(shard, lax.ppermute(shard, axis, [(0, 1), (3, 2)]))  10.5 us
    unnamed x64, local copies, waits for them, and re-layouts  7.13 us
    ppermute x1, waiting for transfers between devices, local(): returned = lax.ppermute(sent, 'section', [(1, 0)])  5.16 us
    ppermute x3, waiting for transfers between devices, total_over(): inward = added(shard, lax.ppermute(shard, axis, [(0, 1), (3, 2)]))  5.13 us
  transfers between devices with their start and end apart: 35, of which 13 were waited for; matrix products, arithmetic and copies ran while one was open for 6% of the time, Pallas kernels for 11%

profile of v1, /device:TPU:0, one launch (start us, length us, event | category | flops | bytes accessed | tf_op | source)
XLA Modules:
  0.0 142.6 jit_solution(10009900015860400946)
XLA Ops:
  2.3 3.0 %collective-permute-start.1 = (bf16[12,96]{1,0:T(8,128)(2,1)S(1)}, bf16[12,96]{1,0:T(8,128)(2,1)S(1)}, u32[]{:S(2)}, u32[]{:S(2)}) collective-permute-start(bf16[12,96]{1,0:T(8,128)(2,1)S(1)} %concatenate.7), channel_id=1, source_target_pairs={{0,8},{4,12},{8,0},{12,4},{1,9},{5,13},{9,1},{13,5},{2,10},{6,14},... | collective-permute-start | bytes 6920 | tf_op jit(solution)/shard_map/ppermute | solution.py:354
  5.8 1.7 %collective-permute-start.4 = (bf16[96,1152]{1,0:T(8,128)(2,1)}, bf16[96,1152]{1,0:T(8,128)(2,1)S(1)}, u32[]{:S(2)}, u32[]{:S(2)}) collective-permute-start(bf16[96,1152]{1,0:T(8,128)(2,1)} %bitcast.41), channel_id=1, source_target_pairs={{0,8},{4,12},{8,0},{12,4},{1,9},{5,13},{9,1},{13,5},{2,10},{6,14},... | collective-permute-start | bytes 663560 | tf_op jit(solution)/shard_map/ppermute | solution.py:354
  13.0 2.4 %collective-permute-done.4.refs_2_ = bf16[96,1152]{1,0:T(8,128)(2,1)S(1)} collective-permute-done((bf16[96,1152]{1,0:T(8,128)(2,1)}, bf16[96,1152]{1,0:T(8,128)(2,1)S(1)}, u32[]{:S(2)}, u32[]{:S(2)}) %collective-permute-start.4) | collective-permute-done | bytes 221216 | tf_op jit(solution)/shard_map/ppermute | solution.py:354
  15.3 6.3 %collective-permute-done.10.refs_2_.refs_10_ = bf16[96,1536]{1,0:T(8,128)(2,1)S(1)} collective-permute-done((bf16[96,1536]{1,0:T(8,128)(2,1)}, bf16[96,1536]{1,0:T(8,128)(2,1)S(1)}, u32[]{:S(2)}, u32[]{:S(2)}) %collective-permute-start.10) | collective-permute-done | bytes 294944 | tf_op jit(solution)/shard_map/ppermute | solution.py:354
  21.6 5.9 %collective-permute-done.13.refs_2_.refs_14_.refs_6_ = bf16[384,384]{1,0:T(8,128)(2,1)S(1)} collective-permute-done((bf16[384,384]{1,0:T(8,128)(2,1)}, bf16[384,384]{1,0:T(8,128)(2,1)S(1)}, u32[]{:S(2)}, u32[]{:S(2)}) %collective-permute-start.13) | collective-permute-done | bytes 294944 | tf_op jit(solution)/shard_map/ppermute | solution.py:354
  30.4 3.7 %attend.1 = (f32[160,384]{1,0:T(8,128)S(1)}, bf16[160,384]{1,0:T(8,128)(2,1)S(1)}) custom-call(s32[4]{0:T(128)S(1)} %pad_add_fusion.info, bf16[2,65,384]{2,1,0:T(8,128)(2,1)S(1)} %copy.35.images, f32[8,384]{1,0:T(8,128)S(1)} %reshape.47.small, bf16[96,1152]{1,0:T(8,128)(2,1)S(1)} %bitcast.43, bf16[96,1152]{1,0:T(8,128)(2,1)S(1)} %collective-permute-done.3.refs_1_, ...), custom_call_target="tpu_custom_call" | custom-call | flops 188743680 | bytes 1660416 | tf_op jit(solution)/shard_map/attend/pallas_call | solution.py:341
  36.8 3.6 %collective-permute-start.15 = (bf16[2,65,384]{2,1,0:T(8,128)(2,1)S(1)}, bf16[2,65,384]{2,1,0:T(8,128)(2,1)S(1)}, u32[]{:S(2)}, u32[]{:S(2)}) collective-permute-start(bf16[2,65,384]{2,1,0:T(8,128)(2,1)S(1)} %narrow.1), channel_id=1, source_target_pairs={{0,16},{1,17},{2,18},{3,19},{4,20},{5,21},{6,22},{7,23},{8,24},{9,... | collective-permute-start | bytes 299528 | tf_op jit(solution)/shard_map/ppermute | solution.py:482
  40.4 2.6 %collective-permute-done.15.arrived = bf16[2,65,384]{2,1,0:T(8,128)(2,1)S(1)} collective-permute-done((bf16[2,65,384]{2,1,0:T(8,128)(2,1)S(1)}, bf16[2,65,384]{2,1,0:T(8,128)(2,1)S(1)}, u32[]{:S(2)}, u32[]{:S(2)}) %collective-permute-start.15) | collective-permute-done | bytes 99872 | tf_op jit(solution)/shard_map/ppermute | solution.py:482
  43.1 10.1 %both_ways.1 = (bf16[2,65,384]{2,1,0:T(8,128)(2,1)S(1)}, bf16[2,65,384]{2,1,0:T(8,128)(2,1)S(1)}, bf16[160,1152]{1,0:T(8,128)(2,1)S(1)}, bf16[160,384]{1,0:T(8,1...) custom-call(s32[4]{0:T(128)S(1)} %pad_add_fusion.info, bf16[2,65,384]{2,1,0:T(8,128)(2,1)S(1)} %copy.35.images, ...), custom_call_target="tpu_custom_call" | custom-call | flops 1132462080 | bytes 5285376 | tf_op jit(solution)/shard_map/both_ways/pallas_call | solution.py:341
  55.3 5.2 %collective-permute-done.16.returned = bf16[2,65,384]{2,1,0:T(8,128)(2,1)S(1)} collective-permute-done((bf16[2,65,384]{2,1,0:T(8,128)(2,1)S(1)}, bf16[2,65,384]{2,1,0:T(8,128)(2,1)S(1)}, u32[]{:S(2)}, u32[]{:S(2)}) %collective-permute-start.16) | collective-permute-done | bytes 99872 | tf_op jit(solution)/shard_map/ppermute | solution.py:501
  60.4 1.9 %down_grad.1 = (bf16[384,384]{1,0:T(8,128)(2,1)S(1)}, bf16[384,384]{1,0:T(8,128)(2,1)S(1)}, bf16[384,384]{1,0:T(8,128)(2,1)S(1)}, bf16[384,384]{1,0:T(8,128)(2,1)}) custom-call(s32[4]{0:T(128)S(1)} %pad_add_fusion.info, bf16[2,65,384]{2,1,0:T(8,128)(2,1)S(1)} %collective-permute-done.16.returned, bf16[2,65,384]{2,1,0:T(8,128)(2,1)S(1)} %copy.36.cotangent, ...), custom_call_target="tpu_custom_call" | custom-call | flops 188743680 | bytes 1870848 | tf_op jit(solution)/shard_map/down_grad/pallas_call | solution.py:341
  64.4 1.6 %copy.41 = bf16[1,2,65,384]{3,1,2,0:T(2,128)(2,1)} copy(bf16[1,2,65,384]{3,2,1,0:T(8,128)(2,1)} %bitcast.52) | data formatting | bytes 199680
  66.6 2.9 %up_grad.1 = (bf16[96,1536]{1,0:T(8,128)(2,1)S(1)}, bf16[96,1536]{1,0:T(8,128)(2,1)S(1)}, bf16[96,1536]{1,0:T(8,128)(2,1)S(1)}, bf16[96,1536]{1,0:T(8,128)(2,1)S(1)}, bf16[160,1536]{1,0:T(8,128)(2,1)S(1)}) custom-call(s32[4]{0:T(128)S(1)} %pad_add_fusion.info, bf16[2,65,384]{2,1,0:T(8,128)(2,1)S(1)} %collective-permute-done.16.returned, ...), custom_call_target="tpu_custom_call" | custom-call | flops 566231040 | bytes 4494336 | tf_op jit(solution)/shard_map/up_grad/pallas_call | solution.py:341
  70.1 7.9 %rest_grad.1 = (bf16[112,1536]{1,0:T(8,128)(2,1)S(1)}, bf16[112,1536]{1,0:T(8,128)(2,1)S(1)}, bf16[112,1536]{1,0:T(8,128)(2,1)S(1)}, bf16[112,1536]{1,0:T(8,128)(2,1)S(1)}, f32[2,65,384]{2,1,0:T(8,128)S(1)}) custom-call(s32[4]{0:T(128)S(1)} %pad_add_fusion.info, bf16[2,65,384]{2,1,0:T(8,128)(2,1)S(1)} %collective-permute-done.16.returned, ...), custom_call_target="tpu_custom_call" | custom-call | flops 566231040 | bytes 5575680 | tf_op jit(solution)/shard_map/rest_grad/pallas_call | solution.py:341
  81.1 1.6 %collective-permute-start.25 = (bf16[96,1536]{1,0:T(8,128)(2,1)S(1)}, bf16[96,1536]{1,0:T(8,128)(2,1)S(1)}, u32[]{:S(2)}, u32[]{:S(2)}) collective-permute-start(bf16[96,1536]{1,0:T(8,128)(2,1)S(1)} %add_convert_fusion.10), channel_id=1, source_target_pairs={{0,8},{4,12},{8,0},{12,4},{1,9},{5,13},{9,1},{13,5},{2,10},{6,14},... | collective-permute-start | bytes 884744 | tf_op jit(solution)/shard_map/ppermute | solution.py:354
  83.4 7.0 %collective-permute-done.31 = bf16[384,384]{1,0:T(8,128)(2,1)S(1)} collective-permute-done((bf16[384,384]{1,0:T(8,128)(2,1)S(1)}, bf16[384,384]{1,0:T(8,128)(2,1)S(1)}, u32[]{:S(2)}, u32[]{:S(2)}) %collective-permute-start.31) | collective-permute-done | bytes 294944 | tf_op jit(solution)/shard_map/ppermute | solution.py:354
  90.5 3.5 %collective-permute-start.32 = (bf16[384,384]{1,0:T(8,128)(2,1)S(1)}, bf16[384,384]{1,0:T(8,128)(2,1)S(1)}, u32[]{:S(2)}, u32[]{:S(2)}) collective-permute-start(bf16[384,384]{1,0:T(8,128)(2,1)S(1)} %add_convert_fusion.5), channel_id=1, source_target_pairs={{0,1},{3,2},{4,5},{7,6},{8,9},{11,10},{12,13},{15,14},{16,17},{19,... | collective-permute-start | bytes 884744 | tf_op jit(solution)/shard_map/ppermute | solution.py:393
  94.0 2.7 %collective-permute-done.25 = bf16[96,1536]{1,0:T(8,128)(2,1)S(1)} collective-permute-done((bf16[96,1536]{1,0:T(8,128)(2,1)S(1)}, bf16[96,1536]{1,0:T(8,128)(2,1)S(1)}, u32[]{:S(2)}, u32[]{:S(2)}) %collective-permute-start.25) | collective-permute-done | bytes 294944 | tf_op jit(solution)/shard_map/ppermute | solution.py:354
  96.8 3.5 %collective-permute-start.26 = (bf16[96,1536]{1,0:T(8,128)(2,1)S(1)}, bf16[96,1536]{1,0:T(8,128)(2,1)S(1)}, u32[]{:S(2)}, u32[]{:S(2)}) collective-permute-start(bf16[96,1536]{1,0:T(8,128)(2,1)S(1)} %add_convert_fusion.9), channel_id=1, source_target_pairs={{0,1},{3,2},{4,5},{7,6},{8,9},{11,10},{12,13},{15,14},{16,17},{19,... | collective-permute-start | bytes 884744 | tf_op jit(solution)/shard_map/ppermute | solution.py:393
  100.3 2.9 %collective-permute-done.19 = bf16[112,1536]{1,0:T(8,128)(2,1)S(1)} collective-permute-done((bf16[112,1536]{1,0:T(8,128)(2,1)S(1)}, bf16[112,1536]{1,0:T(8,128)(2,1)S(1)}, u32[]{:S(2)}, u32[]{:S(2)}) %collective-permute-start.19) | collective-permute-done | bytes 344096 | tf_op jit(solution)/shard_map/ppermute | solution.py:354
  103.3 3.5 %collective-permute-start.20 = (bf16[112,1536]{1,0:T(8,128)(2,1)S(1)}, bf16[112,1536]{1,0:T(8,128)(2,1)S(1)}, u32[]{:S(2)}, u32[]{:S(2)}) collective-permute-start(bf16[112,1536]{1,0:T(8,128)(2,1)S(1)} %add_convert_fusion.1), channel_id=1, source_target_pairs={{0,1},{3,2},{4,5},{7,6},{8,9},{11,10},{12,13},{15,14},{16,17},{19,... | collective-permute-start | bytes 1032200 | tf_op jit(solution)/shard_map/ppermute | solution.py:393
  108.4 5.1 %collective-permute-done.20 = bf16[112,1536]{1,0:T(8,128)(2,1)S(1)} collective-permute-done((bf16[112,1536]{1,0:T(8,128)(2,1)S(1)}, bf16[112,1536]{1,0:T(8,128)(2,1)S(1)}, u32[]{:S(2)}, u32[]{:S(2)}) %collective-permute-start.20) | collective-permute-done | bytes 344096 | tf_op jit(solution)/shard_map/ppermute | solution.py:393
  118.5 15.9 %collective-permute-done.28 = bf16[96,1536]{1,0:T(8,128)(2,1)S(1)} collective-permute-done((bf16[96,1536]{1,0:T(8,128)(2,1)S(1)}, bf16[96,1536]{1,0:T(8,128)(2,1)S(1)}, u32[]{:S(2)}, u32[]{:S(2)}) %collective-permute-start.28) | collective-permute-done | bytes 294944 | tf_op jit(solution)/shard_map/ppermute | solution.py:396
  136.0 3.8 %collective-permute-done.22 = bf16[112,1536]{1,0:T(8,128)(2,1)S(1)} collective-permute-done((bf16[112,1536]{1,0:T(8,128)(2,1)S(1)}, bf16[112,1536]{1,0:T(8,128)(2,1)S(1)}, u32[]{:S(2)}, u32[]{:S(2)}) %collective-permute-start.22) | collective-permute-done | bytes 344096 | tf_op jit(solution)/shard_map/ppermute | solution.py:396
  (152 shorter events, 33.2 us)
Async XLA Ops:
  5.8 9.5 %collective-permute-start.4 = (bf16[96,1152]{1,0:T(8,128)(2,1)}, bf16[96,1152]{1,0:T(8,128)(2,1)S(1)}, u32[]{:S(2)}, u32[]{:S(2)}) collective-permute-start(bf16[96,1152]{1,0:T(8,128)(2,1)} %bitcast.41), channel_id=1, source_target_pairs={{0,8},{4,12},{8,0},{12,4},{1,9},{5,13},{9,1},{13,5},{2,10},{6,14},... | collective-permute-start | bytes 663560 | tf_op jit(solution)/shard_map/ppermute | solution.py:354
  9.3 12.4 %collective-permute-start.10 = (bf16[96,1536]{1,0:T(8,128)(2,1)}, bf16[96,1536]{1,0:T(8,128)(2,1)S(1)}, u32[]{:S(2)}, u32[]{:S(2)}) collective-permute-start(bf16[96,1536]{1,0:T(8,128)(2,1)} %bitcast.30), channel_id=1, source_target_pairs={{0,8},{4,12},{8,0},{12,4},{1,9},{5,13},{9,1},{13,5},{2,10},{6,14},... | collective-permute-start | bytes 884744 | tf_op jit(solution)/shard_map/ppermute | solution.py:354
  10.7 16.9 %collective-permute-start.13 = (bf16[384,384]{1,0:T(8,128)(2,1)}, bf16[384,384]{1,0:T(8,128)(2,1)S(1)}, u32[]{:S(2)}, u32[]{:S(2)}) collective-permute-start(bf16[384,384]{1,0:T(8,128)(2,1)} %bitcast.36), channel_id=1, source_target_pairs={{0,8},{4,12},{8,0},{12,4},{1,9},{5,13},{9,1},{13,5},{2,10},{6,14},... | collective-permute-start | bytes 884744 | tf_op jit(solution)/shard_map/ppermute | solution.py:354
  11.6 16.0 %collective-permute-start.3 = (bf16[96,1152]{1,0:T(8,128)(2,1)}, bf16[96,1152]{1,0:T(8,128)(2,1)S(1)}, u32[]{:S(2)}, u32[]{:S(2)}) collective-permute-start(bf16[96,1152]{1,0:T(8,128)(2,1)} %bitcast.42), channel_id=1, source_target_pairs={{0,4},{4,0},{8,12},{12,8},{1,5},{5,1},{9,13},{13,9},{2,6},{6,2},{1... | collective-permute-start | bytes 663560 | tf_op jit(solution)/shard_map/ppermute | solution.py:354
  12.8 21.3 %collective-permute-start.9 = (bf16[96,1536]{1,0:T(8,128)(2,1)S(1)}, bf16[96,1536]{1,0:T(8,128)(2,1)S(1)}, u32[]{:S(2)}, u32[]{:S(2)}) collective-permute-start(bf16[96,1536]{1,0:T(8,128)(2,1)S(1)} %bitcast.31), channel_id=1, source_target_pairs={{0,4},{4,0},{8,12},{12,8},{1,5},{5,1},{9,13},{13,9},{2,6},{6,2},{1... | collective-permute-start | bytes 884744 | tf_op jit(solution)/shard_map/ppermute | solution.py:354
  15.3 20.1 %collective-permute-start.12 = (bf16[384,384]{1,0:T(8,128)(2,1)}, bf16[384,384]{1,0:T(8,128)(2,1)S(1)}, u32[]{:S(2)}, u32[]{:S(2)}) collective-permute-start(bf16[384,384]{1,0:T(8,128)(2,1)} %bitcast.37), channel_id=1, source_target_pairs={{0,4},{4,0},{8,12},{12,8},{1,5},{5,1},{9,13},{13,9},{2,6},{6,2},{1... | collective-permute-start | bytes 884744 | tf_op jit(solution)/shard_map/ppermute | solution.py:354
  21.6 12.5 %collective-permute-start.11 = (bf16[96,1536]{1,0:T(8,128)(2,1)S(1)}, bf16[96,1536]{1,0:T(8,128)(2,1)S(1)}, u32[]{:S(2)}, u32[]{:S(2)}) collective-permute-start(bf16[96,1536]{1,0:T(8,128)(2,1)S(1)} %collective-permute-done.10.refs_2_.refs_10_), channel_id=1, source_target_pairs={{0,4},{4,0},{8,12},{12,8},{1,5},{5,1},{9,13},{13,9},{2,6},{6,2},{1... | collective-permute-start | bytes 884744 | tf_op jit(solution)/shard_map/ppermute | solution.py:354
  27.6 7.9 %collective-permute-start.14 = (bf16[384,384]{1,0:T(8,128)(2,1)S(1)}, bf16[384,384]{1,0:T(8,128)(2,1)S(1)}, u32[]{:S(2)}, u32[]{:S(2)}) collective-permute-start(bf16[384,384]{1,0:T(8,128)(2,1)S(1)} %collective-permute-done.13.refs_2_.refs_14_.refs_6_), channel_id=1, source_target_pairs={{0,4},{4,0},{8,12},{12,8},{1,5},{5,1},{9,13},{13,9},{2,6},{6,2},{1... | collective-permute-start | bytes 884744 | tf_op jit(solution)/shard_map/ppermute | solution.py:354
  64.4 14.5 %collective-permute-start.30 = (bf16[384,384]{1,0:T(8,128)(2,1)}, bf16[384,384]{1,0:T(8,128)(2,1)}, u32[]{:S(2)}, u32[]{:S(2)}) collective-permute-start(bf16[384,384]{1,0:T(8,128)(2,1)} %get-tuple-element.58), channel_id=1, source_target_pairs={{0,4},{4,0},{8,12},{12,8},{1,5},{5,1},{9,13},{13,9},{2,6},{6,2},{1... | collective-permute-start | bytes 884744 | tf_op jit(solution)/shard_map/ppermute | solution.py:354
  66.1 16.7 %collective-permute-start.29 = (bf16[384,384]{1,0:T(8,128)(2,1)}, bf16[384,384]{1,0:T(8,128)(2,1)S(1)}, u32[]{:S(2)}, u32[]{:S(2)}) collective-permute-start(bf16[384,384]{1,0:T(8,128)(2,1)} %copy-done.28), channel_id=1, source_target_pairs={{0,4},{4,0},{8,12},{12,8},{1,5},{5,1},{9,13},{13,9},{2,6},{6,2},{1... | collective-permute-start | bytes 884744 | tf_op jit(solution)/shard_map/ppermute | solution.py:354
  69.5 10.9 %collective-permute-start.24 = (bf16[96,1536]{1,0:T(8,128)(2,1)S(1)}, bf16[96,1536]{1,0:T(8,128)(2,1)S(1)}, u32[]{:S(2)}, u32[]{:S(2)}) collective-permute-start(bf16[96,1536]{1,0:T(8,128)(2,1)S(1)} %get-tuple-element.53), channel_id=1, source_target_pairs={{0,4},{4,0},{8,12},{12,8},{1,5},{5,1},{9,13},{13,9},{2,6},{6,2},{1... | collective-permute-start | bytes 884744 | tf_op jit(solution)/shard_map/ppermute | solution.py:354
  69.6 24.4 %collective-permute-start.23 = (bf16[96,1536]{1,0:T(8,128)(2,1)S(1)}, bf16[96,1536]{1,0:T(8,128)(2,1)S(1)}, u32[]{:S(2)}, u32[]{:S(2)}) collective-permute-start(bf16[96,1536]{1,0:T(8,128)(2,1)S(1)} %get-tuple-element.51), channel_id=1, source_target_pairs={{0,4},{4,0},{8,12},{12,8},{1,5},{5,1},{9,13},{13,9},{2,6},{6,2},{1... | collective-permute-start | bytes 884744 | tf_op jit(solution)/shard_map/ppermute | solution.py:354
  78.9 21.4 %collective-permute-start.17 = (bf16[112,1536]{1,0:T(8,128)(2,1)S(1)}, bf16[112,1536]{1,0:T(8,128)(2,1)S(1)}, u32[]{:S(2)}, u32[]{:S(2)}) collective-permute-start(bf16[112,1536]{1,0:T(8,128)(2,1)S(1)} %get-tuple-element.47), channel_id=1, source_target_pairs={{0,4},{4,0},{8,12},{12,8},{1,5},{5,1},{9,13},{13,9},{2,6},{6,2},{1... | collective-permute-start | bytes 1032200 | tf_op jit(solution)/shard_map/ppermute | solution.py:354
  80.4 9.9 %collective-permute-start.31 = (bf16[384,384]{1,0:T(8,128)(2,1)S(1)}, bf16[384,384]{1,0:T(8,128)(2,1)S(1)}, u32[]{:S(2)}, u32[]{:S(2)}) collective-permute-start(bf16[384,384]{1,0:T(8,128)(2,1)S(1)} %add_convert_fusion.6), channel_id=1, source_target_pairs={{0,8},{4,12},{8,0},{12,4},{1,9},{5,13},{9,1},{13,5},{2,10},{6,14},... | collective-permute-start | bytes 884744 | tf_op jit(solution)/shard_map/ppermute | solution.py:354
  81.1 15.6 %collective-permute-start.25 = (bf16[96,1536]{1,0:T(8,128)(2,1)S(1)}, bf16[96,1536]{1,0:T(8,128)(2,1)S(1)}, u32[]{:S(2)}, u32[]{:S(2)}) collective-permute-start(bf16[96,1536]{1,0:T(8,128)(2,1)S(1)} %add_convert_fusion.10), channel_id=1, source_target_pairs={{0,8},{4,12},{8,0},{12,4},{1,9},{5,13},{9,1},{13,5},{2,10},{6,14},... | collective-permute-start | bytes 884744 | tf_op jit(solution)/shard_map/ppermute | solution.py:354
  82.8 20.4 %collective-permute-start.19 = (bf16[112,1536]{1,0:T(8,128)(2,1)S(1)}, bf16[112,1536]{1,0:T(8,128)(2,1)S(1)}, u32[]{:S(2)}, u32[]{:S(2)}) collective-permute-start(bf16[112,1536]{1,0:T(8,128)(2,1)S(1)} %add_convert_fusion.2), channel_id=1, source_target_pairs={{0,8},{4,12},{8,0},{12,4},{1,9},{5,13},{9,1},{13,5},{2,10},{6,14},... | collective-permute-start | bytes 1032200 | tf_op jit(solution)/shard_map/ppermute | solution.py:354
  90.5 16.3 %collective-permute-start.32 = (bf16[384,384]{1,0:T(8,128)(2,1)S(1)}, bf16[384,384]{1,0:T(8,128)(2,1)S(1)}, u32[]{:S(2)}, u32[]{:S(2)}) collective-permute-start(bf16[384,384]{1,0:T(8,128)(2,1)S(1)} %add_convert_fusion.5), channel_id=1, source_target_pairs={{0,1},{3,2},{4,5},{7,6},{8,9},{11,10},{12,13},{15,14},{16,17},{19,... | collective-permute-start | bytes 884744 | tf_op jit(solution)/shard_map/ppermute | solution.py:393
  96.8 10.8 %collective-permute-start.26 = (bf16[96,1536]{1,0:T(8,128)(2,1)S(1)}, bf16[96,1536]{1,0:T(8,128)(2,1)S(1)}, u32[]{:S(2)}, u32[]{:S(2)}) collective-permute-start(bf16[96,1536]{1,0:T(8,128)(2,1)S(1)} %add_convert_fusion.9), channel_id=1, source_target_pairs={{0,1},{3,2},{4,5},{7,6},{8,9},{11,10},{12,13},{15,14},{16,17},{19,... | collective-permute-start | bytes 884744 | tf_op jit(solution)/shard_map/ppermute | solution.py:393
  103.3 10.2 %collective-permute-start.20 = (bf16[112,1536]{1,0:T(8,128)(2,1)S(1)}, bf16[112,1536]{1,0:T(8,128)(2,1)S(1)}, u32[]{:S(2)}, u32[]{:S(2)}) collective-permute-start(bf16[112,1536]{1,0:T(8,128)(2,1)S(1)} %add_convert_fusion.1), channel_id=1, source_target_pairs={{0,1},{3,2},{4,5},{7,6},{8,9},{11,10},{12,13},{15,14},{16,17},{19,... | collective-permute-start | bytes 1032200 | tf_op jit(solution)/shard_map/ppermute | solution.py:393
  106.9 7.4 %collective-permute-start.33 = (bf16[384,384]{1,0:T(8,128)(2,1)S(1)}, bf16[384,384]{1,0:T(8,128)(2,1)S(1)}, u32[]{:S(2)}, u32[]{:S(2)}) collective-permute-start(bf16[384,384]{1,0:T(8,128)(2,1)S(1)} %add_convert_fusion.4), channel_id=1, source_target_pairs={{1,2},{2,1},{5,6},{6,5},{9,10},{10,9},{13,14},{14,13},{17,18},{18,... | collective-permute-start | bytes 884744 | tf_op jit(solution)/shard_map/ppermute | solution.py:394
  107.7 8.0 %collective-permute-start.27 = (bf16[96,1536]{1,0:T(8,128)(2,1)S(1)}, bf16[96,1536]{1,0:T(8,128)(2,1)S(1)}, u32[]{:S(2)}, u32[]{:S(2)}) collective-permute-start(bf16[96,1536]{1,0:T(8,128)(2,1)S(1)} %add_convert_fusion.8), channel_id=1, source_target_pairs={{1,2},{2,1},{5,6},{6,5},{9,10},{10,9},{13,14},{14,13},{17,18},{18,... | collective-permute-start | bytes 884744 | tf_op jit(solution)/shard_map/ppermute | solution.py:394
  114.4 20.8 %collective-permute-start.34 = (bf16[384,384]{1,0:T(8,128)(2,1)S(1)}, bf16[384,384]{1,0:T(8,128)(2,1)S(1)}, u32[]{:S(2)}, u32[]{:S(2)}) collective-permute-start(bf16[384,384]{1,0:T(8,128)(2,1)S(1)} %reduce-precision_convert_fusion.1), channel_id=1, source_target_pairs={{1,0},{2,3},{5,4},{6,7},{9,8},{10,11},{13,12},{14,15},{17,16},{18,... | collective-permute-start | bytes 884744 | tf_op jit(solution)/shard_map/ppermute | solution.py:396
  115.8 18.6 %collective-permute-start.28 = (bf16[96,1536]{1,0:T(8,128)(2,1)S(1)}, bf16[96,1536]{1,0:T(8,128)(2,1)S(1)}, u32[]{:S(2)}, u32[]{:S(2)}) collective-permute-start(bf16[96,1536]{1,0:T(8,128)(2,1)S(1)} %reduce-precision_convert_fusion.2), channel_id=1, source_target_pairs={{1,0},{2,3},{5,4},{6,7},{9,8},{10,11},{13,12},{14,15},{17,16},{18,... | collective-permute-start | bytes 884744 | tf_op jit(solution)/shard_map/ppermute | solution.py:396
  117.2 22.7 %collective-permute-start.22 = (bf16[112,1536]{1,0:T(8,128)(2,1)S(1)}, bf16[112,1536]{1,0:T(8,128)(2,1)S(1)}, u32[]{:S(2)}, u32[]{:S(2)}) collective-permute-start(bf16[112,1536]{1,0:T(8,128)(2,1)S(1)} %reduce-precision_convert_fusion), channel_id=1, source_target_pairs={{1,0},{2,3},{5,4},{6,7},{9,8},{10,11},{13,12},{14,15},{17,16},{18,... | collective-permute-start | bytes 1032200 | tf_op jit(solution)/shard_map/ppermute | solution.py:396
  (41 other events, 231.2 us)

commit v2 on v1

v2 whole, which is shorter than its diff:
```python
import functools

import jax
import jax.numpy as jnp
from jax import lax
from jax.experimental import pallas as pl
from jax.experimental.pallas import tpu as pltpu
from jax.sharding import PartitionSpec as P

HD = 64
PAIR = 2 * HD
EPS = 1e-06
SQRT_HALF = 0.7071067811865476
INV_ROOT_TAU = 0.3989422804014327
BF = jnp.bfloat16
F32 = jnp.float32
VMEM_BYTES = 20 * 1024 * 1024

PRE_GAIN, PRE_SHIFT, QUERY_BIAS, VALUE_BIAS, MERGE_BIAS, MID_GAIN, MID_SHIFT, DOWN_BIAS = range(8)


def padded_length(length):
    return -(-length // 16) * 16


def dot(a, b):
    return jnp.dot(a, b, preferred_element_type=F32)


def dot_nt(a, b):
    return lax.dot_general(a, b, (((1,), (1,)), ((), ())), preferred_element_type=F32)


def dot_tn(a, b):
    return lax.dot_general(a, b, (((0,), (0,)), ((), ())), preferred_element_type=F32)


def fetch(pieces, dest, sems, first, me, rows=None, column=0):
    copies = []
    for k, piece in enumerate(pieces):
        if rows is not None:
            piece = piece.at[pl.ds(0, rows), pl.ds(column, dest.shape[1])]
        count = piece.shape[0]
        start = pl.multiple_of(jnp.bitwise_xor(me, k) * count, count)
        copies.append(pltpu.make_async_copy(piece, dest.at[pl.ds(start, count)], sems.at[first + k]))
    for copy in copies:
        copy.start()
    return copies


def arrive(copies):
    for copy in copies:
        copy.wait()


def pad_images(images, scratch):
    length = images[0].shape[0]
    step = padded_length(length)
    scratch[...] = jnp.zeros_like(scratch)
    for n, image in enumerate(images):
        scratch[n * step : n * step + length, :] = image.astype(F32)
    return scratch[...]


def unpad(ref, rows, kind):
    count, length, _ = ref.shape
    step = padded_length(length)
    for n in range(count):
        ref[n] = rows[n * step : n * step + length, :].astype(kind)


def norm_parts(rows):
    mean = jnp.mean(rows, axis=-1, keepdims=True)
    centered = rows - mean
    inverse = lax.rsqrt(jnp.mean(centered * centered, axis=-1, keepdims=True) + EPS)
    return centered * inverse, inverse


def norm_backward(grad_rows, normed, inverse, gain):
    scaled = grad_rows * gain
    mean_one = jnp.mean(scaled, axis=-1, keepdims=True)
    mean_two = jnp.mean(scaled * normed, axis=-1, keepdims=True)
    return inverse * (scaled - mean_one - normed * mean_two)


def column_sum(rows):
    return jnp.sum(rows, axis=0, keepdims=True)


def half_masks():
    lane = lax.broadcasted_iota(jnp.int32, (1, PAIR), 1)
    low = (lane < HD).astype(F32)
    return low.astype(BF), (1.0 - low).astype(BF)


def both_heads(rows):
    low, high = half_masks()
    return jnp.concatenate([rows * low, rows * high], axis=0)


def beside(stacked):
    half = stacked.shape[0] // 2
    lane = lax.broadcasted_iota(jnp.int32, (half, PAIR), 1)
    return jnp.where(lane < HD, stacked[:half], stacked[half:])


def qkv(packed, n, pair, step, width):
    rows = slice(n * step, (n + 1) * step)
    return tuple(packed[rows, part * width + pair * PAIR : part * width + (pair + 1) * PAIR] for part in range(3))


def head_pairs(packed, count, length, width):
    step = padded_length(length)
    parts = [qkv(packed, n, pair, step, width) for n in range(count) for pair in range(width // PAIR)]
    return [both_heads(queries) for queries, _, _ in parts], [keys for _, keys, _ in parts], [v for _, _, v in parts]


def block(rows, n, total):
    high = rows.shape[0] // total
    return rows[n * high : (n + 1) * high]


def attention_forward(packed, mixed, count, length, width):
    step = padded_length(length)
    queries, keys, values = head_pairs(packed, count, length, width)
    scores = jnp.concatenate([dot_nt(q, k) for q, k in zip(queries, keys)], axis=0) * HD**-0.5
    lane = lax.broadcasted_iota(jnp.int32, scores.shape, 1)
    scores = jnp.where(lane < length, scores, -1e30)
    grown = jnp.exp(scores - jnp.max(scores, axis=-1, keepdims=True))
    probs = grown * (1.0 / jnp.sum(grown, axis=-1, keepdims=True))
    rounded = probs.astype(BF)
    outs = [beside(dot(block(rounded, at, len(values)), v)).astype(BF) for at, v in enumerate(values)]
    for at, out in enumerate(outs):
        n, pair = divmod(at, width // PAIR)
        mixed[n * step : (n + 1) * step, pair * PAIR : (pair + 1) * PAIR] = out
    return probs


def attention_backward(packed, probs, grad_mixed, grad_packed, count, length, width):
    step = padded_length(length)
    queries, keys, values = head_pairs(packed, count, length, width)
    pairs = width // PAIR
    incoming = [
        both_heads(grad_mixed[n * step : (n + 1) * step, pair * PAIR : (pair + 1) * PAIR])
        for n in range(count)
        for pair in range(pairs)
    ]
    grad_probs = jnp.concatenate([dot_nt(g, v) for g, v in zip(incoming, values)], axis=0)
    inner = jnp.sum(probs * grad_probs, axis=-1, keepdims=True)
    grad_scores = (probs * (grad_probs - inner)).astype(BF)
    rounded = probs.astype(BF)
    total = len(keys)
    parts = [
        (
            beside(dot(block(grad_scores, at, total), keys[at])) * HD**-0.5,
            dot_tn(block(grad_scores, at, total), queries[at]) * HD**-0.5,
            dot_tn(block(rounded, at, total), incoming[at]),
        )
        for at in range(total)
    ]
    for at, three in enumerate(parts):
        n, pair = divmod(at, pairs)
        for part, value in enumerate(three):
            column = part * width + pair * PAIR
            grad_packed[n * step : (n + 1) * step, column : column + PAIR] = value.astype(BF)


def entry_rows(rows, small):
    normed, inverse = norm_parts(rows)
    return (normed * small[PRE_GAIN : PRE_GAIN + 1] + small[PRE_SHIFT : PRE_SHIFT + 1]).astype(BF), normed, inverse


def mid_rows(middle, small):
    normed, inverse = norm_parts(middle)
    return (normed * small[MID_GAIN : MID_GAIN + 1] + small[MID_SHIFT : MID_SHIFT + 1]).astype(BF), normed, inverse


def packed_bias(small):
    query = small[QUERY_BIAS : QUERY_BIAS + 1]
    return jnp.concatenate([query, jnp.zeros_like(query), small[VALUE_BIAS : VALUE_BIAS + 1]], axis=1)


def gelu_parts(hidden):
    bell = 0.5 * (1.0 + lax.erf(hidden * SQRT_HALF))
    return hidden * bell, bell


def gelu_slope(hidden, bell):
    return bell + hidden * jnp.exp(-0.5 * hidden * hidden) * INV_ROOT_TAU


def picked_images(info, images):
    return [
        jnp.where(info[2 + n] == 0, images[0], images[1]) for n in range(images.shape[0])
    ]


def pack_kernel(heads_ref, merge_ref, *refs):
    many = (len(refs) - 3) // 2
    vectors, (out_ref, rows, *held), sems = refs[:many], refs[many : 2 * many + 2], refs[-1]
    part, wide = heads_ref.shape
    copies = [
        pltpu.make_async_copy(heads_ref, out_ref.at[pl.ds(0, part), pl.ds(0, wide)], sems.at[0]),
        pltpu.make_async_copy(merge_ref, out_ref.at[pl.ds(0, part), pl.ds(wide, merge_ref.shape[1])], sems.at[1]),
    ]
    copies += [pltpu.make_async_copy(v, held[n], sems.at[2 + n]) for n, v in enumerate(vectors)]
    for copy in copies:
        copy.start()
    rows[...] = jnp.zeros_like(rows)
    arrive(copies[2:])
    for n, vector in enumerate(held):
        rows[n : n + 1, : vector.shape[1]] = vector[...].astype(F32)
    out_ref[part:, :] = rows[...].astype(BF)
    arrive(copies[:2])


def attend_kernel(shards, info, images, *refs):
    pieces = refs[:shards]
    middle_ref, mid_ref, heads, merge, small, up_bias, rows_ref, packed, mixed, vectors, sems = refs[shards:]
    me = info[0]
    count, length, width = images.shape
    part = width // shards
    first = fetch(pieces, heads, sems, 0, me, part)
    second = fetch(pieces, merge, sems, shards, me, part, heads.shape[1])
    third = []
    for k, piece in enumerate(pieces):
        source = piece.at[pl.ds(part, 16)]
        third.append(pltpu.make_async_copy(source, vectors.at[jnp.bitwise_xor(me, k)], sems.at[2 * shards + k]))
        third[-1].start()
    rows = pad_images(picked_images(info, images), rows_ref)
    unit, _ = norm_parts(rows)
    arrive(third)
    hidden_part = up_bias.shape[1] // shards
    for at in range(shards):
        given = vectors[at].astype(F32)
        small[:, at * part : (at + 1) * part] = given[:8, :part]
        up_bias[:, at * hidden_part : (at + 1) * hidden_part] = given[8:9, :hidden_part]
    entry = (unit * small[PRE_GAIN : PRE_GAIN + 1] + small[PRE_SHIFT : PRE_SHIFT + 1]).astype(BF)
    arrive(first)
    packed[...] = (dot(entry, heads[...]) + packed_bias(small)).astype(BF)
    attention_forward(packed, mixed, count, length, width)
    arrive(second)
    middle = rows + dot(mixed[...], merge[...]) + small[MERGE_BIAS : MERGE_BIAS + 1]
    middle_ref[...] = middle
    mid_ref[...] = mid_rows(middle, small)[0]


def widen_kernel(shards, info, mid_ref, up_bias, *refs):
    act_ref, up, sems = refs[shards:]
    arrive(fetch(refs[:shards], up, sems, 0, info[0]))
    hidden = dot(mid_ref[...], up[...]) + up_bias[...]
    act_ref[...] = gelu_parts(hidden)[0].astype(BF)


def narrow_kernel(shards, info, act_ref, middle_ref, small, *refs):
    out_ref, down, sems = refs[shards:]
    arrive(fetch(refs[:shards], down, sems, 0, info[0]))
    out = middle_ref[...] + dot(act_ref[...], down[...]) + small[DOWN_BIAS : DOWN_BIAS + 1]
    unpad(out_ref, out, BF)


def both_ways_kernel(
    info,
    images,
    arrived,
    cotangent,
    small,
    up_bias,
    heads,
    merge,
    up,
    down,
    out_ref,
    sent_ref,
    packed,
    probs_ref,
    mixed,
    act_ref,
    slope_ref,
    entry_ref,
    unit_one_ref,
    inverse_one_ref,
    mid_ref,
    unit_two_ref,
    inverse_two_ref,
    rows_ref,
    grad_ref,
    grad_packed,
):
    leading = info[1] == 0
    count, length, width = images.shape
    source = [jnp.where(leading, image, arrived[n]) for n, image in enumerate(picked_images(info, images))]
    rows = pad_images(source, rows_ref)
    entry_ref[...], unit_one_ref[...], inverse_one_ref[...] = entry_rows(rows, small)
    packed[...] = (dot(entry_ref[...], heads[...]) + packed_bias(small)).astype(BF)
    probs_ref[...] = attention_forward(packed, mixed, count, length, width)
    middle = rows + dot(mixed[...], merge[...]) + small[MERGE_BIAS : MERGE_BIAS + 1]
    mid_ref[...], unit_two_ref[...], inverse_two_ref[...] = mid_rows(middle, small)
    hidden = dot(mid_ref[...], up[...]) + up_bias[...]
    act, bell = gelu_parts(hidden)
    slope_ref[...] = gelu_slope(hidden, bell)
    act_ref[...] = act.astype(BF)
    out = middle + dot(act_ref[...], down[...]) + small[DOWN_BIAS : DOWN_BIAS + 1]
    unpad(out_ref, out, BF)
    incoming = pad_images([cotangent[n] for n in range(count)], grad_ref)
    grad_hidden = (dot_nt(incoming.astype(BF), down[...]) * slope_ref[...]).astype(BF)
    grad_mid = dot_nt(grad_hidden, up[...])
    grad_middle = incoming + norm_backward(
        grad_mid, unit_two_ref[...], inverse_two_ref[...], small[MID_GAIN : MID_GAIN + 1]
    )
    grad_mixed = dot_nt(grad_middle.astype(BF), merge[...]).astype(BF)
    attention_backward(packed, probs_ref[...], grad_mixed, grad_packed, count, length, width)
    grad_entry = dot_nt(grad_packed[...], heads[...])
    grad_in = grad_middle + norm_backward(
        grad_entry, unit_one_ref[...], inverse_one_ref[...], small[PRE_GAIN : PRE_GAIN + 1]
    )
    unpad(sent_ref, grad_in, BF)


def own_gradient(info, returned, cotangent, scratch):
    leading = info[1] == 0
    return pad_images(
        [jnp.where(leading, returned[n], cotangent[n]) for n in range(cotangent.shape[0])], scratch
    )


def down_grad_kernel(shards, info, returned, cotangent, act_ref, *refs):
    outs, grad_ref = refs[:shards], refs[shards]
    incoming = own_gradient(info, returned, cotangent, grad_ref).astype(BF)
    rows = outs[0].shape[0]
    for k in range(shards):
        start = pl.multiple_of(jnp.bitwise_xor(info[0], k) * rows, rows)
        outs[k][...] = dot_tn(act_ref[:, pl.ds(start, rows)], incoming).astype(BF)


def rest_grad_kernel(
    shards,
    info,
    returned,
    cotangent,
    small,
    heads,
    merge,
    up,
    down,
    packed,
    probs_ref,
    mixed,
    slope_ref,
    entry_ref,
    unit_one_ref,
    inverse_one_ref,
    mid_ref,
    unit_two_ref,
    inverse_two_ref,
    *refs,
):
    up_outs, rest_outs = refs[:shards], refs[shards : 2 * shards]
    grad_in_ref, grad_ref, grad_packed, whole_up, whole_heads, whole_merge, extra = refs[2 * shards :]
    me, leading = info[0], info[1] == 0
    count, length, width = cotangent.shape
    part = width // shards
    incoming = own_gradient(info, returned, cotangent, grad_ref)
    extra[...] = jnp.zeros_like(extra)
    extra[DOWN_BIAS : DOWN_BIAS + 1, :] = column_sum(incoming)
    grad_hidden = (dot_nt(incoming.astype(BF), down[...]) * slope_ref[...]).astype(BF)
    whole_up[...] = dot_tn(mid_ref[...], grad_hidden).astype(BF)
    wide_sum = column_sum(grad_hidden.astype(F32))
    for n in range(wide_sum.shape[1] // width):
        extra[8 + n : 9 + n, :] = wide_sum[:, n * width : (n + 1) * width]
    grad_mid = dot_nt(grad_hidden, up[...])
    extra[MID_GAIN : MID_GAIN + 1, :] = column_sum(grad_mid * unit_two_ref[...])
    extra[MID_SHIFT : MID_SHIFT + 1, :] = column_sum(grad_mid)
    grad_middle = incoming + norm_backward(
        grad_mid, unit_two_ref[...], inverse_two_ref[...], small[MID_GAIN : MID_GAIN + 1]
    )
    grad_branch = grad_middle.astype(BF)
    extra[MERGE_BIAS : MERGE_BIAS + 1, :] = column_sum(grad_branch.astype(F32))
    whole_merge[...] = dot_tn(mixed[...], grad_branch).astype(BF)
    grad_mixed = dot_nt(grad_branch, merge[...]).astype(BF)
    attention_backward(packed, probs_ref[...], grad_mixed, grad_packed, count, length, width)
    packed_sum = column_sum(grad_packed[...].astype(F32))
    extra[QUERY_BIAS : QUERY_BIAS + 1, :] = packed_sum[:, :width]
    extra[VALUE_BIAS : VALUE_BIAS + 1, :] = packed_sum[:, 2 * width :]
    whole_heads[...] = dot_tn(entry_ref[...], grad_packed[...]).astype(BF)
    grad_entry = dot_nt(grad_packed[...], heads[...])
    extra[PRE_GAIN : PRE_GAIN + 1, :] = column_sum(grad_entry * unit_one_ref[...])
    extra[PRE_SHIFT : PRE_SHIFT + 1, :] = column_sum(grad_entry)
    grad_in = grad_middle + norm_backward(
        grad_entry, unit_one_ref[...], inverse_one_ref[...], small[PRE_GAIN : PRE_GAIN + 1]
    )
    rounded = grad_in.astype(BF).astype(F32)
    unpad(grad_in_ref, jnp.where(leading, grad_in, rounded), F32)
    wide = whole_heads.shape[1]
    for k in range(shards):
        rows = pl.ds(pl.multiple_of(jnp.bitwise_xor(me, k) * part, part), part)
        up_outs[k][...] = whole_up[rows, :]
        rest_outs[k][:part, :wide] = whole_heads[rows, :]
        rest_outs[k][:part, wide:] = whole_merge[rows, :]
        rest_outs[k][part:, :wide] = jnp.zeros((16, wide), BF)
        rest_outs[k][part:, wide:] = extra[...].astype(BF)


def column_blocks_kernel(at, *refs):
    outs = [ref for ref in refs if ref.shape != refs[0].shape]
    wide = outs[0].shape[1]
    for k, out in enumerate(outs):
        columns = pl.ds(pl.multiple_of(jnp.bitwise_xor(at[0], k) * wide, wide), wide)
        out[...] = sum(ref[:, columns].astype(F32) for ref in refs[: len(refs) - len(outs)]).astype(BF)


def call(kernel, name, info, blocks, pieces, outs, scratch, flops, earlier=(), room=VMEM_BYTES):
    space = lambda kind, many: [pl.BlockSpec(memory_space=kind)] * many
    nbytes = sum(a.size * a.dtype.itemsize for a in (*blocks, *pieces, *outs))
    scalars = () if info is None else (info,)
    used = len(scalars) + len(blocks) + len(pieces)
    return pl.pallas_call(
        lambda *refs: kernel(*refs[:used], *refs[used + len(earlier) :]),
        out_shape=outs,
        in_specs=space(pltpu.SMEM, len(scalars)) + space(pltpu.VMEM, len(blocks)) + space(pl.ANY, len(pieces) + len(earlier)),
        out_specs=space(pltpu.VMEM, len(outs)),
        scratch_shapes=scratch,
        compiler_params=pltpu.CompilerParams(vmem_limit_bytes=room),
        cost_estimate=pl.CostEstimate(flops=flops, bytes_accessed=nbytes, transcendentals=0),
        name=name,
    )(*scalars, *blocks, *pieces, *earlier)


def after(value, *others):
    return lax.optimization_barrier((value, *others))[0]


def swapped(block, axis, bit):
    return lax.ppermute(block, axis, [(i, i ^ bit) for i in range(lax.axis_size(axis))])


def bits_of(size):
    return [1 << n for n in range(size.bit_length() - 1)]


def gather_pieces(shard, axis, *earlier):
    pieces = {0: shard}
    for bit in reversed(bits_of(lax.axis_size(axis))):
        pieces.update({k ^ bit: swapped(piece if k == 0 else after(piece, *earlier), axis, bit) for k, piece in list(pieces.items())})
    return [pieces[k] for k in range(len(pieces))]


def added(*terms):
    return sum(term.astype(F32) for term in terms).astype(BF)


def scatter_steps(pieces, axis):
    pieces = dict(enumerate(pieces))
    *nearer, last = bits_of(lax.axis_size(axis))
    for bit in nearer:
        for k in sorted((k for k in pieces if not k & bit), reverse=True):
            received = swapped(pieces.pop(k ^ bit), axis, bit)
            pieces[k] = added(pieces[k], received) if k & last else (pieces[k], received)
    yield pieces[last]
    kept = pieces[0] if isinstance(pieces[0], tuple) else (pieces[0],)
    yield (*kept, swapped(pieces[last], axis, last))


def together(*values):
    return lax.optimization_barrier(values)


def rounded(*terms):
    return lax.reduce_precision(sum(term.astype(F32) for term in terms), 8, 7).astype(BF)


def chosen(at, options):
    while len(options) > 1:
        options = [jnp.where((at & 1) != 0, odd, even) for even, odd in zip(options[::2], options[1::2])]
        at = at >> 1
    return options[0]


def column_blocks(at, terms, count):
    high, wide = terms[0].shape
    shapes = (jax.ShapeDtypeStruct((high, wide // count), BF),) * count
    return call(column_blocks_kernel, "column_blocks", at.reshape(1), terms, (), shapes, [], 1)


def totals_over_line(down_sum, up_steps, rest_steps, axis):
    at = lax.axis_index(axis).astype(jnp.int32)
    size = lax.axis_size(axis)
    inwards = lambda block: lax.ppermute(block, axis, [(0, 1), (3, 2)])
    across = lambda block: lax.ppermute(block, axis, [(1, 2), (2, 1)])
    outwards = lambda block: lax.ppermute(block, axis, [(1, 0), (2, 3)])
    finished = lambda kept, received: jnp.where((at == 0) | (at == 3), received, kept).astype(F32)
    others = lambda blocks: [swapped(blocks[k], axis, k) for k in range(1, size)]

    rest_first = next(rest_steps)
    *up_terms, up_last = next(up_steps)
    up_last, down_in, rest_first = together(up_last, inwards(down_sum), rest_first)
    up_sum, down_half = added(*up_terms, up_last), added(down_sum, down_in)

    *rest_terms, rest_last = next(rest_steps)
    rest_last, down_across, up_in = together(rest_last, across(down_half), inwards(up_sum))
    blocks = column_blocks(at, (*rest_terms, rest_last), size)
    down_full, up_half = rounded(down_half, down_across), added(up_sum, up_in)

    down_out, up_across, *received = together(outwards(down_full), across(up_half), *others(blocks))
    own, up_full = rounded(blocks[0], *received), rounded(up_half, up_across)

    full = [own, *others([own] * size)]
    rest_total = [chosen(at, [full[n ^ k] for k in range(size)]).astype(F32) for n in range(size)]
    return (
        finished(down_full, down_out),
        finished(up_full, outwards(up_full)),
        rest_total,
        up_sum,
    )


def totals_over(down_sum, up_steps, rest_steps, axis):
    if lax.axis_size(axis) == 4:
        return totals_over_line(down_sum, up_steps, rest_steps, axis)
    next(rest_steps)
    up_sum, rest_sum = added(*next(up_steps)), added(*next(rest_steps))
    down, up, rest = (total.astype(F32) for total in lax.psum((down_sum, up_sum, rest_sum), axis))
    return down, up, jnp.split(rest, 4, axis=1), up_sum


def local(
    images,
    slot_image,
    cotangent,
    pre_gain,
    pre_shift,
    heads_weight,
    query_bias,
    value_bias,
    merge_weight,
    merge_bias,
    mid_gain,
    mid_shift,
    up_weight,
    up_bias,
    down_weight,
    down_bias,
):
    me = lax.axis_index("fsdp").astype(jnp.int32)
    section = lax.axis_index("section").astype(jnp.int32)
    shards = lax.axis_size("fsdp")
    info = jnp.concatenate([jnp.stack([me, section]), slot_image[0]])
    count, length, width = images.shape
    tall = count * padded_length(length)
    part = width // shards
    wide = heads_weight.shape[2]
    hidden_width = up_weight.shape[2]

    shape = jax.ShapeDtypeStruct
    scratch_rows = pltpu.VMEM((tall, width), F32)
    scratch_packed = pltpu.VMEM((tall, wide), BF)
    scratch_mixed = pltpu.VMEM((tall, width), BF)
    sems = lambda many: pltpu.SemaphoreType.DMA((many * shards,))
    bind = lambda kernel: functools.partial(kernel, shards)
    work = 2 * tall * width
    full_heads, full_merge = shape((width, wide), BF), shape((width, width), BF)
    full_up, full_down = shape((width, hidden_width), BF), shape((hidden_width, width), BF)
    rows_wide, rows_bf, column = shape((tall, width), F32), shape((tall, width), BF), shape((tall, 1), F32)

    (mix,) = call(
        pack_kernel,
        "pack",
        None,
        (),
        (
            heads_weight[0],
            merge_weight[0],
            pre_gain,
            pre_shift,
            query_bias,
            value_bias,
            merge_bias,
            mid_gain,
            mid_shift,
            down_bias,
            up_bias,
        ),
        (shape((part + 16, wide + width), BF),),
        [pltpu.VMEM((16, wide + width), F32)]
        + [pltpu.VMEM((1, part), BF)] * 8
        + [pltpu.VMEM(up_bias.shape, BF), pltpu.SemaphoreType.DMA((11,))],
        1,
        room=56 * 1024 * 1024,
    )
    up_pieces = gather_pieces(up_weight[0], "fsdp")
    mix_pieces = gather_pieces(mix, "fsdp", up_pieces[shards // 2])

    middle, mid, heads, merge, small, wide_bias = call(
        bind(attend_kernel),
        "attend",
        info,
        (images,),
        mix_pieces,
        (rows_wide, rows_bf, full_heads, full_merge, shape((8, width), F32), shape((1, hidden_width), F32)),
        [
            scratch_rows,
            scratch_packed,
            scratch_mixed,
            pltpu.VMEM((shards, 16, wide + width), BF),
            sems(3),
        ],
        work * (wide + width),
    )
    down_pieces = gather_pieces(down_weight[0], "fsdp", mid)
    act, up = call(
        bind(widen_kernel),
        "widen",
        info,
        (mid, wide_bias),
        up_pieces,
        (shape((tall, hidden_width), BF), full_up),
        [sems(1)],
        work * hidden_width,
        (down_pieces[shards // 2],),
    )
    first_out, down = call(
        bind(narrow_kernel),
        "narrow",
        info,
        (act, middle, small),
        down_pieces,
        (shape(images.shape, BF), full_down),
        [sems(1)],
        work * hidden_width,
    )
    arrived = lax.ppermute(first_out, "section", [(0, 1)])

    layer_out, sent, packed, probs, mixed, act, slope, *kept = call(
        both_ways_kernel,
        "both_ways",
        info,
        (images, arrived, cotangent, small, wide_bias, heads, merge, up, down),
        (),
        (
            shape(images.shape, BF),
            shape(images.shape, BF),
            shape((tall, wide), BF),
            shape((2 * tall * (width // PAIR), tall // count), F32),
            rows_bf,
            shape((tall, hidden_width), BF),
            shape((tall, hidden_width), F32),
            rows_bf,
            rows_wide,
            column,
            rows_bf,
            rows_wide,
            column,
        ),
        [scratch_rows, scratch_rows, scratch_packed],
        2 * work * (wide + width + 2 * hidden_width),
    )
    returned = lax.ppermute(sent, "section", [(1, 0)])

    down_grads = call(
        bind(down_grad_kernel),
        "down_grad",
        info,
        (returned, cotangent, act),
        (),
        (shape((hidden_width // shards, width), BF),) * shards,
        [scratch_rows],
        work * hidden_width,
    )
    down_chain = scatter_steps(down_grads, "fsdp")
    down_first = next(down_chain)
    *grads, grad_in = call(
        bind(rest_grad_kernel),
        "rest_grad",
        info,
        (returned, cotangent, small, heads, merge, up, down, packed, probs, mixed, slope, *kept),
        (),
        (shape((part, hidden_width), BF),) * shards
        + (shape((part + 16, wide + width), BF),) * shards
        + (shape(images.shape, F32),),
        [
            scratch_rows,
            scratch_packed,
            pltpu.VMEM((width, hidden_width), BF),
            pltpu.VMEM((width, wide), BF),
            pltpu.VMEM((width, width), BF),
            pltpu.VMEM((16, width), F32),
        ],
        2 * work * (wide + width + 2 * hidden_width),
        (down_first,),
    )
    down_sum = added(*next(down_chain))
    up_chain = scatter_steps([after(one, down_sum) for one in grads[:shards]], "fsdp")
    up_first = next(up_chain)
    rest_chain = scatter_steps([after(one, down_sum, up_first) for one in grads[shards:]], "fsdp")
    down_total, up_total, rest_total, up_sum = totals_over(down_sum, up_chain, rest_chain, "dp")
    layer_out, grad_in = after(layer_out, up_sum), after(grad_in, up_sum)

    heads_total = jnp.concatenate([block[:part] for block in rest_total[:3]], axis=1)
    merge_total = rest_total[3][:part]
    vector_total = lax.dynamic_slice(rest_total[3], (part, me * part), (8, part))
    up_bias_total = lax.dynamic_slice(rest_total[3], (part + 8 + me, 0), (1, width))
    row = lambda n: vector_total[n : n + 1]
    return (
        layer_out[None],
        grad_in[None],
        row(PRE_GAIN),
        row(PRE_SHIFT),
        heads_total[None],
        row(QUERY_BIAS),
        row(VALUE_BIAS),
        merge_total[None],
        row(MERGE_BIAS),
        row(MID_GAIN),
        row(MID_SHIFT),
        up_total[None],
        up_bias_total,
        down_total[None],
        row(DOWN_BIAS),
    )


def solution(mesh):
    vector, matrix = P("section", "fsdp"), P("section", "fsdp", None)
    rows = P("section", ("fsdp", "dp"), None, None)
    weights = (
        vector,
        vector,
        matrix,
        vector,
        vector,
        matrix,
        vector,
        vector,
        vector,
        matrix,
        vector,
        matrix,
        vector,
    )
    blocks = P(("fsdp", "dp"), None, None)
    return jax.shard_map(
        local,
        mesh=mesh,
        in_specs=(blocks, P(("fsdp", "dp"), None), blocks, *weights),
        out_specs=(rows, rows, *weights),
        check_vma=False,
    )
```

time: 143 us -> 121 us (0.85)
  Pallas kernels: 28.9 us -> 17.1 us
  waiting for transfers between devices: 61.5 us -> 54.8 us
  local copies, waits for them, and re-layouts: 10.9 us -> 5.28 us
  starting transfers between devices: 34.6 us -> 38.3 us
    ppermute x9 -> x6, waiting for transfers between devices: 24.8 us -> 11.3 us  [the longest x2 9.59 us: totals_over_line(): inwards = lambda block: lax.ppermute(block, axis, [(0, 1), (3, 2)])]
    pallas_call x7 -> x8, Pallas kernels: 28.9 us -> 17.1 us  [call(): pl.pallas_call(lambda *refs: kernel(*refs[:used], *refs[used + len(earlie...]
    ppermute x24, starting transfers between devices: 13.1 us -> 21.4 us  [swapped(): lax.ppermute(block, axis, [(i, i ^ bit) for i in range(lax.axis_size(axis...]
    ppermute x24, waiting for transfers between devices: 28.9 us -> 35.5 us  [swapped(): lax.ppermute(block, axis, [(i, i ^ bit) for i in range(lax.axis_size(axis...]
    ppermute x9 -> x6, starting transfers between devices: 16.4 us -> 11.9 us  [the longest x2 7.93 us: totals_over_line(): inwards = lambda block: lax.ppermute(block, axis, [(0, 1), (3, 2)])]
    unnamed x64 -> x12, local copies, waits for them, and re-layouts: 7.13 us -> 3.42 us
  transfers between devices with their start and end apart: 35 -> 32, of which waited for: 13 -> 16; matrix products, arithmetic and copies ran while one was open for 6% -> 6% of each run, Pallas kernels for 11% -> 6%
where the time goes in v2:
time: 121 us
  waiting for transfers between devices  54.8 us (45%)
  starting transfers between devices  38.3 us (32%)
  Pallas kernels  17.1 us (14%)
  local copies, waits for them, and re-layouts  5.28 us (4%)
  other arithmetic  4.14 us (3%)
    ppermute x24, waiting for transfers between devices, swapped(): lax.ppermute(block, axis, [(i, i ^ bit) for i in range(lax.axis_size(axis...  35.5 us
    ppermute x24, starting transfers between devices, swapped(): lax.ppermute(block, axis, [(i, i ^ bit) for i in range(lax.axis_size(axis...  21.4 us
    pallas_call x8, Pallas kernels, call(): pl.pallas_call(lambda *refs: kernel(*refs[:used], *refs[used + len(earlie...  17.1 us
    ppermute x2, waiting for transfers between devices, totals_over_line(): inwards = lambda block: lax.ppermute(block, axis, [(0, 1), (3, 2)])  9.59 us
    ppermute x2, starting transfers between devices, totals_over_line(): inwards = lambda block: lax.ppermute(block, axis, [(0, 1), (3, 2)])  7.93 us
    ppermute x1, waiting for transfers between devices, local(): returned = lax.ppermute(sent, 'section', [(1, 0)])  5.34 us
    ppermute x1, starting transfers between devices, local(): arrived = lax.ppermute(first_out, 'section', [(0, 1)])  3.68 us
    unnamed x12, local copies, waits for them, and re-layouts  3.42 us
  transfers between devices with their start and end apart: 32, of which 16 were waited for; matrix products, arithmetic and copies ran while one was open for 6% of the time, Pallas kernels for 6%

profile of v2, /device:TPU:0, one launch (start us, length us, event | category | flops | bytes accessed | tf_op | source)
XLA Modules:
  0.0 120.6 jit_solution(12677017860659507106)
XLA Ops:
  0.7 1.9 %pack.1.refs_2_ = bf16[112,1536]{1,0:T(8,128)(2,1)} custom-call(bf16[96,1152]{1,0:T(8,128)(2,1)} %bitcast.31, bf16[96,384]{1,0:T(8,128)(2,1)} %bitcast.32, bf16[1,96]{1,0:T(2,128)(2,1)} %refs_2_.3, bf16[1,96]{1,0:T(2,128)(2,1)} %refs_3_.2, bf16[1,96]{1,0:T(2,128)(2,1)} %refs_4_.1, bf16[1,96]{1,0:T(2,128)(2,1)} %refs_5_.1, bf16[1,96]{1,0:T(2,128)(2,1)} %refs_6_.1, ...), custom_call_target="tpu_custom_call" | custom-call | flops 1 | bytes 641280 | tf_op jit(solution)/shard_map/pack/pallas_call | solution.py:417
  2.5 3.0 %collective-permute-start.1 = (bf16[112,1536]{1,0:T(8,128)(2,1)}, bf16[112,1536]{1,0:T(8,128)(2,1)S(1)}, u32[]{:S(2)}, u32[]{:S(2)}) collective-permute-start(bf16[112,1536]{1,0:T(8,128)(2,1)} %pack.1.refs_2_), channel_id=1, source_target_pairs={{0,8},{4,12},{8,0},{12,4},{1,9},{5,13},{9,1},{13,5},{2,10},{6,14},... | collective-permute-start | bytes 1032200 | tf_op jit(solution)/shard_map/ppermute | solution.py:434
  5.6 14.5 %collective-permute-done.2.refs_5_ = bf16[96,1536]{1,0:T(8,128)(2,1)S(1)} collective-permute-done((bf16[96,1536]{1,0:T(8,128)(2,1)}, bf16[96,1536]{1,0:T(8,128)(2,1)S(1)}, u32[]{:S(2)}, u32[]{:S(2)}) %collective-permute-start.2) | collective-permute-done | bytes 294944 | tf_op jit(solution)/shard_map/ppermute | solution.py:434
  20.1 1.7 %collective-permute-start.6 = (bf16[384,384]{1,0:T(8,128)(2,1)}, bf16[384,384]{1,0:T(8,128)(2,1)S(1)}, u32[]{:S(2)}, u32[]{:S(2)}) collective-permute-start(bf16[384,384]{1,0:T(8,128)(2,1)} %bitcast.26), channel_id=1, source_target_pairs={{0,8},{4,12},{8,0},{12,4},{1,9},{5,13},{9,1},{13,5},{2,10},{6,14},... | collective-permute-start | bytes 884744 | tf_op jit(solution)/shard_map/ppermute | solution.py:434
  25.2 2.7 %attend.1 = (f32[160,384]{1,0:T(8,128)S(1)}, bf16[160,384]{1,0:T(8,128)(2,1)S(1)}, bf16[384,1152]{1,0:T(8,128)(2,1)S(1)}, bf16[384,384]{1,0:T(8,128)(2,1)S(1)}, ...) custom-call(s32[4]{0:T(128)S(1)} %pad_add_fusion.refs_0_, bf16[2,65,384]{2,1,0:T(8,128)(2,1)S(1)} %copy.32.refs_1_, ...), custom_call_target="tpu_custom_call" | custom-call | flops 188743680 | bytes 3042816 | tf_op jit(solution)/shard_map/attend/pallas_call | solution.py:417
  28.0 1.8 %collective-permute-done.6.refs_7_.refs_6_ = bf16[384,384]{1,0:T(8,128)(2,1)S(1)} collective-permute-done((bf16[384,384]{1,0:T(8,128)(2,1)}, bf16[384,384]{1,0:T(8,128)(2,1)S(1)}, u32[]{:S(2)}, u32[]{:S(2)}) %collective-permute-start.6) | collective-permute-done | bytes 294944 | tf_op jit(solution)/shard_map/ppermute | solution.py:434
  32.6 3.7 %collective-permute-start.9 = (bf16[2,65,384]{2,1,0:T(8,128)(2,1)S(1)}, bf16[2,65,384]{2,1,0:T(8,128)(2,1)S(1)}, u32[]{:S(2)}, u32[]{:S(2)}) collective-permute-start(bf16[2,65,384]{2,1,0:T(8,128)(2,1)S(1)} %get-tuple-element.84), channel_id=1, source_target_pairs={{0,16},{1,17},{2,18},{3,19},{4,20},{5,21},{6,22},{7,23},{8,24},{9,... | collective-permute-start | bytes 299528 | tf_op jit(solution)/shard_map/ppermute | solution.py:631
  36.3 2.7 %collective-permute-done.9.refs_2_ = bf16[2,65,384]{2,1,0:T(8,128)(2,1)S(1)} collective-permute-done((bf16[2,65,384]{2,1,0:T(8,128)(2,1)S(1)}, bf16[2,65,384]{2,1,0:T(8,128)(2,1)S(1)}, u32[]{:S(2)}, u32[]{:S(2)}) %collective-permute-start.9) | collective-permute-done | bytes 99872 | tf_op jit(solution)/shard_map/ppermute | solution.py:631
  39.0 5.0 %both_ways.1 = (bf16[2,65,384]{2,1,0:T(8,128)(2,1)S(1)}, bf16[2,65,384]{2,1,0:T(8,128)(2,1)S(1)}, bf16[160,1152]{1,0:T(8,128)(2,1)S(1)}, f32[960,80]{1,0:T(8,128...) custom-call(s32[4]{0:T(128)S(1)} %pad_add_fusion.refs_0_, ...), custom_call_target="tpu_custom_call" | custom-call | flops 1132462080 | bytes 7068416 | tf_op jit(solution)/shard_map/both_ways/pallas_call | solution.py:417
  45.4 5.3 %collective-permute-done.10.refs_1_ = bf16[2,65,384]{2,1,0:T(8,128)(2,1)S(1)} collective-permute-done((bf16[2,65,384]{2,1,0:T(8,128)(2,1)S(1)}, bf16[2,65,384]{2,1,0:T(8,128)(2,1)S(1)}, u32[]{:S(2)}, u32[]{:S(2)}) %collective-permute-start.10) | collective-permute-done | bytes 99872 | tf_op jit(solution)/shard_map/ppermute | solution.py:657
  53.6 1.6 %collective-permute-start.13 = (bf16[384,384]{1,0:T(8,128)(2,1)S(1)}, bf16[384,384]{1,0:T(8,128)(2,1)S(1)}, u32[]{:S(2)}, u32[]{:S(2)}) collective-permute-start(bf16[384,384]{1,0:T(8,128)(2,1)S(1)} %add_convert_fusion.6.refs_18_), channel_id=1, source_target_pairs={{0,8},{4,12},{8,0},{12,4},{1,9},{5,13},{9,1},{13,5},{2,10},{6,14},... | collective-permute-start | bytes 884744 | tf_op jit(solution)/shard_map/ppermute | solution.py:434
  55.2 3.7 %rest_grad.1 = (bf16[96,1536]{1,0:T(8,128)(2,1)S(1)}, bf16[96,1536]{1,0:T(8,128)(2,1)S(1)}, bf16[96,1536]{1,0:T(8,128)(2,1)S(1)}, bf16[96,1536]{1,0:T(8,128)(2,1...) custom-call(s32[4]{0:T(128)S(1)} %pad_add_fusion.refs_0_, ...), custom_call_target="tpu_custom_call" | custom-call | flops 1132462080 | bytes 9026816 | tf_op jit(solution)/shard_map/rest_grad/pallas_call | solution.py:417
  58.9 3.8 %collective-permute-done.13 = bf16[384,384]{1,0:T(8,128)(2,1)S(1)} collective-permute-done((bf16[384,384]{1,0:T(8,128)(2,1)S(1)}, bf16[384,384]{1,0:T(8,128)(2,1)S(1)}, u32[]{:S(2)}, u32[]{:S(2)}) %collective-permute-start.13) | collective-permute-done | bytes 294944 | tf_op jit(solution)/shard_map/ppermute | solution.py:434
  62.9 1.6 %collective-permute-done.15 = bf16[96,1536]{1,0:T(8,128)(2,1)S(1)} collective-permute-done((bf16[96,1536]{1,0:T(8,128)(2,1)S(1)}, bf16[96,1536]{1,0:T(8,128)(2,1)S(1)}, u32[]{:S(2)}, u32[]{:S(2)}) %collective-permute-start.15) | collective-permute-done | bytes 294944 | tf_op jit(solution)/shard_map/ppermute | solution.py:434
  64.8 3.5 %collective-permute-start.17 = (bf16[384,384]{1,0:T(8,128)(2,1)S(1)}, bf16[384,384]{1,0:T(8,128)(2,1)S(1)}, u32[]{:S(2)}, u32[]{:S(2)}) collective-permute-start(bf16[384,384]{1,0:T(8,128)(2,1)S(1)} %add_convert_fusion.5), channel_id=1, source_target_pairs={{0,1},{3,2},{4,5},{7,6},{8,9},{11,10},{12,13},{15,14},{16,17},{19,... | collective-permute-start | bytes 884744 | tf_op jit(solution)/shard_map/ppermute | solution.py:488
  70.6 4.4 %collective-permute-done.17 = bf16[384,384]{1,0:T(8,128)(2,1)S(1)} collective-permute-done((bf16[384,384]{1,0:T(8,128)(2,1)S(1)}, bf16[384,384]{1,0:T(8,128)(2,1)S(1)}, u32[]{:S(2)}, u32[]{:S(2)}) %collective-permute-start.17) | collective-permute-done | bytes 294944 | tf_op jit(solution)/shard_map/ppermute | solution.py:488
  75.1 3.2 %collective-permute-done.16 = bf16[96,1536]{1,0:T(8,128)(2,1)S(1)} collective-permute-done((bf16[96,1536]{1,0:T(8,128)(2,1)S(1)}, bf16[96,1536]{1,0:T(8,128)(2,1)S(1)}, u32[]{:S(2)}, u32[]{:S(2)}) %collective-permute-start.16) | collective-permute-done | bytes 294944 | tf_op jit(solution)/shard_map/ppermute | solution.py:434
  79.1 4.4 %collective-permute-start.22 = (bf16[96,1536]{1,0:T(8,128)(2,1)S(1)}, bf16[96,1536]{1,0:T(8,128)(2,1)S(1)}, u32[]{:S(2)}, u32[]{:S(2)}) collective-permute-start(bf16[96,1536]{1,0:T(8,128)(2,1)S(1)} %add_convert_fusion.3), channel_id=1, source_target_pairs={{0,1},{3,2},{4,5},{7,6},{8,9},{11,10},{12,13},{15,14},{16,17},{19,... | collective-permute-start | bytes 884744 | tf_op jit(solution)/shard_map/ppermute | solution.py:488
  83.7 5.2 %collective-permute-done.22 = bf16[96,1536]{1,0:T(8,128)(2,1)S(1)} collective-permute-done((bf16[96,1536]{1,0:T(8,128)(2,1)S(1)}, bf16[96,1536]{1,0:T(8,128)(2,1)S(1)}, u32[]{:S(2)}, u32[]{:S(2)}) %collective-permute-start.22) | collective-permute-done | bytes 294944 | tf_op jit(solution)/shard_map/ppermute | solution.py:488
  91.2 4.2 %collective-permute-start.25 = (bf16[112,384]{1,0:T(8,128)(2,1)S(1)}, bf16[112,384]{1,0:T(8,128)(2,1)S(1)}, u32[]{:S(2)}, u32[]{:S(2)}) collective-permute-start(bf16[112,384]{1,0:T(8,128)(2,1)S(1)} %get-tuple-element.131), channel_id=1, source_target_pairs={{0,1},{1,0},{2,3},{3,2},{4,5},{5,4},{6,7},{7,6},{8,9},{9,8},{10,11... | collective-permute-start | bytes 258056 | tf_op jit(solution)/shard_map/ppermute | solution.py:434
  99.4 5.2 %collective-permute-done.25 = bf16[112,384]{1,0:T(8,128)(2,1)S(1)} collective-permute-done((bf16[112,384]{1,0:T(8,128)(2,1)S(1)}, bf16[112,384]{1,0:T(8,128)(2,1)S(1)}, u32[]{:S(2)}, u32[]{:S(2)}) %collective-permute-start.25) | collective-permute-done | bytes 86048 | tf_op jit(solution)/shard_map/ppermute | solution.py:434
  104.6 1.5 %collective-permute-done.26 = bf16[112,384]{1,0:T(8,128)(2,1)S(1)} collective-permute-done((bf16[112,384]{1,0:T(8,128)(2,1)S(1)}, bf16[112,384]{1,0:T(8,128)(2,1)S(1)}, u32[]{:S(2)}, u32[]{:S(2)}) %collective-permute-start.26) | collective-permute-done | bytes 86048 | tf_op jit(solution)/shard_map/ppermute | solution.py:434
  108.9 1.7 %collective-permute-start.30 = (bf16[112,384]{1,0:T(8,128)(2,1)S(1)}, bf16[112,384]{1,0:T(8,128)(2,1)S(1)}, u32[]{:S(2)}, u32[]{:S(2)}) collective-permute-start(bf16[112,384]{1,0:T(8,128)(2,1)S(1)} %reduce-precision_convert_fusion.2), channel_id=1, source_target_pairs={{0,3},{1,2},{2,1},{3,0},{4,7},{5,6},{6,5},{7,4},{8,11},{9,10},{10,... | collective-permute-start | bytes 258056 | tf_op jit(solution)/shard_map/ppermute | solution.py:434
  118.1 1.6 %collective-permute-done.31 = bf16[96,1536]{1,0:T(8,128)(2,1)S(1)} collective-permute-done((bf16[96,1536]{1,0:T(8,128)(2,1)S(1)}, bf16[96,1536]{1,0:T(8,128)(2,1)S(1)}, u32[]{:S(2)}, u32[]{:S(2)}) %collective-permute-start.31) | collective-permute-done | bytes 294944 | tf_op jit(solution)/shard_map/ppermute | solution.py:490
  (81 shorter events, 31.5 us)
Async XLA Ops:
  2.5 17.6 %collective-permute-start.1 = (bf16[112,1536]{1,0:T(8,128)(2,1)}, bf16[112,1536]{1,0:T(8,128)(2,1)S(1)}, u32[]{:S(2)}, u32[]{:S(2)}) collective-permute-start(bf16[112,1536]{1,0:T(8,128)(2,1)} %pack.1.refs_2_), channel_id=1, source_target_pairs={{0,8},{4,12},{8,0},{12,4},{1,9},{5,13},{9,1},{13,5},{2,10},{6,14},... | collective-permute-start | bytes 1032200 | tf_op jit(solution)/shard_map/ppermute | solution.py:434
  5.5 14.6 %collective-permute-start.2 = (bf16[96,1536]{1,0:T(8,128)(2,1)}, bf16[96,1536]{1,0:T(8,128)(2,1)S(1)}, u32[]{:S(2)}, u32[]{:S(2)}) collective-permute-start(bf16[96,1536]{1,0:T(8,128)(2,1)} %bitcast.23), channel_id=1, source_target_pairs={{0,8},{4,12},{8,0},{12,4},{1,9},{5,13},{9,1},{13,5},{2,10},{6,14},... | collective-permute-start | bytes 884744 | tf_op jit(solution)/shard_map/ppermute | solution.py:434
  5.6 18.4 %collective-permute-start = (bf16[112,1536]{1,0:T(8,128)(2,1)}, bf16[112,1536]{1,0:T(8,128)(2,1)S(1)}, u32[]{:S(2)}, u32[]{:S(2)}) collective-permute-start(bf16[112,1536]{1,0:T(8,128)(2,1)} %pack.1.refs_2_), channel_id=1, source_target_pairs={{0,4},{4,0},{8,12},{12,8},{1,5},{5,1},{9,13},{13,9},{2,6},{6,2},{1... | collective-permute-start | bytes 1032200 | tf_op jit(solution)/shard_map/ppermute | solution.py:434
  20.1 9.6 %collective-permute-start.6 = (bf16[384,384]{1,0:T(8,128)(2,1)}, bf16[384,384]{1,0:T(8,128)(2,1)S(1)}, u32[]{:S(2)}, u32[]{:S(2)}) collective-permute-start(bf16[384,384]{1,0:T(8,128)(2,1)} %bitcast.26), channel_id=1, source_target_pairs={{0,8},{4,12},{8,0},{12,4},{1,9},{5,13},{9,1},{13,5},{2,10},{6,14},... | collective-permute-start | bytes 884744 | tf_op jit(solution)/shard_map/ppermute | solution.py:434
  21.9 7.9 %collective-permute-start.4 = (bf16[96,1536]{1,0:T(8,128)(2,1)}, bf16[96,1536]{1,0:T(8,128)(2,1)S(1)}, u32[]{:S(2)}, u32[]{:S(2)}) collective-permute-start(bf16[96,1536]{1,0:T(8,128)(2,1)} %bitcast.24), channel_id=1, source_target_pairs={{0,4},{4,0},{8,12},{12,8},{1,5},{5,1},{9,13},{13,9},{2,6},{6,2},{1... | collective-permute-start | bytes 884744 | tf_op jit(solution)/shard_map/ppermute | solution.py:434
  22.1 9.0 %collective-permute-start.7 = (bf16[384,384]{1,0:T(8,128)(2,1)}, bf16[384,384]{1,0:T(8,128)(2,1)S(1)}, u32[]{:S(2)}, u32[]{:S(2)}) collective-permute-start(bf16[384,384]{1,0:T(8,128)(2,1)} %bitcast.27), channel_id=1, source_target_pairs={{0,4},{4,0},{8,12},{12,8},{1,5},{5,1},{9,13},{13,9},{2,6},{6,2},{1... | collective-permute-start | bytes 884744 | tf_op jit(solution)/shard_map/ppermute | solution.py:434
  32.6 6.4 %collective-permute-start.9 = (bf16[2,65,384]{2,1,0:T(8,128)(2,1)S(1)}, bf16[2,65,384]{2,1,0:T(8,128)(2,1)S(1)}, u32[]{:S(2)}, u32[]{:S(2)}) collective-permute-start(bf16[2,65,384]{2,1,0:T(8,128)(2,1)S(1)} %get-tuple-element.84), channel_id=1, source_target_pairs={{0,16},{1,17},{2,18},{3,19},{4,20},{5,21},{6,22},{7,23},{8,24},{9,... | collective-permute-start | bytes 299528 | tf_op jit(solution)/shard_map/ppermute | solution.py:631
  44.1 6.6 %collective-permute-start.10 = (bf16[2,65,384]{2,1,0:T(8,128)(2,1)S(1)}, bf16[2,65,384]{2,1,0:T(8,128)(2,1)S(1)}, u32[]{:S(2)}, u32[]{:S(2)}) collective-permute-start(bf16[2,65,384]{2,1,0:T(8,128)(2,1)S(1)} %get-tuple-element.90), channel_id=1, source_target_pairs={{16,0},{17,1},{18,2},{19,3},{20,4},{21,5},{22,6},{23,7},{24,8},{25... | collective-permute-start | bytes 299528 | tf_op jit(solution)/shard_map/ppermute | solution.py:657
  52.0 6.9 %collective-permute-start.12 = (bf16[384,384]{1,0:T(8,128)(2,1)S(1)}, bf16[384,384]{1,0:T(8,128)(2,1)S(1)}, u32[]{:S(2)}, u32[]{:S(2)}) collective-permute-start(bf16[384,384]{1,0:T(8,128)(2,1)S(1)} %get-tuple-element.106), channel_id=1, source_target_pairs={{0,4},{4,0},{8,12},{12,8},{1,5},{5,1},{9,13},{13,9},{2,6},{6,2},{1... | collective-permute-start | bytes 884744 | tf_op jit(solution)/shard_map/ppermute | solution.py:434
  53.6 9.1 %collective-permute-start.13 = (bf16[384,384]{1,0:T(8,128)(2,1)S(1)}, bf16[384,384]{1,0:T(8,128)(2,1)S(1)}, u32[]{:S(2)}, u32[]{:S(2)}) collective-permute-start(bf16[384,384]{1,0:T(8,128)(2,1)S(1)} %add_convert_fusion.6.refs_18_), channel_id=1, source_target_pairs={{0,8},{4,12},{8,0},{12,4},{1,9},{5,13},{9,1},{13,5},{2,10},{6,14},... | collective-permute-start | bytes 884744 | tf_op jit(solution)/shard_map/ppermute | solution.py:434
  64.8 10.3 %collective-permute-start.17 = (bf16[384,384]{1,0:T(8,128)(2,1)S(1)}, bf16[384,384]{1,0:T(8,128)(2,1)S(1)}, u32[]{:S(2)}, u32[]{:S(2)}) collective-permute-start(bf16[384,384]{1,0:T(8,128)(2,1)S(1)} %add_convert_fusion.5), channel_id=1, source_target_pairs={{0,1},{3,2},{4,5},{7,6},{8,9},{11,10},{12,13},{15,14},{16,17},{19,... | collective-permute-start | bytes 884744 | tf_op jit(solution)/shard_map/ppermute | solution.py:488
  68.3 10.7 %collective-permute-start.14 = (bf16[96,1536]{1,0:T(8,128)(2,1)S(1)}, bf16[96,1536]{1,0:T(8,128)(2,1)S(1)}, u32[]{:S(2)}, u32[]{:S(2)}) collective-permute-start(bf16[96,1536]{1,0:T(8,128)(2,1)S(1)} %get-tuple-element.109), channel_id=1, source_target_pairs={{0,4},{4,0},{8,12},{12,8},{1,5},{5,1},{9,13},{13,9},{2,6},{6,2},{1... | collective-permute-start | bytes 884744 | tf_op jit(solution)/shard_map/ppermute | solution.py:434
  68.4 9.8 %collective-permute-start.16 = (bf16[96,1536]{1,0:T(8,128)(2,1)S(1)}, bf16[96,1536]{1,0:T(8,128)(2,1)S(1)}, u32[]{:S(2)}, u32[]{:S(2)}) collective-permute-start(bf16[96,1536]{1,0:T(8,128)(2,1)S(1)} %add_convert_fusion.4), channel_id=1, source_target_pairs={{0,8},{4,12},{8,0},{12,4},{1,9},{5,13},{9,1},{13,5},{2,10},{6,14},... | collective-permute-start | bytes 884744 | tf_op jit(solution)/shard_map/ppermute | solution.py:434
  70.0 18.8 %collective-permute-start.20 = (bf16[112,1536]{1,0:T(8,128)(2,1)S(1)}, bf16[112,1536]{1,0:T(8,128)(2,1)S(1)}, u32[]{:S(2)}, u32[]{:S(2)}) collective-permute-start(bf16[112,1536]{1,0:T(8,128)(2,1)S(1)} %add_convert_fusion), channel_id=1, source_target_pairs={{0,8},{4,12},{8,0},{12,4},{1,9},{5,13},{9,1},{13,5},{2,10},{6,14},... | collective-permute-start | bytes 1032200 | tf_op jit(solution)/shard_map/ppermute | solution.py:434
  79.1 9.7 %collective-permute-start.22 = (bf16[96,1536]{1,0:T(8,128)(2,1)S(1)}, bf16[96,1536]{1,0:T(8,128)(2,1)S(1)}, u32[]{:S(2)}, u32[]{:S(2)}) collective-permute-start(bf16[96,1536]{1,0:T(8,128)(2,1)S(1)} %add_convert_fusion.3), channel_id=1, source_target_pairs={{0,1},{3,2},{4,5},{7,6},{8,9},{11,10},{12,13},{15,14},{16,17},{19,... | collective-permute-start | bytes 884744 | tf_op jit(solution)/shard_map/ppermute | solution.py:488
  83.6 7.4 %collective-permute-start.19 = (bf16[112,1536]{1,0:T(8,128)(2,1)S(1)}, bf16[112,1536]{1,0:T(8,128)(2,1)S(1)}, u32[]{:S(2)}, u32[]{:S(2)}) collective-permute-start(bf16[112,1536]{1,0:T(8,128)(2,1)S(1)} %get-tuple-element.125), channel_id=1, source_target_pairs={{0,4},{4,0},{8,12},{12,8},{1,5},{5,1},{9,13},{13,9},{2,6},{6,2},{1... | collective-permute-start | bytes 1032200 | tf_op jit(solution)/shard_map/ppermute | solution.py:434
  88.9 17.2 %collective-permute-start.24 = (bf16[96,1536]{1,0:T(8,128)(2,1)S(1)}, bf16[96,1536]{1,0:T(8,128)(2,1)S(1)}, u32[]{:S(2)}, u32[]{:S(2)}) collective-permute-start(bf16[96,1536]{1,0:T(8,128)(2,1)S(1)} %add_convert_fusion.1), channel_id=1, source_target_pairs={{1,2},{2,1},{5,6},{6,5},{9,10},{10,9},{13,14},{14,13},{17,18},{18,... | collective-permute-start | bytes 884744 | tf_op jit(solution)/shard_map/ppermute | solution.py:489
  89.7 16.4 %collective-permute-start.23 = (bf16[384,384]{1,0:T(8,128)(2,1)S(1)}, bf16[384,384]{1,0:T(8,128)(2,1)S(1)}, u32[]{:S(2)}, u32[]{:S(2)}) collective-permute-start(bf16[384,384]{1,0:T(8,128)(2,1)S(1)} %reduce-precision_convert_fusion.1), channel_id=1, source_target_pairs={{1,0},{2,3},{5,4},{6,7},{9,8},{10,11},{13,12},{14,15},{17,16},{18,... | collective-permute-start | bytes 884744 | tf_op jit(solution)/shard_map/ppermute | solution.py:490
  91.2 13.4 %collective-permute-start.25 = (bf16[112,384]{1,0:T(8,128)(2,1)S(1)}, bf16[112,384]{1,0:T(8,128)(2,1)S(1)}, u32[]{:S(2)}, u32[]{:S(2)}) collective-permute-start(bf16[112,384]{1,0:T(8,128)(2,1)S(1)} %get-tuple-element.131), channel_id=1, source_target_pairs={{0,1},{1,0},{2,3},{3,2},{4,5},{5,4},{6,7},{7,6},{8,9},{9,8},{10,11... | collective-permute-start | bytes 258056 | tf_op jit(solution)/shard_map/ppermute | solution.py:434
  95.4 10.7 %collective-permute-start.26 = (bf16[112,384]{1,0:T(8,128)(2,1)S(1)}, bf16[112,384]{1,0:T(8,128)(2,1)S(1)}, u32[]{:S(2)}, u32[]{:S(2)}) collective-permute-start(bf16[112,384]{1,0:T(8,128)(2,1)S(1)} %get-tuple-element.132), channel_id=1, source_target_pairs={{0,2},{1,3},{2,0},{3,1},{4,6},{5,7},{6,4},{7,5},{8,10},{9,11},{10,... | collective-permute-start | bytes 258056 | tf_op jit(solution)/shard_map/ppermute | solution.py:434
  96.5 9.6 %collective-permute-start.27 = (bf16[112,384]{1,0:T(8,128)(2,1)S(1)}, bf16[112,384]{1,0:T(8,128)(2,1)S(1)}, u32[]{:S(2)}, u32[]{:S(2)}) collective-permute-start(bf16[112,384]{1,0:T(8,128)(2,1)S(1)} %get-tuple-element.133), channel_id=1, source_target_pairs={{0,3},{1,2},{2,1},{3,0},{4,7},{5,6},{6,5},{7,4},{8,11},{9,10},{10,... | collective-permute-start | bytes 258056 | tf_op jit(solution)/shard_map/ppermute | solution.py:434
  106.2 6.7 %collective-permute-start.28 = (bf16[112,384]{1,0:T(8,128)(2,1)S(1)}, bf16[112,384]{1,0:T(8,128)(2,1)S(1)}, u32[]{:S(2)}, u32[]{:S(2)}) collective-permute-start(bf16[112,384]{1,0:T(8,128)(2,1)S(1)} %reduce-precision_convert_fusion.2), channel_id=1, source_target_pairs={{0,1},{1,0},{2,3},{3,2},{4,5},{5,4},{6,7},{7,6},{8,9},{9,8},{10,11... | collective-permute-start | bytes 258056 | tf_op jit(solution)/shard_map/ppermute | solution.py:434
  108.9 6.4 %collective-permute-start.30 = (bf16[112,384]{1,0:T(8,128)(2,1)S(1)}, bf16[112,384]{1,0:T(8,128)(2,1)S(1)}, u32[]{:S(2)}, u32[]{:S(2)}) collective-permute-start(bf16[112,384]{1,0:T(8,128)(2,1)S(1)} %reduce-precision_convert_fusion.2), channel_id=1, source_target_pairs={{0,3},{1,2},{2,1},{3,0},{4,7},{5,6},{6,5},{7,4},{8,11},{9,10},{10,... | collective-permute-start | bytes 258056 | tf_op jit(solution)/shard_map/ppermute | solution.py:434
  110.7 9.1 %collective-permute-start.31 = (bf16[96,1536]{1,0:T(8,128)(2,1)S(1)}, bf16[96,1536]{1,0:T(8,128)(2,1)S(1)}, u32[]{:S(2)}, u32[]{:S(2)}) collective-permute-start(bf16[96,1536]{1,0:T(8,128)(2,1)S(1)} %reduce-precision_convert_fusion), channel_id=1, source_target_pairs={{1,0},{2,3},{5,4},{6,7},{9,8},{10,11},{13,12},{14,15},{17,16},{18,... | collective-permute-start | bytes 884744 | tf_op jit(solution)/shard_map/ppermute | solution.py:490
  (12 other events, 73.3 us)

commit v3 on v2

--- a/solution.py
+++ b/solution.py
@@ -35,14 +35,19 @@
     return lax.dot_general(a, b, (((0,), (0,)), ((), ())), preferred_element_type=F32)
 
 
-def fetch(pieces, dest, sems, first, me, rows=None, column=0):
+def fetch(pieces, dest, sems, first, me, rows=None, column=0, half=0):
     copies = []
     for k, piece in enumerate(pieces):
         if rows is not None:
             piece = piece.at[pl.ds(0, rows), pl.ds(column, dest.shape[1])]
-        count = piece.shape[0]
+        blocks = piece if isinstance(piece, tuple) else (piece,)
+        count, wide = blocks[0].shape
         start = pl.multiple_of(jnp.bitwise_xor(me, k) * count, count)
-        copies.append(pltpu.make_async_copy(piece, dest.at[pl.ds(start, count)], sems.at[first + k]))
+        for n, one in enumerate(blocks):
+            target = dest.at[pl.ds(start, count)]
+            if len(blocks) > 1:
+                target = dest.at[pl.ds(start, count), pl.ds(pl.multiple_of(jnp.bitwise_xor(half, n) * wide, wide), wide)]
+            copies.append(pltpu.make_async_copy(one, target, sems.at[first + len(copies)]))
     for copy in copies:
         copy.start()
     return copies
@@ -195,30 +200,37 @@
     ]
 
 
-def pack_kernel(heads_ref, merge_ref, *refs):
-    many = (len(refs) - 3) // 2
-    vectors, (out_ref, rows, *held), sems = refs[:many], refs[many : 2 * many + 2], refs[-1]
+def pack_kernel(info, heads_ref, merge_ref, up_ref, *refs):
+    many = (len(refs) - 4) // 2
+    vectors, (out_ref, half_ref, rows, *held), sems = refs[:many], refs[many : 2 * many + 3], refs[-1]
     part, wide = heads_ref.shape
+    half = half_ref.shape[1]
+    columns = pl.ds(pl.multiple_of(info[0] * half, half), half)
     copies = [
         pltpu.make_async_copy(heads_ref, out_ref.at[pl.ds(0, part), pl.ds(0, wide)], sems.at[0]),
         pltpu.make_async_copy(merge_ref, out_ref.at[pl.ds(0, part), pl.ds(wide, merge_ref.shape[1])], sems.at[1]),
+        pltpu.make_async_copy(up_ref.at[:, columns], half_ref, sems.at[2]),
     ]
-    copies += [pltpu.make_async_copy(v, held[n], sems.at[2 + n]) for n, v in enumerate(vectors)]
+    copies += [pltpu.make_async_copy(v, held[n], sems.at[3 + n]) for n, v in enumerate(vectors)]
     for copy in copies:
         copy.start()
     rows[...] = jnp.zeros_like(rows)
-    arrive(copies[2:])
+    arrive(copies[3:])
     for n, vector in enumerate(held):
         rows[n : n + 1, : vector.shape[1]] = vector[...].astype(F32)
     out_ref[part:, :] = rows[...].astype(BF)
-    arrive(copies[:2])
-
-
-def attend_kernel(shards, info, images, *refs):
+    arrive(copies[:3])
+
+
+def pick_kernel(info, images, rows_ref, unit_ref):
+    unit_ref[...], _ = norm_parts(pad_images(picked_images(info, images), rows_ref))
+
+
+def attend_kernel(shards, count, length, info, rows_ref, unit_ref, *refs):
     pieces = refs[:shards]
-    middle_ref, mid_ref, heads, merge, small, up_bias, rows_ref, packed, mixed, vectors, sems = refs[shards:]
+    middle_ref, mid_ref, heads, merge, small, up_bias, packed, mixed, vectors, sems = refs[shards:]
     me = info[0]
-    count, length, width = images.shape
+    width = rows_ref.shape[1]
     part = width // shards
     first = fetch(pieces, heads, sems, 0, me, part)
     second = fetch(pieces, merge, sems, shards, me, part, heads.shape[1])
@@ -227,27 +239,27 @@
         source = piece.at[pl.ds(part, 16)]
         third.append(pltpu.make_async_copy(source, vectors.at[jnp.bitwise_xor(me, k)], sems.at[2 * shards + k]))
         third[-1].start()
-    rows = pad_images(picked_images(info, images), rows_ref)
-    unit, _ = norm_parts(rows)
     arrive(third)
     hidden_part = up_bias.shape[1] // shards
     for at in range(shards):
         given = vectors[at].astype(F32)
         small[:, at * part : (at + 1) * part] = given[:8, :part]
         up_bias[:, at * hidden_part : (at + 1) * hidden_part] = given[8:9, :hidden_part]
-    entry = (unit * small[PRE_GAIN : PRE_GAIN + 1] + small[PRE_SHIFT : PRE_SHIFT + 1]).astype(BF)
+    entry = (unit_ref[...] * small[PRE_GAIN : PRE_GAIN + 1] + small[PRE_SHIFT : PRE_SHIFT + 1]).astype(BF)
     arrive(first)
     packed[...] = (dot(entry, heads[...]) + packed_bias(small)).astype(BF)
     attention_forward(packed, mixed, count, length, width)
     arrive(second)
-    middle = rows + dot(mixed[...], merge[...]) + small[MERGE_BIAS : MERGE_BIAS + 1]
+    middle = rows_ref[...] + dot(mixed[...], merge[...]) + small[MERGE_BIAS : MERGE_BIAS + 1]
     middle_ref[...] = middle
     mid_ref[...] = mid_rows(middle, small)[0]
 
 
 def widen_kernel(shards, info, mid_ref, up_bias, *refs):
-    act_ref, up, sems = refs[shards:]
-    arrive(fetch(refs[:shards], up, sems, 0, info[0]))
+    act_ref, up, sems = refs[shards * 3 // 2 :]
+    near, far = refs[: shards // 2], refs[shards // 2 : shards * 3 // 2]
+    pieces = (*near, *zip(far[::2], far[1::2]))
+    arrive(fetch(pieces, up, sems, 0, info[0], half=info[4]))
     hidden = dot(mid_ref[...], up[...]) + up_bias[...]
     act_ref[...] = gelu_parts(hidden)[0].astype(BF)
 
@@ -261,7 +273,7 @@
 
 def both_ways_kernel(
     info,
-    images,
+    first_rows,
     arrived,
     cotangent,
     small,
@@ -288,9 +300,8 @@
     grad_packed,
 ):
     leading = info[1] == 0
-    count, length, width = images.shape
-    source = [jnp.where(leading, image, arrived[n]) for n, image in enumerate(picked_images(info, images))]
-    rows = pad_images(source, rows_ref)
+    count, length, width = arrived.shape
+    rows = jnp.where(leading, first_rows[...], pad_images([arrived[n] for n in range(count)], rows_ref))
     entry_ref[...], unit_one_ref[...], inverse_one_ref[...] = entry_rows(rows, small)
     packed[...] = (dot(entry_ref[...], heads[...]) + packed_bias(small)).astype(BF)
     probs_ref[...] = attention_forward(packed, mixed, count, length, width)
@@ -324,15 +335,6 @@
     )
 
 
-def down_grad_kernel(shards, info, returned, cotangent, act_ref, *refs):
-    outs, grad_ref = refs[:shards], refs[shards]
-    incoming = own_gradient(info, returned, cotangent, grad_ref).astype(BF)
-    rows = outs[0].shape[0]
-    for k in range(shards):
-        start = pl.multiple_of(jnp.bitwise_xor(info[0], k) * rows, rows)
-        outs[k][...] = dot_tn(act_ref[:, pl.ds(start, rows)], incoming).astype(BF)
-
-
 def rest_grad_kernel(
     shards,
     info,
@@ -346,6 +348,7 @@
     packed,
     probs_ref,
     mixed,
+    act_ref,
     slope_ref,
     entry_ref,
     unit_one_ref,
@@ -355,15 +358,20 @@
     inverse_two_ref,
     *refs,
 ):
-    up_outs, rest_outs = refs[:shards], refs[shards : 2 * shards]
-    grad_in_ref, grad_ref, grad_packed, whole_up, whole_heads, whole_merge, extra = refs[2 * shards :]
+    down_outs, up_outs, rest_outs = (refs[n * shards : (n + 1) * shards] for n in range(3))
+    grad_in_ref, grad_ref, grad_packed, whole_up, whole_heads, whole_merge, extra = refs[3 * shards :]
     me, leading = info[0], info[1] == 0
     count, length, width = cotangent.shape
     part = width // shards
     incoming = own_gradient(info, returned, cotangent, grad_ref)
     extra[...] = jnp.zeros_like(extra)
     extra[DOWN_BIAS : DOWN_BIAS + 1, :] = column_sum(incoming)
-    grad_hidden = (dot_nt(incoming.astype(BF), down[...]) * slope_ref[...]).astype(BF)
+    grad_out = incoming.astype(BF)
+    high = act_ref.shape[1] // shards
+    for k in range(shards):
+        columns = pl.ds(pl.multiple_of(jnp.bitwise_xor(me, k) * high, high), high)
+        down_outs[k][:high, :] = dot_tn(act_ref[:, columns], grad_out).astype(BF)
+    grad_hidden = (dot_nt(grad_out, down[...]) * slope_ref[...]).astype(BF)
     whole_up[...] = dot_tn(mid_ref[...], grad_hidden).astype(BF)
     wide_sum = column_sum(grad_hidden.astype(F32))
     for n in range(wide_sum.shape[1] // width):
@@ -395,10 +403,9 @@
     for k in range(shards):
         rows = pl.ds(pl.multiple_of(jnp.bitwise_xor(me, k) * part, part), part)
         up_outs[k][...] = whole_up[rows, :]
-        rest_outs[k][:part, :wide] = whole_heads[rows, :]
-        rest_outs[k][:part, wide:] = whole_merge[rows, :]
-        rest_outs[k][part:, :wide] = jnp.zeros((16, wide), BF)
-        rest_outs[k][part:, wide:] = extra[...].astype(BF)
+        rest_outs[k][:, :wide] = whole_heads[rows, :]
+        rest_outs[k][:, wide:] = whole_merge[rows, :]
+        down_outs[k][high:, :] = extra[...].astype(BF)
 
 
 def column_blocks_kernel(at, *refs):
@@ -438,6 +445,12 @@
     return [1 << n for n in range(size.bit_length() - 1)]
 
 
+def gather_nearer(pieces, axis):
+    for bit in bits_of(lax.axis_size(axis))[:-1]:
+        pieces = pieces + [swapped(piece, axis, bit) for piece in pieces]
+    return pieces
+
+
 def gather_pieces(shard, axis, *earlier):
     pieces = {0: shard}
     for bit in reversed(bits_of(lax.axis_size(axis))):
@@ -449,16 +462,13 @@
     return sum(term.astype(F32) for term in terms).astype(BF)
 
 
-def scatter_steps(pieces, axis):
-    pieces = dict(enumerate(pieces))
+def nearer_sums(pieces, axis):
+    terms = {k: (piece,) for k, piece in enumerate(pieces)}
     *nearer, last = bits_of(lax.axis_size(axis))
     for bit in nearer:
-        for k in sorted((k for k in pieces if not k & bit), reverse=True):
-            received = swapped(pieces.pop(k ^ bit), axis, bit)
-            pieces[k] = added(pieces[k], received) if k & last else (pieces[k], received)
-    yield pieces[last]
-    kept = pieces[0] if isinstance(pieces[0], tuple) else (pieces[0],)
-    yield (*kept, swapped(pieces[last], axis, last))
+        for k in sorted((k for k in terms if not k & bit), reverse=True):
+            terms[k] += (swapped(added(*terms.pop(k ^ bit)), axis, bit),)
+    return added(*terms[last]), terms[0]
 
 
 def together(*values):
@@ -482,45 +492,47 @@
     return call(column_blocks_kernel, "column_blocks", at.reshape(1), terms, (), shapes, [], 1)
 
 
-def totals_over_line(down_sum, up_steps, rest_steps, axis):
+def totals_over_line(leaving, kept, axes):
+    scattered, axis = axes
     at = lax.axis_index(axis).astype(jnp.int32)
     size = lax.axis_size(axis)
-    inwards = lambda block: lax.ppermute(block, axis, [(0, 1), (3, 2)])
-    across = lambda block: lax.ppermute(block, axis, [(1, 2), (2, 1)])
-    outwards = lambda block: lax.ppermute(block, axis, [(1, 0), (2, 3)])
-    finished = lambda kept, received: jnp.where((at == 0) | (at == 3), received, kept).astype(F32)
+    odd = (at & 1) != 0
+    far = lambda block: swapped(block, scattered, lax.axis_size(scattered) // 2)
     others = lambda blocks: [swapped(blocks[k], axis, k) for k in range(1, size)]
-
-    rest_first = next(rest_steps)
-    *up_terms, up_last = next(up_steps)
-    up_last, down_in, rest_first = together(up_last, inwards(down_sum), rest_first)
-    up_sum, down_half = added(*up_terms, up_last), added(down_sum, down_in)
-
-    *rest_terms, rest_last = next(rest_steps)
-    rest_last, down_across, up_in = together(rest_last, across(down_half), inwards(up_sum))
-    blocks = column_blocks(at, (*rest_terms, rest_last), size)
-    down_full, up_half = rounded(down_half, down_across), added(up_sum, up_in)
-
-    down_out, up_across, *received = together(outwards(down_full), across(up_half), *others(blocks))
-    own, up_full = rounded(blocks[0], *received), rounded(up_half, up_across)
-
-    full = [own, *others([own] * size)]
+    lower = lambda block: block[: block.shape[0] // 2]
+    upper = lambda block: block[block.shape[0] // 2 :]
+    own_half = lambda block: jnp.where(odd, upper(block), lower(block))
+    whole = lambda own, other: jnp.concatenate([jnp.where(odd, other, own), jnp.where(odd, own, other)]).astype(F32)
+
+    down_far, *leaving = together(far(leaving[0]), *leaving[1:])
+    down = added(*kept[0], down_far)
+
+    up_far, down_near = together(far(leaving[0]), swapped(down, axis, 1))
+    up, down = added(*kept[1], up_far), added(down, down_near)
+
+    rest_far, up_near, down_next = together(far(leaving[1]), swapped(up, axis, 1), swapped(own_half(down), axis, 2))
+    blocks = column_blocks(at, (*kept[2], rest_far), size)
+    pair = added(up, up_near)
+    down = rounded(own_half(down), down_next)
+
+    down_back, up_next, *received = together(swapped(down, axis, 1), swapped(own_half(pair), axis, 2), *others(blocks))
+    own, up_full = rounded(blocks[0], *received), rounded(own_half(pair), up_next)
+
+    up_total = whole(up_full, swapped(up_full, axis, 1))
+    full = [own, *after(tuple(others([own] * size)), up_total)]
     rest_total = [chosen(at, [full[n ^ k] for k in range(size)]).astype(F32) for n in range(size)]
-    return (
-        finished(down_full, down_out),
-        finished(up_full, outwards(up_full)),
-        rest_total,
-        up_sum,
-    )
-
-
-def totals_over(down_sum, up_steps, rest_steps, axis):
+    return whole(down, down_back), up_total, rest_total, up
+
+
+def totals_over(grads, axes):
+    scattered, axis = axes
+    leaving, kept = zip(*(nearer_sums(pieces, scattered) for pieces in grads))
     if lax.axis_size(axis) == 4:
-        return totals_over_line(down_sum, up_steps, rest_steps, axis)
-    next(rest_steps)
-    up_sum, rest_sum = added(*next(up_steps)), added(*next(rest_steps))
-    down, up, rest = (total.astype(F32) for total in lax.psum((down_sum, up_sum, rest_sum), axis))
-    return down, up, jnp.split(rest, 4, axis=1), up_sum
+        return totals_over_line(leaving, kept, axes)
+    last = lax.axis_size(scattered) // 2
+    sums = tuple(added(*terms, swapped(one, scattered, last)) for one, terms in zip(leaving, kept))
+    down, up, rest = (total.astype(F32) for total in lax.psum(sums, axis))
+    return down, up, jnp.split(rest, 4, axis=1), sums[1]
 
 
 def local(
@@ -544,7 +556,8 @@
     me = lax.axis_index("fsdp").astype(jnp.int32)
     section = lax.axis_index("section").astype(jnp.int32)
     shards = lax.axis_size("fsdp")
-    info = jnp.concatenate([jnp.stack([me, section]), slot_image[0]])
+    half = lax.axis_index("dp").astype(jnp.int32) & 1
+    info = jnp.concatenate([jnp.stack([me, section]), slot_image[0], half[None]])
     count, length, width = images.shape
     tall = count * padded_length(length)
     part = width // shards
@@ -562,14 +575,15 @@
     full_up, full_down = shape((width, hidden_width), BF), shape((hidden_width, width), BF)
     rows_wide, rows_bf, column = shape((tall, width), F32), shape((tall, width), BF), shape((tall, 1), F32)
 
-    (mix,) = call(
+    mix, up_half = call(
         pack_kernel,
         "pack",
-        None,
+        half.reshape(1),
         (),
         (
             heads_weight[0],
             merge_weight[0],
+            up_weight[0],
             pre_gain,
             pre_shift,
             query_bias,
@@ -580,25 +594,29 @@
             down_bias,
             up_bias,
         ),
-        (shape((part + 16, wide + width), BF),),
+        (shape((part + 16, wide + width), BF), shape((part, hidden_width // 2), BF)),
         [pltpu.VMEM((16, wide + width), F32)]
         + [pltpu.VMEM((1, part), BF)] * 8
-        + [pltpu.VMEM(up_bias.shape, BF), pltpu.SemaphoreType.DMA((11,))],
+        + [pltpu.VMEM(up_bias.shape, BF), pltpu.SemaphoreType.DMA((12,))],
         1,
         room=56 * 1024 * 1024,
     )
-    up_pieces = gather_pieces(up_weight[0], "fsdp")
-    mix_pieces = gather_pieces(mix, "fsdp", up_pieces[shards // 2])
+    first_rows, first_unit = call(pick_kernel, "pick", info, (images,), (), (rows_wide, rows_wide), [], 1)
+    farthest = shards // 2
+    up_far = swapped(up_half, "fsdp", farthest)
+    mix_pieces = gather_pieces(mix, "fsdp", up_far, first_rows)
+    up_other = swapped(after(up_far, mix_pieces[-1]), "dp", 1)
+    up_near = gather_nearer([up_weight[0]], "fsdp")
+    up_halves = (gather_nearer([one], "fsdp") for one in (up_far, up_other))
 
     middle, mid, heads, merge, small, wide_bias = call(
-        bind(attend_kernel),
+        functools.partial(attend_kernel, shards, count, length),
         "attend",
         info,
-        (images,),
+        (first_rows, first_unit),
         mix_pieces,
         (rows_wide, rows_bf, full_heads, full_merge, shape((8, width), F32), shape((1, hidden_width), F32)),
         [
-            scratch_rows,
             scratch_packed,
             scratch_mixed,
             pltpu.VMEM((shards, 16, wide + width), BF),
@@ -612,9 +630,9 @@
         "widen",
         info,
         (mid, wide_bias),
-        up_pieces,
+        (*up_near, *(one for two in zip(*up_halves) for one in two)),
         (shape((tall, hidden_width), BF), full_up),
-        [sems(1)],
+        [sems(2)],
         work * hidden_width,
         (down_pieces[shards // 2],),
     )
@@ -634,7 +652,7 @@
         both_ways_kernel,
         "both_ways",
         info,
-        (images, arrived, cotangent, small, wide_bias, heads, merge, up, down),
+        (first_rows, arrived, cotangent, small, wide_bias, heads, merge, up, down),
         (),
         (
             shape(images.shape, BF),
@@ -656,26 +674,15 @@
     )
     returned = lax.ppermute(sent, "section", [(1, 0)])
 
-    down_grads = call(
-        bind(down_grad_kernel),
-        "down_grad",
-        info,
-        (returned, cotangent, act),
-        (),
-        (shape((hidden_width // shards, width), BF),) * shards,
-        [scratch_rows],
-        work * hidden_width,
-    )
-    down_chain = scatter_steps(down_grads, "fsdp")
-    down_first = next(down_chain)
     *grads, grad_in = call(
         bind(rest_grad_kernel),
         "rest_grad",
         info,
-        (returned, cotangent, small, heads, merge, up, down, packed, probs, mixed, slope, *kept),
+        (returned, cotangent, small, heads, merge, up, down, packed, probs, mixed, act, slope, *kept),
         (),
-        (shape((part, hidden_width), BF),) * shards
-        + (shape((part + 16, wide + width), BF),) * shards
+        (shape((hidden_width // shards + 16, width), BF),) * shards
+        + (shape((part, hidden_width), BF),) * shards
+        + (shape((part, wide + width), BF),) * shards
         + (shape(images.shape, F32),),
         [
             scratch_rows,
@@ -686,19 +693,16 @@
             pltpu.VMEM((16, width), F32),
         ],
         2 * work * (wide + width + 2 * hidden_width),
-        (down_first,),
-    )
-    down_sum = added(*next(down_chain))
-    up_chain = scatter_steps([after(one, down_sum) for one in grads[:shards]], "fsdp")
-    up_first = next(up_chain)
-    rest_chain = scatter_steps([after(one, down_sum, up_first) for one in grads[shards:]], "fsdp")
-    down_total, up_total, rest_total, up_sum = totals_over(down_sum, up_chain, rest_chain, "dp")
+    )
+    down_total, up_total, rest_total, up_sum = totals_over(
+        [grads[n * shards : (n + 1) * shards] for n in range(3)], ("fsdp", "dp")
+    )
     layer_out, grad_in = after(layer_out, up_sum), after(grad_in, up_sum)
 
-    heads_total = jnp.concatenate([block[:part] for block in rest_total[:3]], axis=1)
-    merge_total = rest_total[3][:part]
-    vector_total = lax.dynamic_slice(rest_total[3], (part, me * part), (8, part))
-    up_bias_total = lax.dynamic_slice(rest_total[3], (part + 8 + me, 0), (1, width))
+    vectors, down_total = down_total[-16:], down_total[:-16]
+    heads_total, merge_total = jnp.concatenate(rest_total[:3], axis=1), rest_total[3]
+    vector_total = lax.dynamic_slice(vectors, (0, me * part), (8, part))
+    up_bias_total = lax.dynamic_slice(vectors, (8 + me, 0), (1, width))
     row = lambda n: vector_total[n : n + 1]
     return (
         layer_out[None],

time: 121 us -> 115 us (0.950)
  waiting for transfers between devices: 54.8 us -> 48.7 us
    ppermute x24 -> x32, starting transfers between devices: 21.4 us -> 33.4 us  [swapped(): lax.ppermute(block, axis, [(i, i ^ bit) for i in range(lax.axis_size(axis...]
    ppermute x6 -> x0, starting transfers between devices: 11.9 us -> none  [the longest x2 7.93 us: totals_over_line(): inwards = lambda block: lax.ppermute(block, axis, [(0, 1), (3, 2)])]
    ppermute x6 -> x0, waiting for transfers between devices: 11.3 us -> none  [the longest x2 9.59 us: totals_over_line(): inwards = lambda block: lax.ppermute(block, axis, [(0, 1), (3, 2)])]
    ppermute x24 -> x32, waiting for transfers between devices: 35.5 us -> 41 us  [swapped(): lax.ppermute(block, axis, [(i, i ^ bit) for i in range(lax.axis_size(axis...]
  transfers between devices with their start and end apart: 32 -> 34, of which waited for: 16 -> 18; matrix products, arithmetic and copies ran while one was open for 6% -> 6% of each run, Pallas kernels for 6% -> 4%
where the time goes in v3:
time: 115 us
  waiting for transfers between devices  48.7 us (42%)
  starting transfers between devices  38.6 us (34%)
  Pallas kernels  17 us (15%)
  other arithmetic  4.81 us (4%)
  local copies, waits for them, and re-layouts  4.6 us (4%)
    ppermute x32, waiting for transfers between devices, swapped(): lax.ppermute(block, axis, [(i, i ^ bit) for i in range(lax.axis_size(axis...  41 us
    ppermute x32, starting transfers between devices, swapped(): lax.ppermute(block, axis, [(i, i ^ bit) for i in range(lax.axis_size(axis...  33.4 us
    pallas_call x8, Pallas kernels, call(): pl.pallas_call(lambda *refs: kernel(*refs[:used], *refs[used + len(earlie...  17 us
    ppermute x1, waiting for transfers between devices, local(): returned = lax.ppermute(sent, 'section', [(1, 0)])  5.16 us
    ppermute x1, starting transfers between devices, local(): arrived = lax.ppermute(first_out, 'section', [(0, 1)])  3.66 us
    unnamed x12, local copies, waits for them, and re-layouts  3.42 us
    ppermute x1, waiting for transfers between devices, local(): arrived = lax.ppermute(first_out, 'section', [(0, 1)])  2.56 us
  transfers between devices with their start and end apart: 34, of which 18 were waited for; matrix products, arithmetic and copies ran while one was open for 6% of the time, Pallas kernels for 4%

profile of v3, /device:TPU:0, one launch (start us, length us, event | category | flops | bytes accessed | tf_op | source)
XLA Modules:
  0.0 114.7 jit_solution(3860593218358827105)
XLA Ops:
  0.7 1.9 %pack.1 = (bf16[112,1536]{1,0:T(8,128)(2,1)}, bf16[96,768]{1,0:T(8,128)(2,1)}) custom-call(s32[1]{0:T(128)} %bitcast.3.refs_0_, bf16[96,1152]{1,0:T(8,128)(2,1)} %bitcast.33, bf16[96,384]{1,0:T(8,128)(2,1)} %bitcast.34, bf16[96,1536]{1,0:T(8,128)(2,1)} %bitcast.25, bf16[1,96]{1,0:T(2,128)(2,1)} %refs_4_.1, bf16[1,96]{1,0:T(2,128)(2,1)} %refs_5_.1, ...), custom_call_target="tpu_custom_call" | custom-call | flops 1 | bytes 1083648 | tf_op jit(solution)/shard_map/pack/pallas_call | solution.py:424
  2.6 3.0 %collective-permute-start.1 = (bf16[112,1536]{1,0:T(8,128)(2,1)}, bf16[112,1536]{1,0:T(8,128)(2,1)S(1)}, u32[]{:S(2)}, u32[]{:S(2)}) collective-permute-start(bf16[112,1536]{1,0:T(8,128)(2,1)} %get-tuple-element.82.refs_3_), channel_id=1, source_target_pairs={{0,8},{4,12},{8,0},{12,4},{1,9},{5,13},{9,1},{13,5},{2,10},{6,14},... | collective-permute-start | bytes 1032200 | tf_op jit(solution)/shard_map/ppermute | solution.py:441
  8.1 9.0 %collective-permute-done.2.refs_5_ = bf16[96,768]{1,0:T(8,128)(2,1)S(1)} collective-permute-done((bf16[96,768]{1,0:T(8,128)(2,1)}, bf16[96,768]{1,0:T(8,128)(2,1)S(1)}, u32[]{:S(2)}, u32[]{:S(2)}) %collective-permute-start.2) | collective-permute-done | bytes 147488 | tf_op jit(solution)/shard_map/ppermute | solution.py:441
  17.6 1.7 %collective-permute-start.8 = (bf16[384,384]{1,0:T(8,128)(2,1)}, bf16[384,384]{1,0:T(8,128)(2,1)S(1)}, u32[]{:S(2)}, u32[]{:S(2)}) collective-permute-start(bf16[384,384]{1,0:T(8,128)(2,1)} %bitcast.28), channel_id=1, source_target_pairs={{0,8},{4,12},{8,0},{12,4},{1,9},{5,13},{9,1},{13,5},{2,10},{6,14},... | collective-permute-start | bytes 884744 | tf_op jit(solution)/shard_map/ppermute | solution.py:441
  19.8 1.6 %collective-permute-start.5 = (bf16[96,768]{1,0:T(8,128)(2,1)S(1)}, bf16[96,768]{1,0:T(8,128)(2,1)S(1)}, u32[]{:S(2)}, u32[]{:S(2)}) collective-permute-start(bf16[96,768]{1,0:T(8,128)(2,1)S(1)} %collective-permute-done.2.refs_5_), channel_id=1, source_target_pairs={{0,1},{1,0},{2,3},{3,2},{4,5},{5,4},{6,7},{7,6},{8,9},{9,8},{10,11... | collective-permute-start | bytes 442376 | tf_op jit(solution)/shard_map/ppermute | solution.py:441
  22.4 2.5 %attend.1 = (f32[160,384]{1,0:T(8,128)S(1)}, bf16[160,384]{1,0:T(8,128)(2,1)S(1)}, bf16[384,1152]{1,0:T(8,128)(2,1)S(1)}, bf16[384,384]{1,0:T(8,128)(2,1)S(1)}, ...) custom-call(s32[5]{0:T(128)S(1)} %pad_add_fusion.refs_0_, f32[160,384]{1,0:T(8,128)S(1)} %get-tuple-element.80.refs_1_, ...), custom_call_target="tpu_custom_call" | custom-call | flops 188743680 | bytes 3434496 | tf_op jit(solution)/shard_map/attend/pallas_call | solution.py:424
  24.9 1.8 %collective-permute-done.8.refs_9_.refs_6_ = bf16[384,384]{1,0:T(8,128)(2,1)S(1)} collective-permute-done((bf16[384,384]{1,0:T(8,128)(2,1)}, bf16[384,384]{1,0:T(8,128)(2,1)S(1)}, u32[]{:S(2)}, u32[]{:S(2)}) %collective-permute-start.8) | collective-permute-done | bytes 294944 | tf_op jit(solution)/shard_map/ppermute | solution.py:441
  31.3 3.7 %collective-permute-start.11 = (bf16[2,65,384]{2,1,0:T(8,128)(2,1)S(1)}, bf16[2,65,384]{2,1,0:T(8,128)(2,1)S(1)}, u32[]{:S(2)}, u32[]{:S(2)}) collective-permute-start(bf16[2,65,384]{2,1,0:T(8,128)(2,1)S(1)} %get-tuple-element.92), channel_id=1, source_target_pairs={{0,16},{1,17},{2,18},{3,19},{4,20},{5,21},{6,22},{7,23},{8,24},{9,... | collective-permute-start | bytes 299528 | tf_op jit(solution)/shard_map/ppermute | solution.py:649
  35.0 2.6 %collective-permute-done.11.refs_2_ = bf16[2,65,384]{2,1,0:T(8,128)(2,1)S(1)} collective-permute-done((bf16[2,65,384]{2,1,0:T(8,128)(2,1)S(1)}, bf16[2,65,384]{2,1,0:T(8,128)(2,1)S(1)}, u32[]{:S(2)}, u32[]{:S(2)}) %collective-permute-start.11) | collective-permute-done | bytes 99872 | tf_op jit(solution)/shard_map/ppermute | solution.py:649
  37.6 5.1 %both_ways.1 = (bf16[2,65,384]{2,1,0:T(8,128)(2,1)S(1)}, bf16[2,65,384]{2,1,0:T(8,128)(2,1)S(1)}, bf16[160,1152]{1,0:T(8,128)(2,1)S(1)}, f32[960,80]{1,0:T(8,128...) custom-call(s32[5]{0:T(128)S(1)} %pad_add_fusion.refs_0_, ...), custom_call_target="tpu_custom_call" | custom-call | flops 1132462080 | bytes 7214336 | tf_op jit(solution)/shard_map/both_ways/pallas_call | solution.py:424
  44.1 5.2 %collective-permute-done.12.refs_1_ = bf16[2,65,384]{2,1,0:T(8,128)(2,1)S(1)} collective-permute-done((bf16[2,65,384]{2,1,0:T(8,128)(2,1)S(1)}, bf16[2,65,384]{2,1,0:T(8,128)(2,1)S(1)}, u32[]{:S(2)}, u32[]{:S(2)}) %collective-permute-start.12) | collective-permute-done | bytes 99872 | tf_op jit(solution)/shard_map/ppermute | solution.py:675
  49.3 4.1 %rest_grad.1 = (bf16[400,384]{1,0:T(8,128)(2,1)S(1)}, bf16[400,384]{1,0:T(8,128)(2,1)S(1)}, bf16[400,384]{1,0:T(8,128)(2,1)S(1)}, bf16[400,384]{1,0:T(8,128)(2,1...) custom-call(s32[5]{0:T(128)S(1)} %pad_add_fusion.refs_0_, ...), custom_call_target="tpu_custom_call" | custom-call | flops 1132462080 | bytes 10550528 | tf_op jit(solution)/shard_map/rest_grad/pallas_call | solution.py:424
  57.2 7.7 %collective-permute-done.15 = bf16[400,384]{1,0:T(8,128)(2,1)S(1)} collective-permute-done((bf16[400,384]{1,0:T(8,128)(2,1)S(1)}, bf16[400,384]{1,0:T(8,128)(2,1)S(1)}, u32[]{:S(2)}, u32[]{:S(2)}) %collective-permute-start.15) | collective-permute-done | bytes 307232 | tf_op jit(solution)/shard_map/ppermute | solution.py:441
  65.1 1.6 %collective-permute-start.20 = (bf16[400,384]{1,0:T(8,128)(2,1)S(1)}, bf16[400,384]{1,0:T(8,128)(2,1)S(1)}, u32[]{:S(2)}, u32[]{:S(2)}) collective-permute-start(bf16[400,384]{1,0:T(8,128)(2,1)S(1)} %add_convert_fusion.1), channel_id=1, source_target_pairs={{0,1},{1,0},{2,3},{3,2},{4,5},{5,4},{6,7},{7,6},{8,9},{9,8},{10,11... | collective-permute-start | bytes 921608 | tf_op jit(solution)/shard_map/ppermute | solution.py:441
  68.8 7.9 %collective-permute-done.18 = bf16[96,1536]{1,0:T(8,128)(2,1)S(1)} collective-permute-done((bf16[96,1536]{1,0:T(8,128)(2,1)S(1)}, bf16[96,1536]{1,0:T(8,128)(2,1)S(1)}, u32[]{:S(2)}, u32[]{:S(2)}) %collective-permute-start.18) | collective-permute-done | bytes 294944 | tf_op jit(solution)/shard_map/ppermute | solution.py:441
  77.4 2.7 %collective-permute-start.23 = (bf16[200,384]{1,0:T(8,128)(2,1)S(1)}, bf16[200,384]{1,0:T(8,128)(2,1)S(1)}, u32[]{:S(2)}, u32[]{:S(2)}) collective-permute-start(bf16[200,384]{1,0:T(8,128)(2,1)S(1)} %slice_select_fusion), channel_id=1, source_target_pairs={{0,2},{1,3},{2,0},{3,1},{4,6},{5,7},{6,4},{7,5},{8,10},{9,11},{10,... | collective-permute-start | bytes 460808 | tf_op jit(solution)/shard_map/ppermute | solution.py:441
  81.0 3.2 %collective-permute-done.23 = bf16[200,384]{1,0:T(8,128)(2,1)S(1)} collective-permute-done((bf16[200,384]{1,0:T(8,128)(2,1)S(1)}, bf16[200,384]{1,0:T(8,128)(2,1)S(1)}, u32[]{:S(2)}, u32[]{:S(2)}) %collective-permute-start.23) | collective-permute-done | bytes 153632 | tf_op jit(solution)/shard_map/ppermute | solution.py:441
  84.2 2.1 %collective-permute-done.22 = bf16[96,1536]{1,0:T(8,128)(2,1)S(1)} collective-permute-done((bf16[96,1536]{1,0:T(8,128)(2,1)S(1)}, bf16[96,1536]{1,0:T(8,128)(2,1)S(1)}, u32[]{:S(2)}, u32[]{:S(2)}) %collective-permute-start.22) | collective-permute-done | bytes 294944 | tf_op jit(solution)/shard_map/ppermute | solution.py:441
  86.3 4.3 %collective-permute-start.24 = (bf16[200,384]{1,0:T(8,128)(2,1)S(1)}, bf16[200,384]{1,0:T(8,128)(2,1)S(1)}, u32[]{:S(2)}, u32[]{:S(2)}) collective-permute-start(bf16[200,384]{1,0:T(8,128)(2,1)S(1)} %reduce-precision_convert_fusion), channel_id=1, source_target_pairs={{0,1},{1,0},{2,3},{3,2},{4,5},{5,4},{6,7},{7,6},{8,9},{9,8},{10,11... | collective-permute-start | bytes 460808 | tf_op jit(solution)/shard_map/ppermute | solution.py:441
  90.7 1.6 %collective-permute-start.25 = (bf16[48,1536]{1,0:T(8,128)(2,1)S(1)}, bf16[48,1536]{1,0:T(8,128)(2,1)S(1)}, u32[]{:S(2)}, u32[]{:S(2)}) collective-permute-start(bf16[48,1536]{1,0:T(8,128)(2,1)S(1)} %slice_select_fusion.1), channel_id=1, source_target_pairs={{0,2},{1,3},{2,0},{3,1},{4,6},{5,7},{6,4},{7,5},{8,10},{9,11},{10,... | collective-permute-start | bytes 442376 | tf_op jit(solution)/shard_map/ppermute | solution.py:441
  94.0 2.9 %collective-permute-start.29 = (bf16[96,384]{1,0:T(8,128)(2,1)S(1)}, bf16[96,384]{1,0:T(8,128)(2,1)S(1)}, u32[]{:S(2)}, u32[]{:S(2)}) collective-permute-start(bf16[96,384]{1,0:T(8,128)(2,1)S(1)} %get-tuple-element.135), channel_id=1, source_target_pairs={{0,3},{1,2},{2,1},{3,0},{4,7},{5,6},{6,5},{7,4},{8,11},{9,10},{10,... | collective-permute-start | bytes 221192 | tf_op jit(solution)/shard_map/ppermute | solution.py:441
  99.4 2.9 %collective-permute-done.28 = bf16[96,384]{1,0:T(8,128)(2,1)S(1)} collective-permute-done((bf16[96,384]{1,0:T(8,128)(2,1)S(1)}, bf16[96,384]{1,0:T(8,128)(2,1)S(1)}, u32[]{:S(2)}, u32[]{:S(2)}) %collective-permute-start.28) | collective-permute-done | bytes 73760 | tf_op jit(solution)/shard_map/ppermute | solution.py:441
  102.4 2.1 %collective-permute-start.30 = (bf16[96,384]{1,0:T(8,128)(2,1)S(1)}, bf16[96,384]{1,0:T(8,128)(2,1)S(1)}, u32[]{:S(2)}, u32[]{:S(2)}) collective-permute-start(bf16[96,384]{1,0:T(8,128)(2,1)S(1)} %reduce-precision_convert_fusion.2), channel_id=1, source_target_pairs={{0,1},{1,0},{2,3},{3,2},{4,5},{5,4},{6,7},{7,6},{8,9},{9,8},{10,11... | collective-permute-start | bytes 221192 | tf_op jit(solution)/shard_map/ppermute | solution.py:441
  105.2 1.8 %collective-permute-start.32 = (bf16[96,384]{1,0:T(8,128)(2,1)S(1)}, bf16[96,384]{1,0:T(8,128)(2,1)S(1)}, u32[]{:S(2)}, u32[]{:S(2)}) collective-permute-start(bf16[96,384]{1,0:T(8,128)(2,1)S(1)} %reduce-precision_convert_fusion.2), channel_id=1, source_target_pairs={{0,3},{1,2},{2,1},{3,0},{4,7},{5,6},{6,5},{7,4},{8,11},{9,10},{10,... | collective-permute-start | bytes 221192 | tf_op jit(solution)/shard_map/ppermute | solution.py:441
  (87 shorter events, 30.8 us)
Async XLA Ops:
  2.6 14.4 %collective-permute-start.1 = (bf16[112,1536]{1,0:T(8,128)(2,1)}, bf16[112,1536]{1,0:T(8,128)(2,1)S(1)}, u32[]{:S(2)}, u32[]{:S(2)}) collective-permute-start(bf16[112,1536]{1,0:T(8,128)(2,1)} %get-tuple-element.82.refs_3_), channel_id=1, source_target_pairs={{0,8},{4,12},{8,0},{12,4},{1,9},{5,13},{9,1},{13,5},{2,10},{6,14},... | collective-permute-start | bytes 1032200 | tf_op jit(solution)/shard_map/ppermute | solution.py:441
  5.6 11.4 %collective-permute-start.2 = (bf16[96,768]{1,0:T(8,128)(2,1)}, bf16[96,768]{1,0:T(8,128)(2,1)S(1)}, u32[]{:S(2)}, u32[]{:S(2)}) collective-permute-start(bf16[96,768]{1,0:T(8,128)(2,1)} %get-tuple-element.83), channel_id=1, source_target_pairs={{0,8},{4,12},{8,0},{12,4},{1,9},{5,13},{9,1},{13,5},{2,10},{6,14},... | collective-permute-start | bytes 442376 | tf_op jit(solution)/shard_map/ppermute | solution.py:441
  17.6 9.1 %collective-permute-start.8 = (bf16[384,384]{1,0:T(8,128)(2,1)}, bf16[384,384]{1,0:T(8,128)(2,1)S(1)}, u32[]{:S(2)}, u32[]{:S(2)}) collective-permute-start(bf16[384,384]{1,0:T(8,128)(2,1)} %bitcast.28), channel_id=1, source_target_pairs={{0,8},{4,12},{8,0},{12,4},{1,9},{5,13},{9,1},{13,5},{2,10},{6,14},... | collective-permute-start | bytes 884744 | tf_op jit(solution)/shard_map/ppermute | solution.py:441
  19.3 7.9 %collective-permute-start.4 = (bf16[96,1536]{1,0:T(8,128)(2,1)}, bf16[96,1536]{1,0:T(8,128)(2,1)S(1)}, u32[]{:S(2)}, u32[]{:S(2)}) collective-permute-start(bf16[96,1536]{1,0:T(8,128)(2,1)} %bitcast.26), channel_id=1, source_target_pairs={{0,4},{4,0},{8,12},{12,8},{1,5},{5,1},{9,13},{13,9},{2,6},{6,2},{1... | collective-permute-start | bytes 884744 | tf_op jit(solution)/shard_map/ppermute | solution.py:441
  19.3 10.7 %collective-permute-start.9 = (bf16[384,384]{1,0:T(8,128)(2,1)}, bf16[384,384]{1,0:T(8,128)(2,1)S(1)}, u32[]{:S(2)}, u32[]{:S(2)}) collective-permute-start(bf16[384,384]{1,0:T(8,128)(2,1)} %bitcast.29), channel_id=1, source_target_pairs={{0,4},{4,0},{8,12},{12,8},{1,5},{5,1},{9,13},{13,9},{2,6},{6,2},{1... | collective-permute-start | bytes 884744 | tf_op jit(solution)/shard_map/ppermute | solution.py:441
  19.8 7.4 %collective-permute-start.5 = (bf16[96,768]{1,0:T(8,128)(2,1)S(1)}, bf16[96,768]{1,0:T(8,128)(2,1)S(1)}, u32[]{:S(2)}, u32[]{:S(2)}) collective-permute-start(bf16[96,768]{1,0:T(8,128)(2,1)S(1)} %collective-permute-done.2.refs_5_), channel_id=1, source_target_pairs={{0,1},{1,0},{2,3},{3,2},{4,5},{5,4},{6,7},{7,6},{8,9},{9,8},{10,11... | collective-permute-start | bytes 442376 | tf_op jit(solution)/shard_map/ppermute | solution.py:441
  31.3 6.3 %collective-permute-start.11 = (bf16[2,65,384]{2,1,0:T(8,128)(2,1)S(1)}, bf16[2,65,384]{2,1,0:T(8,128)(2,1)S(1)}, u32[]{:S(2)}, u32[]{:S(2)}) collective-permute-start(bf16[2,65,384]{2,1,0:T(8,128)(2,1)S(1)} %get-tuple-element.92), channel_id=1, source_target_pairs={{0,16},{1,17},{2,18},{3,19},{4,20},{5,21},{6,22},{7,23},{8,24},{9,... | collective-permute-start | bytes 299528 | tf_op jit(solution)/shard_map/ppermute | solution.py:649
  42.6 6.6 %collective-permute-start.12 = (bf16[2,65,384]{2,1,0:T(8,128)(2,1)S(1)}, bf16[2,65,384]{2,1,0:T(8,128)(2,1)S(1)}, u32[]{:S(2)}, u32[]{:S(2)}) collective-permute-start(bf16[2,65,384]{2,1,0:T(8,128)(2,1)S(1)} %get-tuple-element.98), channel_id=1, source_target_pairs={{16,0},{17,1},{18,2},{19,3},{20,4},{21,5},{22,6},{23,7},{24,8},{25... | collective-permute-start | bytes 299528 | tf_op jit(solution)/shard_map/ppermute | solution.py:675
  54.1 10.9 %collective-permute-start.19 = (bf16[400,384]{1,0:T(8,128)(2,1)S(1)}, bf16[400,384]{1,0:T(8,128)(2,1)S(1)}, u32[]{:S(2)}, u32[]{:S(2)}) collective-permute-start(bf16[400,384]{1,0:T(8,128)(2,1)S(1)} %get-tuple-element.120), channel_id=1, source_target_pairs={{0,4},{4,0},{8,12},{12,8},{1,5},{5,1},{9,13},{13,9},{2,6},{6,2},{1... | collective-permute-start | bytes 921608 | tf_op jit(solution)/shard_map/ppermute | solution.py:441
  55.6 9.4 %collective-permute-start.15 = (bf16[400,384]{1,0:T(8,128)(2,1)S(1)}, bf16[400,384]{1,0:T(8,128)(2,1)S(1)}, u32[]{:S(2)}, u32[]{:S(2)}) collective-permute-start(bf16[400,384]{1,0:T(8,128)(2,1)S(1)} %add_convert_fusion.2), channel_id=1, source_target_pairs={{0,8},{4,12},{8,0},{12,4},{1,9},{5,13},{9,1},{13,5},{2,10},{6,14},... | collective-permute-start | bytes 921608 | tf_op jit(solution)/shard_map/ppermute | solution.py:441
  65.1 11.6 %collective-permute-start.20 = (bf16[400,384]{1,0:T(8,128)(2,1)S(1)}, bf16[400,384]{1,0:T(8,128)(2,1)S(1)}, u32[]{:S(2)}, u32[]{:S(2)}) collective-permute-start(bf16[400,384]{1,0:T(8,128)(2,1)S(1)} %add_convert_fusion.1), channel_id=1, source_target_pairs={{0,1},{1,0},{2,3},{3,2},{4,5},{5,4},{6,7},{7,6},{8,9},{9,8},{10,11... | collective-permute-start | bytes 921608 | tf_op jit(solution)/shard_map/ppermute | solution.py:441
  66.7 9.9 %collective-permute-start.18 = (bf16[96,1536]{1,0:T(8,128)(2,1)S(1)}, bf16[96,1536]{1,0:T(8,128)(2,1)S(1)}, u32[]{:S(2)}, u32[]{:S(2)}) collective-permute-start(bf16[96,1536]{1,0:T(8,128)(2,1)S(1)} %add_convert_fusion.6), channel_id=1, source_target_pairs={{0,8},{4,12},{8,0},{12,4},{1,9},{5,13},{9,1},{13,5},{2,10},{6,14},... | collective-permute-start | bytes 884744 | tf_op jit(solution)/shard_map/ppermute | solution.py:441
  68.2 8.5 %collective-permute-start.13 = (bf16[96,1536]{1,0:T(8,128)(2,1)S(1)}, bf16[96,1536]{1,0:T(8,128)(2,1)S(1)}, u32[]{:S(2)}, u32[]{:S(2)}) collective-permute-start(bf16[96,1536]{1,0:T(8,128)(2,1)S(1)} %get-tuple-element.111), channel_id=1, source_target_pairs={{0,4},{4,0},{8,12},{12,8},{1,5},{5,1},{9,13},{13,9},{2,6},{6,2},{1... | collective-permute-start | bytes 884744 | tf_op jit(solution)/shard_map/ppermute | solution.py:441
  68.2 12.8 %collective-permute-start.21 = (bf16[96,1536]{1,0:T(8,128)(2,1)S(1)}, bf16[96,1536]{1,0:T(8,128)(2,1)S(1)}, u32[]{:S(2)}, u32[]{:S(2)}) collective-permute-start(bf16[96,1536]{1,0:T(8,128)(2,1)S(1)} %add_convert_fusion.5), channel_id=1, source_target_pairs={{0,8},{4,12},{8,0},{12,4},{1,9},{5,13},{9,1},{13,5},{2,10},{6,14},... | collective-permute-start | bytes 884744 | tf_op jit(solution)/shard_map/ppermute | solution.py:441
  76.8 9.4 %collective-permute-start.22 = (bf16[96,1536]{1,0:T(8,128)(2,1)S(1)}, bf16[96,1536]{1,0:T(8,128)(2,1)S(1)}, u32[]{:S(2)}, u32[]{:S(2)}) collective-permute-start(bf16[96,1536]{1,0:T(8,128)(2,1)S(1)} %add_convert_fusion.4), channel_id=1, source_target_pairs={{0,1},{1,0},{2,3},{3,2},{4,5},{5,4},{6,7},{7,6},{8,9},{9,8},{10,11... | collective-permute-start | bytes 884744 | tf_op jit(solution)/shard_map/ppermute | solution.py:441
  77.4 6.7 %collective-permute-start.23 = (bf16[200,384]{1,0:T(8,128)(2,1)S(1)}, bf16[200,384]{1,0:T(8,128)(2,1)S(1)}, u32[]{:S(2)}, u32[]{:S(2)}) collective-permute-start(bf16[200,384]{1,0:T(8,128)(2,1)S(1)} %slice_select_fusion), channel_id=1, source_target_pairs={{0,2},{1,3},{2,0},{3,1},{4,6},{5,7},{6,4},{7,5},{8,10},{9,11},{10,... | collective-permute-start | bytes 460808 | tf_op jit(solution)/shard_map/ppermute | solution.py:441
  80.1 12.2 %collective-permute-start.26 = (bf16[96,1536]{1,0:T(8,128)(2,1)S(1)}, bf16[96,1536]{1,0:T(8,128)(2,1)S(1)}, u32[]{:S(2)}, u32[]{:S(2)}) collective-permute-start(bf16[96,1536]{1,0:T(8,128)(2,1)S(1)} %get-tuple-element.131), channel_id=1, source_target_pairs={{0,4},{4,0},{8,12},{12,8},{1,5},{5,1},{9,13},{13,9},{2,6},{6,2},{1... | collective-permute-start | bytes 884744 | tf_op jit(solution)/shard_map/ppermute | solution.py:441
  86.3 16.1 %collective-permute-start.24 = (bf16[200,384]{1,0:T(8,128)(2,1)S(1)}, bf16[200,384]{1,0:T(8,128)(2,1)S(1)}, u32[]{:S(2)}, u32[]{:S(2)}) collective-permute-start(bf16[200,384]{1,0:T(8,128)(2,1)S(1)} %reduce-precision_convert_fusion), channel_id=1, source_target_pairs={{0,1},{1,0},{2,3},{3,2},{4,5},{5,4},{6,7},{7,6},{8,9},{9,8},{10,11... | collective-permute-start | bytes 460808 | tf_op jit(solution)/shard_map/ppermute | solution.py:441
  90.7 11.6 %collective-permute-start.25 = (bf16[48,1536]{1,0:T(8,128)(2,1)S(1)}, bf16[48,1536]{1,0:T(8,128)(2,1)S(1)}, u32[]{:S(2)}, u32[]{:S(2)}) collective-permute-start(bf16[48,1536]{1,0:T(8,128)(2,1)S(1)} %slice_select_fusion.1), channel_id=1, source_target_pairs={{0,2},{1,3},{2,0},{3,1},{4,6},{5,7},{6,4},{7,5},{8,10},{9,11},{10,... | collective-permute-start | bytes 442376 | tf_op jit(solution)/shard_map/ppermute | solution.py:441
  92.4 7.0 %collective-permute-start.27 = (bf16[96,384]{1,0:T(8,128)(2,1)S(1)}, bf16[96,384]{1,0:T(8,128)(2,1)S(1)}, u32[]{:S(2)}, u32[]{:S(2)}) collective-permute-start(bf16[96,384]{1,0:T(8,128)(2,1)S(1)} %get-tuple-element.133), channel_id=1, source_target_pairs={{0,1},{1,0},{2,3},{3,2},{4,5},{5,4},{6,7},{7,6},{8,9},{9,8},{10,11... | collective-permute-start | bytes 221192 | tf_op jit(solution)/shard_map/ppermute | solution.py:441
  92.5 9.9 %collective-permute-start.28 = (bf16[96,384]{1,0:T(8,128)(2,1)S(1)}, bf16[96,384]{1,0:T(8,128)(2,1)S(1)}, u32[]{:S(2)}, u32[]{:S(2)}) collective-permute-start(bf16[96,384]{1,0:T(8,128)(2,1)S(1)} %get-tuple-element.134), channel_id=1, source_target_pairs={{0,2},{1,3},{2,0},{3,1},{4,6},{5,7},{6,4},{7,5},{8,10},{9,11},{10,... | collective-permute-start | bytes 221192 | tf_op jit(solution)/shard_map/ppermute | solution.py:441
  94.0 8.4 %collective-permute-start.29 = (bf16[96,384]{1,0:T(8,128)(2,1)S(1)}, bf16[96,384]{1,0:T(8,128)(2,1)S(1)}, u32[]{:S(2)}, u32[]{:S(2)}) collective-permute-start(bf16[96,384]{1,0:T(8,128)(2,1)S(1)} %get-tuple-element.135), channel_id=1, source_target_pairs={{0,3},{1,2},{2,1},{3,0},{4,7},{5,6},{6,5},{7,4},{8,11},{9,10},{10,... | collective-permute-start | bytes 221192 | tf_op jit(solution)/shard_map/ppermute | solution.py:441
  102.4 7.8 %collective-permute-start.30 = (bf16[96,384]{1,0:T(8,128)(2,1)S(1)}, bf16[96,384]{1,0:T(8,128)(2,1)S(1)}, u32[]{:S(2)}, u32[]{:S(2)}) collective-permute-start(bf16[96,384]{1,0:T(8,128)(2,1)S(1)} %reduce-precision_convert_fusion.2), channel_id=1, source_target_pairs={{0,1},{1,0},{2,3},{3,2},{4,5},{5,4},{6,7},{7,6},{8,9},{9,8},{10,11... | collective-permute-start | bytes 221192 | tf_op jit(solution)/shard_map/ppermute | solution.py:441
  105.2 6.3 %collective-permute-start.32 = (bf16[96,384]{1,0:T(8,128)(2,1)S(1)}, bf16[96,384]{1,0:T(8,128)(2,1)S(1)}, u32[]{:S(2)}, u32[]{:S(2)}) collective-permute-start(bf16[96,384]{1,0:T(8,128)(2,1)S(1)} %reduce-precision_convert_fusion.2), channel_id=1, source_target_pairs={{0,3},{1,2},{2,1},{3,0},{4,7},{5,6},{6,5},{7,4},{8,11},{9,10},{10,... | collective-permute-start | bytes 221192 | tf_op jit(solution)/shard_map/ppermute | solution.py:441
  (14 other events, 68.8 us)

commit v4 on v3

--- a/solution.py
+++ b/solution.py
@@ -245,30 +245,40 @@
         given = vectors[at].astype(F32)
         small[:, at * part : (at + 1) * part] = given[:8, :part]
         up_bias[:, at * hidden_part : (at + 1) * hidden_part] = given[8:9, :hidden_part]
-    entry = (unit_ref[...] * small[PRE_GAIN : PRE_GAIN + 1] + small[PRE_SHIFT : PRE_SHIFT + 1]).astype(BF)
     arrive(first)
-    packed[...] = (dot(entry, heads[...]) + packed_bias(small)).astype(BF)
-    attention_forward(packed, mixed, count, length, width)
     arrive(second)
-    middle = rows_ref[...] + dot(mixed[...], merge[...]) + small[MERGE_BIAS : MERGE_BIAS + 1]
-    middle_ref[...] = middle
-    mid_ref[...] = mid_rows(middle, small)[0]
-
-
-def widen_kernel(shards, info, mid_ref, up_bias, *refs):
-    act_ref, up, sems = refs[shards * 3 // 2 :]
+
+    @pl.when(info[1] == 0)
+    def _():
+        entry = (unit_ref[...] * small[PRE_GAIN : PRE_GAIN + 1] + small[PRE_SHIFT : PRE_SHIFT + 1]).astype(BF)
+        packed[...] = (dot(entry, heads[...]) + packed_bias(small)).astype(BF)
+        attention_forward(packed, mixed, count, length, width)
+        middle = rows_ref[...] + dot(mixed[...], merge[...]) + small[MERGE_BIAS : MERGE_BIAS + 1]
+        middle_ref[...] = middle
+        mid_ref[...] = mid_rows(middle, small)[0]
+
+
+def feed_forward_kernel(shards, info, mid_ref, middle_ref, small, up_bias, *refs):
     near, far = refs[: shards // 2], refs[shards // 2 : shards * 3 // 2]
-    pieces = (*near, *zip(far[::2], far[1::2]))
-    arrive(fetch(pieces, up, sems, 0, info[0], half=info[4]))
-    hidden = dot(mid_ref[...], up[...]) + up_bias[...]
-    act_ref[...] = gelu_parts(hidden)[0].astype(BF)
-
-
-def narrow_kernel(shards, info, act_ref, middle_ref, small, *refs):
-    out_ref, down, sems = refs[shards:]
-    arrive(fetch(refs[:shards], down, sems, 0, info[0]))
-    out = middle_ref[...] + dot(act_ref[...], down[...]) + small[DOWN_BIAS : DOWN_BIAS + 1]
-    unpad(out_ref, out, BF)
+    down_pieces = refs[shards * 3 // 2 : shards * 5 // 2]
+    out_ref, up, down, sems = refs[shards * 5 // 2 :]
+    me = info[0]
+    first = fetch((*near, *zip(far[::2], far[1::2])), up, sems, 0, me, half=info[4])
+    second = fetch(down_pieces, down, sems, 2 * shards, me)
+    arrive(first)
+    arrive(second)
+
+    @pl.when(info[1] == 0)
+    def _():
+        hidden = dot(mid_ref[...], up[...]) + up_bias[...]
+        act = gelu_parts(hidden)[0].astype(BF)
+        out = middle_ref[...] + dot(act, down[...]) + small[DOWN_BIAS : DOWN_BIAS + 1]
+        unpad(out_ref, out, BF)
+
+
+def act_gradient_kernel(cotangent, down, grad_act_ref, grad_ref):
+    incoming = pad_images([cotangent[n] for n in range(cotangent.shape[0])], grad_ref)
+    grad_act_ref[...] = dot_nt(incoming.astype(BF), down[...])
 
 
 def both_ways_kernel(
@@ -276,6 +286,7 @@
     first_rows,
     arrived,
     cotangent,
+    grad_act,
     small,
     up_bias,
     heads,
@@ -314,7 +325,7 @@
     out = middle + dot(act_ref[...], down[...]) + small[DOWN_BIAS : DOWN_BIAS + 1]
     unpad(out_ref, out, BF)
     incoming = pad_images([cotangent[n] for n in range(count)], grad_ref)
-    grad_hidden = (dot_nt(incoming.astype(BF), down[...]) * slope_ref[...]).astype(BF)
+    grad_hidden = (grad_act[...] * slope_ref[...]).astype(BF)
     grad_mid = dot_nt(grad_hidden, up[...])
     grad_middle = incoming + norm_backward(
         grad_mid, unit_two_ref[...], inverse_two_ref[...], small[MID_GAIN : MID_GAIN + 1]
@@ -502,21 +513,21 @@
     lower = lambda block: block[: block.shape[0] // 2]
     upper = lambda block: block[block.shape[0] // 2 :]
     own_half = lambda block: jnp.where(odd, upper(block), lower(block))
+    other_half = lambda block: jnp.where(odd, lower(block), upper(block))
     whole = lambda own, other: jnp.concatenate([jnp.where(odd, other, own), jnp.where(odd, own, other)]).astype(F32)
 
     down_far, *leaving = together(far(leaving[0]), *leaving[1:])
     down = added(*kept[0], down_far)
 
-    up_far, down_near = together(far(leaving[0]), swapped(down, axis, 1))
-    up, down = added(*kept[1], up_far), added(down, down_near)
-
-    rest_far, up_near, down_next = together(far(leaving[1]), swapped(up, axis, 1), swapped(own_half(down), axis, 2))
+    up_far, down_near, rest = together(far(leaving[0]), swapped(other_half(down), axis, 1), leaving[1])
+    up, down = added(*kept[1], up_far), added(own_half(down), down_near)
+
+    rest_far, up_near, down_next = together(far(rest), swapped(other_half(up), axis, 1), swapped(down, axis, 2))
     blocks = column_blocks(at, (*kept[2], rest_far), size)
-    pair = added(up, up_near)
-    down = rounded(own_half(down), down_next)
-
-    down_back, up_next, *received = together(swapped(down, axis, 1), swapped(own_half(pair), axis, 2), *others(blocks))
-    own, up_full = rounded(blocks[0], *received), rounded(own_half(pair), up_next)
+    up, down = added(own_half(up), up_near), rounded(down, down_next)
+
+    down_back, up_next, *received = together(swapped(down, axis, 1), swapped(up, axis, 2), *others(blocks))
+    own, up_full = rounded(blocks[0], *received), rounded(up, up_next)
 
     up_total = whole(up_full, swapped(up_full, axis, 1))
     full = [own, *after(tuple(others([own] * size)), up_total)]
@@ -526,7 +537,11 @@
 
 def totals_over(grads, axes):
     scattered, axis = axes
-    leaving, kept = zip(*(nearer_sums(pieces, scattered) for pieces in grads))
+    leaving, kept = [], []
+    for pieces in grads:
+        one, terms = nearer_sums([after(piece, *leaving[:1]) for piece in pieces], scattered)
+        leaving.append(one)
+        kept.append(terms)
     if lax.axis_size(axis) == 4:
         return totals_over_line(leaving, kept, axes)
     last = lax.axis_size(scattered) // 2
@@ -625,34 +640,34 @@
         work * (wide + width),
     )
     down_pieces = gather_pieces(down_weight[0], "fsdp", mid)
-    act, up = call(
-        bind(widen_kernel),
-        "widen",
+    first_out, up, down = call(
+        bind(feed_forward_kernel),
+        "feed_forward",
         info,
-        (mid, wide_bias),
-        (*up_near, *(one for two in zip(*up_halves) for one in two)),
-        (shape((tall, hidden_width), BF), full_up),
-        [sems(2)],
+        (mid, middle, small, wide_bias),
+        (*up_near, *(one for two in zip(*up_halves) for one in two), *down_pieces),
+        (shape(images.shape, BF), full_up, full_down),
+        [sems(3)],
+        2 * work * hidden_width,
+    )
+    arrived = lax.ppermute(first_out, "section", [(0, 1)])
+
+    (grad_act,) = call(
+        act_gradient_kernel,
+        "act_gradient",
+        None,
+        (cotangent, down),
+        (),
+        (shape((tall, hidden_width), F32),),
+        [scratch_rows],
         work * hidden_width,
-        (down_pieces[shards // 2],),
-    )
-    first_out, down = call(
-        bind(narrow_kernel),
-        "narrow",
-        info,
-        (act, middle, small),
-        down_pieces,
-        (shape(images.shape, BF), full_down),
-        [sems(1)],
-        work * hidden_width,
-    )
-    arrived = lax.ppermute(first_out, "section", [(0, 1)])
+    )
 
     layer_out, sent, packed, probs, mixed, act, slope, *kept = call(
         both_ways_kernel,
         "both_ways",
         info,
-        (first_rows, arrived, cotangent, small, wide_bias, heads, merge, up, down),
+        (first_rows, arrived, cotangent, grad_act, small, wide_bias, heads, merge, up, down),
         (),
         (
             shape(images.shape, BF),

time: 115 us -> 110 us (0.957)
  waiting for transfers between devices: 48.7 us -> 45.1 us
  starting transfers between devices: 38.6 us -> 36.5 us
  other arithmetic: 4.81 us -> 6.44 us
    ppermute x32, waiting for transfers between devices: 41 us -> 37.9 us  [swapped(): lax.ppermute(block, axis, [(i, i ^ bit) for i in range(lax.axis_size(axis...]
    convert_element_type x7, other arithmetic: 0.59 us -> 2.26 us  [added(): return sum((term.astype(F32) for term in terms)).astype(BF)]
    ppermute x32, starting transfers between devices: 33.4 us -> 32.1 us  [swapped(): lax.ppermute(block, axis, [(i, i ^ bit) for i in range(lax.axis_size(axis...]
  transfers between devices with their start and end apart: 34 -> 34, of which waited for: 18 -> 17; matrix products, arithmetic and copies ran while one was open for 6% -> 8% of each run, Pallas kernels for 4% -> 3%
where the time goes in v4:
time: 110 us
  waiting for transfers between devices  45.1 us (41%)
  starting transfers between devices  36.5 us (33%)
  Pallas kernels  16.5 us (15%)
  other arithmetic  6.44 us (6%)
  local copies, waits for them, and re-layouts  4.6 us (4%)
    ppermute x32, waiting for transfers between devices, swapped(): lax.ppermute(block, axis, [(i, i ^ bit) for i in range(lax.axis_size(axis...  37.9 us
    ppermute x32, starting transfers between devices, swapped(): lax.ppermute(block, axis, [(i, i ^ bit) for i in range(lax.axis_size(axis...  32.1 us
    pallas_call x8, Pallas kernels, call(): pl.pallas_call(lambda *refs: kernel(*refs[:used], *refs[used + len(earlie...  16.5 us
    ppermute x1, waiting for transfers between devices, local(): returned = lax.ppermute(sent, 'section', [(1, 0)])  5.16 us
    unnamed x12, local copies, waits for them, and re-layouts  3.42 us
    ppermute x1, starting transfers between devices, local(): arrived = lax.ppermute(first_out, 'section', [(0, 1)])  2.99 us
    convert_element_type x7, other arithmetic, added(): return sum((term.astype(F32) for term in terms)).astype(BF)  2.26 us
  transfers between devices with their start and end apart: 34, of which 17 were waited for; matrix products, arithmetic and copies ran while one was open for 8% of the time, Pallas kernels for 3%

profile of v4, /device:TPU:0, one launch (start us, length us, event | category | flops | bytes accessed | tf_op | source)
XLA Modules:
  0.0 110.0 jit_solution(16239812581499137287)
XLA Ops:
  0.7 2.0 %pack.1 = (bf16[112,1536]{1,0:T(8,128)(2,1)}, bf16[96,768]{1,0:T(8,128)(2,1)}) custom-call(s32[1]{0:T(128)} %bitcast.3.refs_0_, bf16[96,1152]{1,0:T(8,128)(2,1)} %bitcast.33, bf16[96,384]{1,0:T(8,128)(2,1)} %bitcast.34, bf16[96,1536]{1,0:T(8,128)(2,1)} %bitcast.25, bf16[1,96]{1,0:T(2,128)(2,1)} %refs_4_.1, bf16[1,96]{1,0:T(2,128)(2,1)} %refs_5_.1, ...), custom_call_target="tpu_custom_call" | custom-call | flops 1 | bytes 1083648 | tf_op jit(solution)/shard_map/pack/pallas_call | solution.py:435
  2.7 3.0 %collective-permute-start.1 = (bf16[112,1536]{1,0:T(8,128)(2,1)}, bf16[112,1536]{1,0:T(8,128)(2,1)S(1)}, u32[]{:S(2)}, u32[]{:S(2)}) collective-permute-start(bf16[112,1536]{1,0:T(8,128)(2,1)} %get-tuple-element.90.refs_3_), channel_id=1, source_target_pairs={{0,8},{4,12},{8,0},{12,4},{1,9},{5,13},{9,1},{13,5},{2,10},{6,14},... | collective-permute-start | bytes 1032200 | tf_op jit(solution)/shard_map/ppermute | solution.py:452
  8.1 9.0 %collective-permute-done.2.refs_7_ = bf16[96,768]{1,0:T(8,128)(2,1)S(1)} collective-permute-done((bf16[96,768]{1,0:T(8,128)(2,1)}, bf16[96,768]{1,0:T(8,128)(2,1)S(1)}, u32[]{:S(2)}, u32[]{:S(2)}) %collective-permute-start.2) | collective-permute-done | bytes 147488 | tf_op jit(solution)/shard_map/ppermute | solution.py:452
  17.6 1.7 %collective-permute-start.9 = (bf16[384,384]{1,0:T(8,128)(2,1)}, bf16[384,384]{1,0:T(8,128)(2,1)S(1)}, u32[]{:S(2)}, u32[]{:S(2)}) collective-permute-start(bf16[384,384]{1,0:T(8,128)(2,1)} %bitcast.28), channel_id=1, source_target_pairs={{0,8},{4,12},{8,0},{12,4},{1,9},{5,13},{9,1},{13,5},{2,10},{6,14},... | collective-permute-start | bytes 884744 | tf_op jit(solution)/shard_map/ppermute | solution.py:452
  19.9 1.6 %collective-permute-start.5 = (bf16[96,768]{1,0:T(8,128)(2,1)S(1)}, bf16[96,768]{1,0:T(8,128)(2,1)S(1)}, u32[]{:S(2)}, u32[]{:S(2)}) collective-permute-start(bf16[96,768]{1,0:T(8,128)(2,1)S(1)} %collective-permute-done.2.refs_7_), channel_id=1, source_target_pairs={{0,1},{1,0},{2,3},{3,2},{4,5},{5,4},{6,7},{7,6},{8,9},{9,8},{10,11... | collective-permute-start | bytes 442376 | tf_op jit(solution)/shard_map/ppermute | solution.py:452
  22.4 2.4 %attend.1 = (f32[160,384]{1,0:T(8,128)S(1)}, bf16[160,384]{1,0:T(8,128)(2,1)S(1)}, bf16[384,1152]{1,0:T(8,128)(2,1)S(1)}, bf16[384,384]{1,0:T(8,128)(2,1)S(1)}, ...) custom-call(s32[5]{0:T(128)S(1)} %pad_add_fusion.refs_0_, f32[160,384]{1,0:T(8,128)S(1)} %get-tuple-element.88.refs_1_, ...), custom_call_target="tpu_custom_call" | custom-call | flops 188743680 | bytes 3434496 | tf_op jit(solution)/shard_map/attend/pallas_call | solution.py:435
  24.9 1.9 %collective-permute-done.9.refs_13_ = bf16[384,384]{1,0:T(8,128)(2,1)S(1)} collective-permute-done((bf16[384,384]{1,0:T(8,128)(2,1)}, bf16[384,384]{1,0:T(8,128)(2,1)S(1)}, u32[]{:S(2)}, u32[]{:S(2)}) %collective-permute-start.9) | collective-permute-done | bytes 294944 | tf_op jit(solution)/shard_map/ppermute | solution.py:452
  28.8 1.8 %feed_forward.1 = (bf16[2,65,384]{2,1,0:T(8,128)(2,1)S(1)}, bf16[384,1536]{1,0:T(8,128)(2,1)S(1)}, bf16[1536,384]{1,0:T(8,128)(2,1)S(1)}) custom-call(s32[5]{0:T(128)S(1)} %pad_add_fusion.refs_0_, bf16[160,384]{1,0:T(8,128)(2,1)S(1)} %get-tuple-element.93.refs_1_, f32[160,384]{1,0:T(8,128)S(1)} %get-tuple-element.94.refs_2_, ...), custom_call_target="tpu_custom_call" | custom-call | flops 377487360 | bytes 5205504 | tf_op jit(solution)/shard_map/feed_forward/pallas_call | solution.py:435
  30.6 3.0 %collective-permute-start.11 = (bf16[2,65,384]{2,1,0:T(8,128)(2,1)S(1)}, bf16[2,65,384]{2,1,0:T(8,128)(2,1)S(1)}, u32[]{:S(2)}, u32[]{:S(2)}) collective-permute-start(bf16[2,65,384]{2,1,0:T(8,128)(2,1)S(1)} %get-tuple-element.99), channel_id=1, source_target_pairs={{0,16},{1,17},{2,18},{3,19},{4,20},{5,21},{6,22},{7,23},{8,24},{9,... | collective-permute-start | bytes 299528 | tf_op jit(solution)/shard_map/ppermute | solution.py:653
  34.2 2.0 %collective-permute-done.11.refs_2_ = bf16[2,65,384]{2,1,0:T(8,128)(2,1)S(1)} collective-permute-done((bf16[2,65,384]{2,1,0:T(8,128)(2,1)S(1)}, bf16[2,65,384]{2,1,0:T(8,128)(2,1)S(1)}, u32[]{:S(2)}, u32[]{:S(2)}) %collective-permute-start.11) | collective-permute-done | bytes 99872 | tf_op jit(solution)/shard_map/ppermute | solution.py:653
  36.2 4.7 %both_ways.1 = (bf16[2,65,384]{2,1,0:T(8,128)(2,1)S(1)}, bf16[2,65,384]{2,1,0:T(8,128)(2,1)S(1)}, bf16[160,1152]{1,0:T(8,128)(2,1)S(1)}, f32[960,80]{1,0:T(8,128...) custom-call(s32[5]{0:T(128)S(1)} %pad_add_fusion.refs_0_, ...), custom_call_target="tpu_custom_call" | custom-call | flops 1132462080 | bytes 8197376 | tf_op jit(solution)/shard_map/both_ways/pallas_call | solution.py:435
  42.4 5.2 %collective-permute-done.12.refs_1_ = bf16[2,65,384]{2,1,0:T(8,128)(2,1)S(1)} collective-permute-done((bf16[2,65,384]{2,1,0:T(8,128)(2,1)S(1)}, bf16[2,65,384]{2,1,0:T(8,128)(2,1)S(1)}, u32[]{:S(2)}, u32[]{:S(2)}) %collective-permute-start.12) | collective-permute-done | bytes 99872 | tf_op jit(solution)/shard_map/ppermute | solution.py:690
  47.5 4.2 %rest_grad.1 = (bf16[400,384]{1,0:T(8,128)(2,1)S(1)}, bf16[400,384]{1,0:T(8,128)(2,1)S(1)}, bf16[400,384]{1,0:T(8,128)(2,1)S(1)}, bf16[400,384]{1,0:T(8,128)(2,1...) custom-call(s32[5]{0:T(128)S(1)} %pad_add_fusion.refs_0_, ...), custom_call_target="tpu_custom_call" | custom-call | flops 1132462080 | bytes 10550528 | tf_op jit(solution)/shard_map/rest_grad/pallas_call | solution.py:435
  51.8 1.6 %collective-permute-done.13 = bf16[400,384]{1,0:T(8,128)(2,1)S(1)} collective-permute-done((bf16[400,384]{1,0:T(8,128)(2,1)S(1)}, bf16[400,384]{1,0:T(8,128)(2,1)S(1)}, u32[]{:S(2)}, u32[]{:S(2)}) %collective-permute-start.13) | collective-permute-done | bytes 307232 | tf_op jit(solution)/shard_map/ppermute | solution.py:452
  57.8 6.4 %collective-permute-done.15 = bf16[400,384]{1,0:T(8,128)(2,1)S(1)} collective-permute-done((bf16[400,384]{1,0:T(8,128)(2,1)}, bf16[400,384]{1,0:T(8,128)(2,1)S(1)}, u32[]{:S(2)}, u32[]{:S(2)}) %collective-permute-start.15) | collective-permute-done | bytes 307232 | tf_op jit(solution)/shard_map/ppermute | solution.py:452
  65.8 1.6 %collective-permute-start.20 = (bf16[200,384]{1,0:T(8,128)(2,1)S(1)}, bf16[200,384]{1,0:T(8,128)(2,1)S(1)}, u32[]{:S(2)}, u32[]{:S(2)}) collective-permute-start(bf16[200,384]{1,0:T(8,128)(2,1)S(1)} %broadcast_select_fusion.2), channel_id=1, source_target_pairs={{0,1},{1,0},{2,3},{3,2},{4,5},{5,4},{6,7},{7,6},{8,9},{9,8},{10,11... | collective-permute-start | bytes 460808 | tf_op jit(solution)/shard_map/ppermute | solution.py:452
  67.5 3.6 %collective-permute-done.20 = bf16[200,384]{1,0:T(8,128)(2,1)S(1)} collective-permute-done((bf16[200,384]{1,0:T(8,128)(2,1)S(1)}, bf16[200,384]{1,0:T(8,128)(2,1)S(1)}, u32[]{:S(2)}, u32[]{:S(2)}) %collective-permute-start.20) | collective-permute-done | bytes 153632 | tf_op jit(solution)/shard_map/ppermute | solution.py:452
  74.0 2.7 %collective-permute-start.23 = (bf16[200,384]{1,0:T(8,128)(2,1)S(1)}, bf16[200,384]{1,0:T(8,128)(2,1)S(1)}, u32[]{:S(2)}, u32[]{:S(2)}) collective-permute-start(bf16[200,384]{1,0:T(8,128)(2,1)S(1)} %add_convert_fusion.5), channel_id=1, source_target_pairs={{0,2},{1,3},{2,0},{3,1},{4,6},{5,7},{6,4},{7,5},{8,10},{9,11},{10,... | collective-permute-start | bytes 460808 | tf_op jit(solution)/shard_map/ppermute | solution.py:452
  76.8 1.6 %collective-permute-start.22 = (bf16[48,1536]{1,0:T(8,128)(2,1)S(1)}, bf16[48,1536]{1,0:T(8,128)(2,1)S(1)}, u32[]{:S(2)}, u32[]{:S(2)}) collective-permute-start(bf16[48,1536]{1,0:T(8,128)(2,1)S(1)} %broadcast_select_fusion.3), channel_id=1, source_target_pairs={{0,1},{1,0},{2,3},{3,2},{4,5},{5,4},{6,7},{7,6},{8,9},{9,8},{10,11... | collective-permute-start | bytes 442376 | tf_op jit(solution)/shard_map/ppermute | solution.py:452
  78.4 4.2 %collective-permute-done.22 = bf16[48,1536]{1,0:T(8,128)(2,1)S(1)} collective-permute-done((bf16[48,1536]{1,0:T(8,128)(2,1)S(1)}, bf16[48,1536]{1,0:T(8,128)(2,1)S(1)}, u32[]{:S(2)}, u32[]{:S(2)}) %collective-permute-start.22) | collective-permute-done | bytes 147488 | tf_op jit(solution)/shard_map/ppermute | solution.py:452
  84.1 2.4 %collective-permute-start.25 = (bf16[48,1536]{1,0:T(8,128)(2,1)S(1)}, bf16[48,1536]{1,0:T(8,128)(2,1)S(1)}, u32[]{:S(2)}, u32[]{:S(2)}) collective-permute-start(bf16[48,1536]{1,0:T(8,128)(2,1)S(1)} %add_convert_fusion.6), channel_id=1, source_target_pairs={{0,2},{1,3},{2,0},{3,1},{4,6},{5,7},{6,4},{7,5},{8,10},{9,11},{10,... | collective-permute-start | bytes 442376 | tf_op jit(solution)/shard_map/ppermute | solution.py:452
  88.0 3.1 %collective-permute-start.29 = (bf16[96,384]{1,0:T(8,128)(2,1)S(1)}, bf16[96,384]{1,0:T(8,128)(2,1)S(1)}, u32[]{:S(2)}, u32[]{:S(2)}) collective-permute-start(bf16[96,384]{1,0:T(8,128)(2,1)S(1)} %get-tuple-element.151), channel_id=1, source_target_pairs={{0,3},{1,2},{2,1},{3,0},{4,7},{5,6},{6,5},{7,4},{8,11},{9,10},{10,... | collective-permute-start | bytes 221192 | tf_op jit(solution)/shard_map/ppermute | solution.py:452
  93.0 4.8 %collective-permute-done.28 = bf16[96,384]{1,0:T(8,128)(2,1)S(1)} collective-permute-done((bf16[96,384]{1,0:T(8,128)(2,1)S(1)}, bf16[96,384]{1,0:T(8,128)(2,1)S(1)}, u32[]{:S(2)}, u32[]{:S(2)}) %collective-permute-start.28) | collective-permute-done | bytes 73760 | tf_op jit(solution)/shard_map/ppermute | solution.py:452
  105.5 1.6 %collective-permute-done.32 = bf16[96,384]{1,0:T(8,128)(2,1)S(1)} collective-permute-done((bf16[96,384]{1,0:T(8,128)(2,1)S(1)}, bf16[96,384]{1,0:T(8,128)(2,1)S(1)}, u32[]{:S(2)}, u32[]{:S(2)}) %collective-permute-start.32) | collective-permute-done | bytes 73760 | tf_op jit(solution)/shard_map/ppermute | solution.py:452
  (87 shorter events, 33.1 us)
Async XLA Ops:
  2.7 14.4 %collective-permute-start.1 = (bf16[112,1536]{1,0:T(8,128)(2,1)}, bf16[112,1536]{1,0:T(8,128)(2,1)S(1)}, u32[]{:S(2)}, u32[]{:S(2)}) collective-permute-start(bf16[112,1536]{1,0:T(8,128)(2,1)} %get-tuple-element.90.refs_3_), channel_id=1, source_target_pairs={{0,8},{4,12},{8,0},{12,4},{1,9},{5,13},{9,1},{13,5},{2,10},{6,14},... | collective-permute-start | bytes 1032200 | tf_op jit(solution)/shard_map/ppermute | solution.py:452
  5.7 11.4 %collective-permute-start.2 = (bf16[96,768]{1,0:T(8,128)(2,1)}, bf16[96,768]{1,0:T(8,128)(2,1)S(1)}, u32[]{:S(2)}, u32[]{:S(2)}) collective-permute-start(bf16[96,768]{1,0:T(8,128)(2,1)} %get-tuple-element.91), channel_id=1, source_target_pairs={{0,8},{4,12},{8,0},{12,4},{1,9},{5,13},{9,1},{13,5},{2,10},{6,14},... | collective-permute-start | bytes 442376 | tf_op jit(solution)/shard_map/ppermute | solution.py:452
  17.6 9.1 %collective-permute-start.9 = (bf16[384,384]{1,0:T(8,128)(2,1)}, bf16[384,384]{1,0:T(8,128)(2,1)S(1)}, u32[]{:S(2)}, u32[]{:S(2)}) collective-permute-start(bf16[384,384]{1,0:T(8,128)(2,1)} %bitcast.28), channel_id=1, source_target_pairs={{0,8},{4,12},{8,0},{12,4},{1,9},{5,13},{9,1},{13,5},{2,10},{6,14},... | collective-permute-start | bytes 884744 | tf_op jit(solution)/shard_map/ppermute | solution.py:452
  19.4 7.9 %collective-permute-start.4 = (bf16[96,1536]{1,0:T(8,128)(2,1)}, bf16[96,1536]{1,0:T(8,128)(2,1)S(1)}, u32[]{:S(2)}, u32[]{:S(2)}) collective-permute-start(bf16[96,1536]{1,0:T(8,128)(2,1)} %bitcast.26), channel_id=1, source_target_pairs={{0,4},{4,0},{8,12},{12,8},{1,5},{5,1},{9,13},{13,9},{2,6},{6,2},{1... | collective-permute-start | bytes 884744 | tf_op jit(solution)/shard_map/ppermute | solution.py:452
  19.4 9.2 %collective-permute-start.8 = (bf16[384,384]{1,0:T(8,128)(2,1)}, bf16[384,384]{1,0:T(8,128)(2,1)S(1)}, u32[]{:S(2)}, u32[]{:S(2)}) collective-permute-start(bf16[384,384]{1,0:T(8,128)(2,1)} %bitcast.29), channel_id=1, source_target_pairs={{0,4},{4,0},{8,12},{12,8},{1,5},{5,1},{9,13},{13,9},{2,6},{6,2},{1... | collective-permute-start | bytes 884744 | tf_op jit(solution)/shard_map/ppermute | solution.py:452
  19.9 7.4 %collective-permute-start.5 = (bf16[96,768]{1,0:T(8,128)(2,1)S(1)}, bf16[96,768]{1,0:T(8,128)(2,1)S(1)}, u32[]{:S(2)}, u32[]{:S(2)}) collective-permute-start(bf16[96,768]{1,0:T(8,128)(2,1)S(1)} %collective-permute-done.2.refs_7_), channel_id=1, source_target_pairs={{0,1},{1,0},{2,3},{3,2},{4,5},{5,4},{6,7},{7,6},{8,9},{9,8},{10,11... | collective-permute-start | bytes 442376 | tf_op jit(solution)/shard_map/ppermute | solution.py:452
  30.6 5.6 %collective-permute-start.11 = (bf16[2,65,384]{2,1,0:T(8,128)(2,1)S(1)}, bf16[2,65,384]{2,1,0:T(8,128)(2,1)S(1)}, u32[]{:S(2)}, u32[]{:S(2)}) collective-permute-start(bf16[2,65,384]{2,1,0:T(8,128)(2,1)S(1)} %get-tuple-element.99), channel_id=1, source_target_pairs={{0,16},{1,17},{2,18},{3,19},{4,20},{5,21},{6,22},{7,23},{8,24},{9,... | collective-permute-start | bytes 299528 | tf_op jit(solution)/shard_map/ppermute | solution.py:653
  40.9 6.6 %collective-permute-start.12 = (bf16[2,65,384]{2,1,0:T(8,128)(2,1)S(1)}, bf16[2,65,384]{2,1,0:T(8,128)(2,1)S(1)}, u32[]{:S(2)}, u32[]{:S(2)}) collective-permute-start(bf16[2,65,384]{2,1,0:T(8,128)(2,1)S(1)} %get-tuple-element.105), channel_id=1, source_target_pairs={{16,0},{17,1},{18,2},{19,3},{20,4},{21,5},{22,6},{23,7},{24,8},{25... | collective-permute-start | bytes 299528 | tf_op jit(solution)/shard_map/ppermute | solution.py:690
  54.3 11.4 %collective-permute-start.19 = (bf16[400,384]{1,0:T(8,128)(2,1)S(1)}, bf16[400,384]{1,0:T(8,128)(2,1)S(1)}, u32[]{:S(2)}, u32[]{:S(2)}) collective-permute-start(bf16[400,384]{1,0:T(8,128)(2,1)S(1)} %get-tuple-element.133), channel_id=1, source_target_pairs={{0,4},{4,0},{8,12},{12,8},{1,5},{5,1},{9,13},{13,9},{2,6},{6,2},{1... | collective-permute-start | bytes 921608 | tf_op jit(solution)/shard_map/ppermute | solution.py:452
  54.7 9.5 %collective-permute-start.15 = (bf16[400,384]{1,0:T(8,128)(2,1)}, bf16[400,384]{1,0:T(8,128)(2,1)S(1)}, u32[]{:S(2)}, u32[]{:S(2)}) collective-permute-start(bf16[400,384]{1,0:T(8,128)(2,1)} %add_convert_fusion.1), channel_id=1, source_target_pairs={{0,8},{4,12},{8,0},{12,4},{1,9},{5,13},{9,1},{13,5},{2,10},{6,14},... | collective-permute-start | bytes 921608 | tf_op jit(solution)/shard_map/ppermute | solution.py:452
  64.2 8.2 %collective-permute-start.18 = (bf16[96,1536]{1,0:T(8,128)(2,1)S(1)}, bf16[96,1536]{1,0:T(8,128)(2,1)S(1)}, u32[]{:S(2)}, u32[]{:S(2)}) collective-permute-start(bf16[96,1536]{1,0:T(8,128)(2,1)S(1)} %add_convert_fusion.4), channel_id=1, source_target_pairs={{0,8},{4,12},{8,0},{12,4},{1,9},{5,13},{9,1},{13,5},{2,10},{6,14},... | collective-permute-start | bytes 884744 | tf_op jit(solution)/shard_map/ppermute | solution.py:452
  67.5 9.2 %collective-permute-start.14 = (bf16[96,1536]{1,0:T(8,128)(2,1)S(1)}, bf16[96,1536]{1,0:T(8,128)(2,1)S(1)}, u32[]{:S(2)}, u32[]{:S(2)}) collective-permute-start(bf16[96,1536]{1,0:T(8,128)(2,1)S(1)} %get-tuple-element.122), channel_id=1, source_target_pairs={{0,4},{4,0},{8,12},{12,8},{1,5},{5,1},{9,13},{13,9},{2,6},{6,2},{1... | collective-permute-start | bytes 884744 | tf_op jit(solution)/shard_map/ppermute | solution.py:452
  72.4 10.2 %collective-permute-start.21 = (bf16[96,1536]{1,0:T(8,128)(2,1)S(1)}, bf16[96,1536]{1,0:T(8,128)(2,1)S(1)}, u32[]{:S(2)}, u32[]{:S(2)}) collective-permute-start(bf16[96,1536]{1,0:T(8,128)(2,1)S(1)} %add_convert_fusion.3), channel_id=1, source_target_pairs={{0,8},{4,12},{8,0},{12,4},{1,9},{5,13},{9,1},{13,5},{2,10},{6,14},... | collective-permute-start | bytes 884744 | tf_op jit(solution)/shard_map/ppermute | solution.py:452
  74.0 8.6 %collective-permute-start.23 = (bf16[200,384]{1,0:T(8,128)(2,1)S(1)}, bf16[200,384]{1,0:T(8,128)(2,1)S(1)}, u32[]{:S(2)}, u32[]{:S(2)}) collective-permute-start(bf16[200,384]{1,0:T(8,128)(2,1)S(1)} %add_convert_fusion.5), channel_id=1, source_target_pairs={{0,2},{1,3},{2,0},{3,1},{4,6},{5,7},{6,4},{7,5},{8,10},{9,11},{10,... | collective-permute-start | bytes 460808 | tf_op jit(solution)/shard_map/ppermute | solution.py:452
  76.8 5.8 %collective-permute-start.22 = (bf16[48,1536]{1,0:T(8,128)(2,1)S(1)}, bf16[48,1536]{1,0:T(8,128)(2,1)S(1)}, u32[]{:S(2)}, u32[]{:S(2)}) collective-permute-start(bf16[48,1536]{1,0:T(8,128)(2,1)S(1)} %broadcast_select_fusion.3), channel_id=1, source_target_pairs={{0,1},{1,0},{2,3},{3,2},{4,5},{5,4},{6,7},{7,6},{8,9},{9,8},{10,11... | collective-permute-start | bytes 442376 | tf_op jit(solution)/shard_map/ppermute | solution.py:452
  78.4 8.1 %collective-permute-start.26 = (bf16[96,1536]{1,0:T(8,128)(2,1)S(1)}, bf16[96,1536]{1,0:T(8,128)(2,1)S(1)}, u32[]{:S(2)}, u32[]{:S(2)}) collective-permute-start(bf16[96,1536]{1,0:T(8,128)(2,1)S(1)} %get-tuple-element.147), channel_id=1, source_target_pairs={{0,4},{4,0},{8,12},{12,8},{1,5},{5,1},{9,13},{13,9},{2,6},{6,2},{1... | collective-permute-start | bytes 884744 | tf_op jit(solution)/shard_map/ppermute | solution.py:452
  82.6 15.2 %collective-permute-start.24 = (bf16[200,384]{1,0:T(8,128)(2,1)S(1)}, bf16[200,384]{1,0:T(8,128)(2,1)S(1)}, u32[]{:S(2)}, u32[]{:S(2)}) collective-permute-start(bf16[200,384]{1,0:T(8,128)(2,1)S(1)} %reduce-precision_convert_fusion), channel_id=1, source_target_pairs={{0,1},{1,0},{2,3},{3,2},{4,5},{5,4},{6,7},{7,6},{8,9},{9,8},{10,11... | collective-permute-start | bytes 460808 | tf_op jit(solution)/shard_map/ppermute | solution.py:452
  84.1 13.8 %collective-permute-start.25 = (bf16[48,1536]{1,0:T(8,128)(2,1)S(1)}, bf16[48,1536]{1,0:T(8,128)(2,1)S(1)}, u32[]{:S(2)}, u32[]{:S(2)}) collective-permute-start(bf16[48,1536]{1,0:T(8,128)(2,1)S(1)} %add_convert_fusion.6), channel_id=1, source_target_pairs={{0,2},{1,3},{2,0},{3,1},{4,6},{5,7},{6,4},{7,5},{8,10},{9,11},{10,... | collective-permute-start | bytes 442376 | tf_op jit(solution)/shard_map/ppermute | solution.py:452
  86.6 6.4 %collective-permute-start.27 = (bf16[96,384]{1,0:T(8,128)(2,1)S(1)}, bf16[96,384]{1,0:T(8,128)(2,1)S(1)}, u32[]{:S(2)}, u32[]{:S(2)}) collective-permute-start(bf16[96,384]{1,0:T(8,128)(2,1)S(1)} %get-tuple-element.149), channel_id=1, source_target_pairs={{0,1},{1,0},{2,3},{3,2},{4,5},{5,4},{6,7},{7,6},{8,9},{9,8},{10,11... | collective-permute-start | bytes 221192 | tf_op jit(solution)/shard_map/ppermute | solution.py:452
  86.7 11.1 %collective-permute-start.28 = (bf16[96,384]{1,0:T(8,128)(2,1)S(1)}, bf16[96,384]{1,0:T(8,128)(2,1)S(1)}, u32[]{:S(2)}, u32[]{:S(2)}) collective-permute-start(bf16[96,384]{1,0:T(8,128)(2,1)S(1)} %get-tuple-element.150), channel_id=1, source_target_pairs={{0,2},{1,3},{2,0},{3,1},{4,6},{5,7},{6,4},{7,5},{8,10},{9,11},{10,... | collective-permute-start | bytes 221192 | tf_op jit(solution)/shard_map/ppermute | solution.py:452
  88.0 9.9 %collective-permute-start.29 = (bf16[96,384]{1,0:T(8,128)(2,1)S(1)}, bf16[96,384]{1,0:T(8,128)(2,1)S(1)}, u32[]{:S(2)}, u32[]{:S(2)}) collective-permute-start(bf16[96,384]{1,0:T(8,128)(2,1)S(1)} %get-tuple-element.151), channel_id=1, source_target_pairs={{0,3},{1,2},{2,1},{3,0},{4,7},{5,6},{6,5},{7,4},{8,11},{9,10},{10,... | collective-permute-start | bytes 221192 | tf_op jit(solution)/shard_map/ppermute | solution.py:452
  97.9 7.1 %collective-permute-start.30 = (bf16[96,384]{1,0:T(8,128)(2,1)S(1)}, bf16[96,384]{1,0:T(8,128)(2,1)S(1)}, u32[]{:S(2)}, u32[]{:S(2)}) collective-permute-start(bf16[96,384]{1,0:T(8,128)(2,1)S(1)} %reduce-precision_convert_fusion.2), channel_id=1, source_target_pairs={{0,1},{1,0},{2,3},{3,2},{4,5},{5,4},{6,7},{7,6},{8,9},{9,8},{10,11... | collective-permute-start | bytes 221192 | tf_op jit(solution)/shard_map/ppermute | solution.py:452
  99.3 6.2 %collective-permute-start.31 = (bf16[96,384]{1,0:T(8,128)(2,1)S(1)}, bf16[96,384]{1,0:T(8,128)(2,1)S(1)}, u32[]{:S(2)}, u32[]{:S(2)}) collective-permute-start(bf16[96,384]{1,0:T(8,128)(2,1)S(1)} %reduce-precision_convert_fusion.2), channel_id=1, source_target_pairs={{0,2},{1,3},{2,0},{3,1},{4,6},{5,7},{6,4},{7,5},{8,10},{9,11},{10,... | collective-permute-start | bytes 221192 | tf_op jit(solution)/shard_map/ppermute | solution.py:452
  100.8 6.4 %collective-permute-start.32 = (bf16[96,384]{1,0:T(8,128)(2,1)S(1)}, bf16[96,384]{1,0:T(8,128)(2,1)S(1)}, u32[]{:S(2)}, u32[]{:S(2)}) collective-permute-start(bf16[96,384]{1,0:T(8,128)(2,1)S(1)} %reduce-precision_convert_fusion.2), channel_id=1, source_target_pairs={{0,3},{1,2},{2,1},{3,0},{4,7},{5,6},{6,5},{7,4},{8,11},{9,10},{10,... | collective-permute-start | bytes 221192 | tf_op jit(solution)/shard_map/ppermute | solution.py:452
  (14 other events, 88.1 us)

commit v5 on v4

--- a/solution.py
+++ b/solution.py
@@ -526,7 +526,8 @@
     blocks = column_blocks(at, (*kept[2], rest_far), size)
     up, down = added(own_half(up), up_near), rounded(down, down_next)
 
-    down_back, up_next, *received = together(swapped(down, axis, 1), swapped(up, axis, 2), *others(blocks))
+    down_back = swapped(down, axis, 1)
+    up_next, *received = together(swapped(up, axis, 2), *others(blocks))
     own, up_full = rounded(blocks[0], *received), rounded(up, up_next)
 
     up_total = whole(up_full, swapped(up_full, axis, 1))

time: 110 us -> 109 us (level)
  transfers between devices with their start and end apart: 34 -> 34, of which waited for: 17 -> 15; matrix products, arithmetic and copies ran while one was open for 8% -> 8% of each run, Pallas kernels for 3% -> 4%
where the time goes in v5:
time: 109 us; the launch traced here: 108 us
  waiting for transfers between devices  44.3 us (41%)
  starting transfers between devices  35.6 us (33%)
  Pallas kernels  16.5 us (15%)
  other arithmetic  6.46 us (6%)
  local copies, waits for them, and re-layouts  4.61 us (4%)
    ppermute x32, waiting for transfers between devices, swapped(): lax.ppermute(block, axis, [(i, i ^ bit) for i in range(lax.axis_size(axis...  37.1 us
    ppermute x32, starting transfers between devices, swapped(): lax.ppermute(block, axis, [(i, i ^ bit) for i in range(lax.axis_size(axis...  31.2 us
    pallas_call x8, Pallas kernels, call(): pl.pallas_call(lambda *refs: kernel(*refs[:used], *refs[used + len(earlie...  16.5 us
    ppermute x1, waiting for transfers between devices, local(): returned = lax.ppermute(sent, 'section', [(1, 0)])  5.16 us
    unnamed x12, local copies, waits for them, and re-layouts  3.42 us
    ppermute x1, starting transfers between devices, local(): arrived = lax.ppermute(first_out, 'section', [(0, 1)])  2.99 us
    convert_element_type x7, other arithmetic, added(): return sum((term.astype(F32) for term in terms)).astype(BF)  2.28 us
  transfers between devices with their start and end apart: 34, of which 15 were waited for; matrix products, arithmetic and copies ran while one was open for 8% of the time, Pallas kernels for 4%

profile of v5, /device:TPU:0, one launch (start us, length us, event | category | flops | bytes accessed | tf_op | source)
XLA Modules:
  0.0 108.3 jit_solution(6657119352404516163)
XLA Ops:
  0.7 2.0 %pack.1 = (bf16[112,1536]{1,0:T(8,128)(2,1)}, bf16[96,768]{1,0:T(8,128)(2,1)}) custom-call(s32[1]{0:T(128)} %bitcast.3.refs_0_, bf16[96,1152]{1,0:T(8,128)(2,1)} %bitcast.33, bf16[96,384]{1,0:T(8,128)(2,1)} %bitcast.34, bf16[96,1536]{1,0:T(8,128)(2,1)} %bitcast.25, bf16[1,96]{1,0:T(2,128)(2,1)} %refs_4_.1, bf16[1,96]{1,0:T(2,128)(2,1)} %refs_5_.1, ...), custom_call_target="tpu_custom_call" | custom-call | flops 1 | bytes 1083648 | tf_op jit(solution)/shard_map/pack/pallas_call | solution.py:435
  2.7 3.0 %collective-permute-start.1 = (bf16[112,1536]{1,0:T(8,128)(2,1)}, bf16[112,1536]{1,0:T(8,128)(2,1)S(1)}, u32[]{:S(2)}, u32[]{:S(2)}) collective-permute-start(bf16[112,1536]{1,0:T(8,128)(2,1)} %get-tuple-element.89.refs_3_), channel_id=1, source_target_pairs={{0,8},{4,12},{8,0},{12,4},{1,9},{5,13},{9,1},{13,5},{2,10},{6,14},... | collective-permute-start | bytes 1032200 | tf_op jit(solution)/shard_map/ppermute | solution.py:452
  8.1 9.0 %collective-permute-done.2.refs_7_ = bf16[96,768]{1,0:T(8,128)(2,1)S(1)} collective-permute-done((bf16[96,768]{1,0:T(8,128)(2,1)}, bf16[96,768]{1,0:T(8,128)(2,1)S(1)}, u32[]{:S(2)}, u32[]{:S(2)}) %collective-permute-start.2) | collective-permute-done | bytes 147488 | tf_op jit(solution)/shard_map/ppermute | solution.py:452
  17.6 1.7 %collective-permute-start.9 = (bf16[384,384]{1,0:T(8,128)(2,1)}, bf16[384,384]{1,0:T(8,128)(2,1)S(1)}, u32[]{:S(2)}, u32[]{:S(2)}) collective-permute-start(bf16[384,384]{1,0:T(8,128)(2,1)} %bitcast.28), channel_id=1, source_target_pairs={{0,8},{4,12},{8,0},{12,4},{1,9},{5,13},{9,1},{13,5},{2,10},{6,14},... | collective-permute-start | bytes 884744 | tf_op jit(solution)/shard_map/ppermute | solution.py:452
  19.9 1.6 %collective-permute-start.5 = (bf16[96,768]{1,0:T(8,128)(2,1)S(1)}, bf16[96,768]{1,0:T(8,128)(2,1)S(1)}, u32[]{:S(2)}, u32[]{:S(2)}) collective-permute-start(bf16[96,768]{1,0:T(8,128)(2,1)S(1)} %collective-permute-done.2.refs_7_), channel_id=1, source_target_pairs={{0,1},{1,0},{2,3},{3,2},{4,5},{5,4},{6,7},{7,6},{8,9},{9,8},{10,11... | collective-permute-start | bytes 442376 | tf_op jit(solution)/shard_map/ppermute | solution.py:452
  22.4 2.4 %attend.1 = (f32[160,384]{1,0:T(8,128)S(1)}, bf16[160,384]{1,0:T(8,128)(2,1)S(1)}, bf16[384,1152]{1,0:T(8,128)(2,1)S(1)}, bf16[384,384]{1,0:T(8,128)(2,1)S(1)}, ...) custom-call(s32[5]{0:T(128)S(1)} %pad_add_fusion.refs_0_, f32[160,384]{1,0:T(8,128)S(1)} %get-tuple-element.87.refs_1_, ...), custom_call_target="tpu_custom_call" | custom-call | flops 188743680 | bytes 3434496 | tf_op jit(solution)/shard_map/attend/pallas_call | solution.py:435
  24.9 1.9 %collective-permute-done.9.refs_13_ = bf16[384,384]{1,0:T(8,128)(2,1)S(1)} collective-permute-done((bf16[384,384]{1,0:T(8,128)(2,1)}, bf16[384,384]{1,0:T(8,128)(2,1)S(1)}, u32[]{:S(2)}, u32[]{:S(2)}) %collective-permute-start.9) | collective-permute-done | bytes 294944 | tf_op jit(solution)/shard_map/ppermute | solution.py:452
  28.8 1.8 %feed_forward.1 = (bf16[2,65,384]{2,1,0:T(8,128)(2,1)S(1)}, bf16[384,1536]{1,0:T(8,128)(2,1)S(1)}, bf16[1536,384]{1,0:T(8,128)(2,1)S(1)}) custom-call(s32[5]{0:T(128)S(1)} %pad_add_fusion.refs_0_, bf16[160,384]{1,0:T(8,128)(2,1)S(1)} %get-tuple-element.92.refs_1_, f32[160,384]{1,0:T(8,128)S(1)} %get-tuple-element.93.refs_2_, ...), custom_call_target="tpu_custom_call" | custom-call | flops 377487360 | bytes 5205504 | tf_op jit(solution)/shard_map/feed_forward/pallas_call | solution.py:435
  30.6 3.0 %collective-permute-start.11 = (bf16[2,65,384]{2,1,0:T(8,128)(2,1)S(1)}, bf16[2,65,384]{2,1,0:T(8,128)(2,1)S(1)}, u32[]{:S(2)}, u32[]{:S(2)}) collective-permute-start(bf16[2,65,384]{2,1,0:T(8,128)(2,1)S(1)} %get-tuple-element.98), channel_id=1, source_target_pairs={{0,16},{1,17},{2,18},{3,19},{4,20},{5,21},{6,22},{7,23},{8,24},{9,... | collective-permute-start | bytes 299528 | tf_op jit(solution)/shard_map/ppermute | solution.py:654
  34.2 2.0 %collective-permute-done.11.refs_2_ = bf16[2,65,384]{2,1,0:T(8,128)(2,1)S(1)} collective-permute-done((bf16[2,65,384]{2,1,0:T(8,128)(2,1)S(1)}, bf16[2,65,384]{2,1,0:T(8,128)(2,1)S(1)}, u32[]{:S(2)}, u32[]{:S(2)}) %collective-permute-start.11) | collective-permute-done | bytes 99872 | tf_op jit(solution)/shard_map/ppermute | solution.py:654
  36.2 4.7 %both_ways.1 = (bf16[2,65,384]{2,1,0:T(8,128)(2,1)S(1)}, bf16[2,65,384]{2,1,0:T(8,128)(2,1)S(1)}, bf16[160,1152]{1,0:T(8,128)(2,1)S(1)}, f32[960,80]{1,0:T(8,128...) custom-call(s32[5]{0:T(128)S(1)} %pad_add_fusion.refs_0_, ...), custom_call_target="tpu_custom_call" | custom-call | flops 1132462080 | bytes 8197376 | tf_op jit(solution)/shard_map/both_ways/pallas_call | solution.py:435
  42.4 5.2 %collective-permute-done.12.refs_1_ = bf16[2,65,384]{2,1,0:T(8,128)(2,1)S(1)} collective-permute-done((bf16[2,65,384]{2,1,0:T(8,128)(2,1)S(1)}, bf16[2,65,384]{2,1,0:T(8,128)(2,1)S(1)}, u32[]{:S(2)}, u32[]{:S(2)}) %collective-permute-start.12) | collective-permute-done | bytes 99872 | tf_op jit(solution)/shard_map/ppermute | solution.py:691
  47.5 4.2 %rest_grad.1 = (bf16[400,384]{1,0:T(8,128)(2,1)S(1)}, bf16[400,384]{1,0:T(8,128)(2,1)S(1)}, bf16[400,384]{1,0:T(8,128)(2,1)S(1)}, bf16[400,384]{1,0:T(8,128)(2,1...) custom-call(s32[5]{0:T(128)S(1)} %pad_add_fusion.refs_0_, ...), custom_call_target="tpu_custom_call" | custom-call | flops 1132462080 | bytes 10550528 | tf_op jit(solution)/shard_map/rest_grad/pallas_call | solution.py:435
  51.8 1.6 %collective-permute-done.13 = bf16[400,384]{1,0:T(8,128)(2,1)S(1)} collective-permute-done((bf16[400,384]{1,0:T(8,128)(2,1)S(1)}, bf16[400,384]{1,0:T(8,128)(2,1)S(1)}, u32[]{:S(2)}, u32[]{:S(2)}) %collective-permute-start.13) | collective-permute-done | bytes 307232 | tf_op jit(solution)/shard_map/ppermute | solution.py:452
  57.8 6.4 %collective-permute-done.15 = bf16[400,384]{1,0:T(8,128)(2,1)S(1)} collective-permute-done((bf16[400,384]{1,0:T(8,128)(2,1)}, bf16[400,384]{1,0:T(8,128)(2,1)S(1)}, u32[]{:S(2)}, u32[]{:S(2)}) %collective-permute-start.15) | collective-permute-done | bytes 307232 | tf_op jit(solution)/shard_map/ppermute | solution.py:452
  65.8 1.6 %collective-permute-start.20 = (bf16[200,384]{1,0:T(8,128)(2,1)S(1)}, bf16[200,384]{1,0:T(8,128)(2,1)S(1)}, u32[]{:S(2)}, u32[]{:S(2)}) collective-permute-start(bf16[200,384]{1,0:T(8,128)(2,1)S(1)} %broadcast_select_fusion.2), channel_id=1, source_target_pairs={{0,1},{1,0},{2,3},{3,2},{4,5},{5,4},{6,7},{7,6},{8,9},{9,8},{10,11... | collective-permute-start | bytes 460808 | tf_op jit(solution)/shard_map/ppermute | solution.py:452
  67.5 3.6 %collective-permute-done.20 = bf16[200,384]{1,0:T(8,128)(2,1)S(1)} collective-permute-done((bf16[200,384]{1,0:T(8,128)(2,1)S(1)}, bf16[200,384]{1,0:T(8,128)(2,1)S(1)}, u32[]{:S(2)}, u32[]{:S(2)}) %collective-permute-start.20) | collective-permute-done | bytes 153632 | tf_op jit(solution)/shard_map/ppermute | solution.py:452
  74.0 2.7 %collective-permute-start.23 = (bf16[200,384]{1,0:T(8,128)(2,1)S(1)}, bf16[200,384]{1,0:T(8,128)(2,1)S(1)}, u32[]{:S(2)}, u32[]{:S(2)}) collective-permute-start(bf16[200,384]{1,0:T(8,128)(2,1)S(1)} %add_convert_fusion.5), channel_id=1, source_target_pairs={{0,2},{1,3},{2,0},{3,1},{4,6},{5,7},{6,4},{7,5},{8,10},{9,11},{10,... | collective-permute-start | bytes 460808 | tf_op jit(solution)/shard_map/ppermute | solution.py:452
  76.8 1.6 %collective-permute-start.22 = (bf16[48,1536]{1,0:T(8,128)(2,1)S(1)}, bf16[48,1536]{1,0:T(8,128)(2,1)S(1)}, u32[]{:S(2)}, u32[]{:S(2)}) collective-permute-start(bf16[48,1536]{1,0:T(8,128)(2,1)S(1)} %broadcast_select_fusion.3), channel_id=1, source_target_pairs={{0,1},{1,0},{2,3},{3,2},{4,5},{5,4},{6,7},{7,6},{8,9},{9,8},{10,11... | collective-permute-start | bytes 442376 | tf_op jit(solution)/shard_map/ppermute | solution.py:452
  78.4 4.2 %collective-permute-done.22 = bf16[48,1536]{1,0:T(8,128)(2,1)S(1)} collective-permute-done((bf16[48,1536]{1,0:T(8,128)(2,1)S(1)}, bf16[48,1536]{1,0:T(8,128)(2,1)S(1)}, u32[]{:S(2)}, u32[]{:S(2)}) %collective-permute-start.22) | collective-permute-done | bytes 147488 | tf_op jit(solution)/shard_map/ppermute | solution.py:452
  84.0 2.7 %collective-permute-start.27 = (bf16[96,384]{1,0:T(8,128)(2,1)S(1)}, bf16[96,384]{1,0:T(8,128)(2,1)S(1)}, u32[]{:S(2)}, u32[]{:S(2)}) collective-permute-start(bf16[96,384]{1,0:T(8,128)(2,1)S(1)} %get-tuple-element.149), channel_id=1, source_target_pairs={{0,1},{1,0},{2,3},{3,2},{4,5},{5,4},{6,7},{7,6},{8,9},{9,8},{10,11... | collective-permute-start | bytes 221192 | tf_op jit(solution)/shard_map/ppermute | solution.py:452
  87.2 2.0 %collective-permute-start.29 = (bf16[96,384]{1,0:T(8,128)(2,1)S(1)}, bf16[96,384]{1,0:T(8,128)(2,1)S(1)}, u32[]{:S(2)}, u32[]{:S(2)}) collective-permute-start(bf16[96,384]{1,0:T(8,128)(2,1)S(1)} %get-tuple-element.151), channel_id=1, source_target_pairs={{0,3},{1,2},{2,1},{3,0},{4,7},{5,6},{6,5},{7,4},{8,11},{9,10},{10,... | collective-permute-start | bytes 221192 | tf_op jit(solution)/shard_map/ppermute | solution.py:452
  91.7 4.3 %collective-permute-done.28 = bf16[96,384]{1,0:T(8,128)(2,1)S(1)} collective-permute-done((bf16[96,384]{1,0:T(8,128)(2,1)S(1)}, bf16[96,384]{1,0:T(8,128)(2,1)S(1)}, u32[]{:S(2)}, u32[]{:S(2)}) %collective-permute-start.28) | collective-permute-done | bytes 73760 | tf_op jit(solution)/shard_map/ppermute | solution.py:452
  97.5 1.6 %collective-permute-start.31 = (bf16[96,384]{1,0:T(8,128)(2,1)S(1)}, bf16[96,384]{1,0:T(8,128)(2,1)S(1)}, u32[]{:S(2)}, u32[]{:S(2)}) collective-permute-start(bf16[96,384]{1,0:T(8,128)(2,1)S(1)} %reduce-precision_convert_fusion.2), channel_id=1, source_target_pairs={{0,2},{1,3},{2,0},{3,1},{4,6},{5,7},{6,4},{7,5},{8,10},{9,11},{10,... | collective-permute-start | bytes 221192 | tf_op jit(solution)/shard_map/ppermute | solution.py:452
  (87 shorter events, 32.7 us)
Async XLA Ops:
  2.7 14.4 %collective-permute-start.1 = (bf16[112,1536]{1,0:T(8,128)(2,1)}, bf16[112,1536]{1,0:T(8,128)(2,1)S(1)}, u32[]{:S(2)}, u32[]{:S(2)}) collective-permute-start(bf16[112,1536]{1,0:T(8,128)(2,1)} %get-tuple-element.89.refs_3_), channel_id=1, source_target_pairs={{0,8},{4,12},{8,0},{12,4},{1,9},{5,13},{9,1},{13,5},{2,10},{6,14},... | collective-permute-start | bytes 1032200 | tf_op jit(solution)/shard_map/ppermute | solution.py:452
  5.7 11.4 %collective-permute-start.2 = (bf16[96,768]{1,0:T(8,128)(2,1)}, bf16[96,768]{1,0:T(8,128)(2,1)S(1)}, u32[]{:S(2)}, u32[]{:S(2)}) collective-permute-start(bf16[96,768]{1,0:T(8,128)(2,1)} %get-tuple-element.90), channel_id=1, source_target_pairs={{0,8},{4,12},{8,0},{12,4},{1,9},{5,13},{9,1},{13,5},{2,10},{6,14},... | collective-permute-start | bytes 442376 | tf_op jit(solution)/shard_map/ppermute | solution.py:452
  17.6 9.1 %collective-permute-start.9 = (bf16[384,384]{1,0:T(8,128)(2,1)}, bf16[384,384]{1,0:T(8,128)(2,1)S(1)}, u32[]{:S(2)}, u32[]{:S(2)}) collective-permute-start(bf16[384,384]{1,0:T(8,128)(2,1)} %bitcast.28), channel_id=1, source_target_pairs={{0,8},{4,12},{8,0},{12,4},{1,9},{5,13},{9,1},{13,5},{2,10},{6,14},... | collective-permute-start | bytes 884744 | tf_op jit(solution)/shard_map/ppermute | solution.py:452
  19.4 7.9 %collective-permute-start.4 = (bf16[96,1536]{1,0:T(8,128)(2,1)}, bf16[96,1536]{1,0:T(8,128)(2,1)S(1)}, u32[]{:S(2)}, u32[]{:S(2)}) collective-permute-start(bf16[96,1536]{1,0:T(8,128)(2,1)} %bitcast.26), channel_id=1, source_target_pairs={{0,4},{4,0},{8,12},{12,8},{1,5},{5,1},{9,13},{13,9},{2,6},{6,2},{1... | collective-permute-start | bytes 884744 | tf_op jit(solution)/shard_map/ppermute | solution.py:452
  19.4 9.2 %collective-permute-start.8 = (bf16[384,384]{1,0:T(8,128)(2,1)}, bf16[384,384]{1,0:T(8,128)(2,1)S(1)}, u32[]{:S(2)}, u32[]{:S(2)}) collective-permute-start(bf16[384,384]{1,0:T(8,128)(2,1)} %bitcast.29), channel_id=1, source_target_pairs={{0,4},{4,0},{8,12},{12,8},{1,5},{5,1},{9,13},{13,9},{2,6},{6,2},{1... | collective-permute-start | bytes 884744 | tf_op jit(solution)/shard_map/ppermute | solution.py:452
  19.9 7.4 %collective-permute-start.5 = (bf16[96,768]{1,0:T(8,128)(2,1)S(1)}, bf16[96,768]{1,0:T(8,128)(2,1)S(1)}, u32[]{:S(2)}, u32[]{:S(2)}) collective-permute-start(bf16[96,768]{1,0:T(8,128)(2,1)S(1)} %collective-permute-done.2.refs_7_), channel_id=1, source_target_pairs={{0,1},{1,0},{2,3},{3,2},{4,5},{5,4},{6,7},{7,6},{8,9},{9,8},{10,11... | collective-permute-start | bytes 442376 | tf_op jit(solution)/shard_map/ppermute | solution.py:452
  30.6 5.6 %collective-permute-start.11 = (bf16[2,65,384]{2,1,0:T(8,128)(2,1)S(1)}, bf16[2,65,384]{2,1,0:T(8,128)(2,1)S(1)}, u32[]{:S(2)}, u32[]{:S(2)}) collective-permute-start(bf16[2,65,384]{2,1,0:T(8,128)(2,1)S(1)} %get-tuple-element.98), channel_id=1, source_target_pairs={{0,16},{1,17},{2,18},{3,19},{4,20},{5,21},{6,22},{7,23},{8,24},{9,... | collective-permute-start | bytes 299528 | tf_op jit(solution)/shard_map/ppermute | solution.py:654
  40.9 6.6 %collective-permute-start.12 = (bf16[2,65,384]{2,1,0:T(8,128)(2,1)S(1)}, bf16[2,65,384]{2,1,0:T(8,128)(2,1)S(1)}, u32[]{:S(2)}, u32[]{:S(2)}) collective-permute-start(bf16[2,65,384]{2,1,0:T(8,128)(2,1)S(1)} %get-tuple-element.104), channel_id=1, source_target_pairs={{16,0},{17,1},{18,2},{19,3},{20,4},{21,5},{22,6},{23,7},{24,8},{25... | collective-permute-start | bytes 299528 | tf_op jit(solution)/shard_map/ppermute | solution.py:691
  54.3 11.4 %collective-permute-start.19 = (bf16[400,384]{1,0:T(8,128)(2,1)S(1)}, bf16[400,384]{1,0:T(8,128)(2,1)S(1)}, u32[]{:S(2)}, u32[]{:S(2)}) collective-permute-start(bf16[400,384]{1,0:T(8,128)(2,1)S(1)} %get-tuple-element.132), channel_id=1, source_target_pairs={{0,4},{4,0},{8,12},{12,8},{1,5},{5,1},{9,13},{13,9},{2,6},{6,2},{1... | collective-permute-start | bytes 921608 | tf_op jit(solution)/shard_map/ppermute | solution.py:452
  54.7 9.5 %collective-permute-start.15 = (bf16[400,384]{1,0:T(8,128)(2,1)}, bf16[400,384]{1,0:T(8,128)(2,1)S(1)}, u32[]{:S(2)}, u32[]{:S(2)}) collective-permute-start(bf16[400,384]{1,0:T(8,128)(2,1)} %add_convert_fusion.1), channel_id=1, source_target_pairs={{0,8},{4,12},{8,0},{12,4},{1,9},{5,13},{9,1},{13,5},{2,10},{6,14},... | collective-permute-start | bytes 921608 | tf_op jit(solution)/shard_map/ppermute | solution.py:452
  64.2 8.2 %collective-permute-start.18 = (bf16[96,1536]{1,0:T(8,128)(2,1)S(1)}, bf16[96,1536]{1,0:T(8,128)(2,1)S(1)}, u32[]{:S(2)}, u32[]{:S(2)}) collective-permute-start(bf16[96,1536]{1,0:T(8,128)(2,1)S(1)} %add_convert_fusion.4), channel_id=1, source_target_pairs={{0,8},{4,12},{8,0},{12,4},{1,9},{5,13},{9,1},{13,5},{2,10},{6,14},... | collective-permute-start | bytes 884744 | tf_op jit(solution)/shard_map/ppermute | solution.py:452
  67.5 9.2 %collective-permute-start.14 = (bf16[96,1536]{1,0:T(8,128)(2,1)S(1)}, bf16[96,1536]{1,0:T(8,128)(2,1)S(1)}, u32[]{:S(2)}, u32[]{:S(2)}) collective-permute-start(bf16[96,1536]{1,0:T(8,128)(2,1)S(1)} %get-tuple-element.121), channel_id=1, source_target_pairs={{0,4},{4,0},{8,12},{12,8},{1,5},{5,1},{9,13},{13,9},{2,6},{6,2},{1... | collective-permute-start | bytes 884744 | tf_op jit(solution)/shard_map/ppermute | solution.py:452
  72.4 10.2 %collective-permute-start.21 = (bf16[96,1536]{1,0:T(8,128)(2,1)S(1)}, bf16[96,1536]{1,0:T(8,128)(2,1)S(1)}, u32[]{:S(2)}, u32[]{:S(2)}) collective-permute-start(bf16[96,1536]{1,0:T(8,128)(2,1)S(1)} %add_convert_fusion.3), channel_id=1, source_target_pairs={{0,8},{4,12},{8,0},{12,4},{1,9},{5,13},{9,1},{13,5},{2,10},{6,14},... | collective-permute-start | bytes 884744 | tf_op jit(solution)/shard_map/ppermute | solution.py:452
  74.0 8.6 %collective-permute-start.23 = (bf16[200,384]{1,0:T(8,128)(2,1)S(1)}, bf16[200,384]{1,0:T(8,128)(2,1)S(1)}, u32[]{:S(2)}, u32[]{:S(2)}) collective-permute-start(bf16[200,384]{1,0:T(8,128)(2,1)S(1)} %add_convert_fusion.5), channel_id=1, source_target_pairs={{0,2},{1,3},{2,0},{3,1},{4,6},{5,7},{6,4},{7,5},{8,10},{9,11},{10,... | collective-permute-start | bytes 460808 | tf_op jit(solution)/shard_map/ppermute | solution.py:452
  76.8 5.8 %collective-permute-start.22 = (bf16[48,1536]{1,0:T(8,128)(2,1)S(1)}, bf16[48,1536]{1,0:T(8,128)(2,1)S(1)}, u32[]{:S(2)}, u32[]{:S(2)}) collective-permute-start(bf16[48,1536]{1,0:T(8,128)(2,1)S(1)} %broadcast_select_fusion.3), channel_id=1, source_target_pairs={{0,1},{1,0},{2,3},{3,2},{4,5},{5,4},{6,7},{7,6},{8,9},{9,8},{10,11... | collective-permute-start | bytes 442376 | tf_op jit(solution)/shard_map/ppermute | solution.py:452
  82.7 13.4 %collective-permute-start.26 = (bf16[48,1536]{1,0:T(8,128)(2,1)S(1)}, bf16[48,1536]{1,0:T(8,128)(2,1)S(1)}, u32[]{:S(2)}, u32[]{:S(2)}) collective-permute-start(bf16[48,1536]{1,0:T(8,128)(2,1)S(1)} %add_convert_fusion.6), channel_id=1, source_target_pairs={{0,2},{1,3},{2,0},{3,1},{4,6},{5,7},{6,4},{7,5},{8,10},{9,11},{10,... | collective-permute-start | bytes 442376 | tf_op jit(solution)/shard_map/ppermute | solution.py:452
  84.0 7.7 %collective-permute-start.27 = (bf16[96,384]{1,0:T(8,128)(2,1)S(1)}, bf16[96,384]{1,0:T(8,128)(2,1)S(1)}, u32[]{:S(2)}, u32[]{:S(2)}) collective-permute-start(bf16[96,384]{1,0:T(8,128)(2,1)S(1)} %get-tuple-element.149), channel_id=1, source_target_pairs={{0,1},{1,0},{2,3},{3,2},{4,5},{5,4},{6,7},{7,6},{8,9},{9,8},{10,11... | collective-permute-start | bytes 221192 | tf_op jit(solution)/shard_map/ppermute | solution.py:452
  86.7 9.4 %collective-permute-start.28 = (bf16[96,384]{1,0:T(8,128)(2,1)S(1)}, bf16[96,384]{1,0:T(8,128)(2,1)S(1)}, u32[]{:S(2)}, u32[]{:S(2)}) collective-permute-start(bf16[96,384]{1,0:T(8,128)(2,1)S(1)} %get-tuple-element.150), channel_id=1, source_target_pairs={{0,2},{1,3},{2,0},{3,1},{4,6},{5,7},{6,4},{7,5},{8,10},{9,11},{10,... | collective-permute-start | bytes 221192 | tf_op jit(solution)/shard_map/ppermute | solution.py:452
  87.2 8.9 %collective-permute-start.29 = (bf16[96,384]{1,0:T(8,128)(2,1)S(1)}, bf16[96,384]{1,0:T(8,128)(2,1)S(1)}, u32[]{:S(2)}, u32[]{:S(2)}) collective-permute-start(bf16[96,384]{1,0:T(8,128)(2,1)S(1)} %get-tuple-element.151), channel_id=1, source_target_pairs={{0,3},{1,2},{2,1},{3,0},{4,7},{5,6},{6,5},{7,4},{8,11},{9,10},{10,... | collective-permute-start | bytes 221192 | tf_op jit(solution)/shard_map/ppermute | solution.py:452
  90.7 10.5 %collective-permute-start.24 = (bf16[200,384]{1,0:T(8,128)(2,1)S(1)}, bf16[200,384]{1,0:T(8,128)(2,1)S(1)}, u32[]{:S(2)}, u32[]{:S(2)}) collective-permute-start(bf16[200,384]{1,0:T(8,128)(2,1)S(1)} %reduce-precision_convert_fusion), channel_id=1, source_target_pairs={{0,1},{1,0},{2,3},{3,2},{4,5},{5,4},{6,7},{7,6},{8,9},{9,8},{10,11... | collective-permute-start | bytes 460808 | tf_op jit(solution)/shard_map/ppermute | solution.py:452
  96.1 7.1 %collective-permute-start.30 = (bf16[96,384]{1,0:T(8,128)(2,1)S(1)}, bf16[96,384]{1,0:T(8,128)(2,1)S(1)}, u32[]{:S(2)}, u32[]{:S(2)}) collective-permute-start(bf16[96,384]{1,0:T(8,128)(2,1)S(1)} %reduce-precision_convert_fusion.2), channel_id=1, source_target_pairs={{0,1},{1,0},{2,3},{3,2},{4,5},{5,4},{6,7},{7,6},{8,9},{9,8},{10,11... | collective-permute-start | bytes 221192 | tf_op jit(solution)/shard_map/ppermute | solution.py:452
  97.5 7.0 %collective-permute-start.31 = (bf16[96,384]{1,0:T(8,128)(2,1)S(1)}, bf16[96,384]{1,0:T(8,128)(2,1)S(1)}, u32[]{:S(2)}, u32[]{:S(2)}) collective-permute-start(bf16[96,384]{1,0:T(8,128)(2,1)S(1)} %reduce-precision_convert_fusion.2), channel_id=1, source_target_pairs={{0,2},{1,3},{2,0},{3,1},{4,6},{5,7},{6,4},{7,5},{8,10},{9,11},{10,... | collective-permute-start | bytes 221192 | tf_op jit(solution)/shard_map/ppermute | solution.py:452
  99.2 6.8 %collective-permute-start.32 = (bf16[96,384]{1,0:T(8,128)(2,1)S(1)}, bf16[96,384]{1,0:T(8,128)(2,1)S(1)}, u32[]{:S(2)}, u32[]{:S(2)}) collective-permute-start(bf16[96,384]{1,0:T(8,128)(2,1)S(1)} %reduce-precision_convert_fusion.2), channel_id=1, source_target_pairs={{0,3},{1,2},{2,1},{3,0},{4,7},{5,6},{6,5},{7,4},{8,11},{9,10},{10,... | collective-permute-start | bytes 221192 | tf_op jit(solution)/shard_map/ppermute | solution.py:452
  100.6 6.8 %collective-permute-start.33 = (bf16[48,1536]{1,0:T(8,128)(2,1)S(1)}, bf16[48,1536]{1,0:T(8,128)(2,1)S(1)}, u32[]{:S(2)}, u32[]{:S(2)}) collective-permute-start(bf16[48,1536]{1,0:T(8,128)(2,1)S(1)} %reduce-precision_convert_fusion.1), channel_id=1, source_target_pairs={{0,1},{1,0},{2,3},{3,2},{4,5},{5,4},{6,7},{7,6},{8,9},{9,8},{10,11... | collective-permute-start | bytes 442376 | tf_op jit(solution)/shard_map/ppermute | solution.py:452
  (14 other events, 88.4 us)

commit v6 on v5

--- a/solution.py
+++ b/solution.py
@@ -222,8 +222,11 @@
     arrive(copies[:3])
 
 
-def pick_kernel(info, images, rows_ref, unit_ref):
+def pick_kernel(info, images, mix_ref, rows_ref, unit_ref, own_ref, sem):
+    copy = pltpu.make_async_copy(mix_ref, own_ref, sem)
+    copy.start()
     unit_ref[...], _ = norm_parts(pad_images(picked_images(info, images), rows_ref))
+    copy.wait()
 
 
 def attend_kernel(shards, count, length, info, rows_ref, unit_ref, *refs):
@@ -519,7 +522,9 @@
     down_far, *leaving = together(far(leaving[0]), *leaving[1:])
     down = added(*kept[0], down_far)
 
-    up_far, down_near, rest = together(far(leaving[0]), swapped(other_half(down), axis, 1), leaving[1])
+    down_near = swapped(other_half(down), axis, 1)
+    rest = after(leaving[1], down_near)
+    up_far, down_near = after(far(leaving[0]), down_near), down_near
     up, down = added(*kept[1], up_far), added(own_half(down), down_near)
 
     rest_far, up_near, down_next = together(far(rest), swapped(other_half(up), axis, 1), swapped(down, axis, 2))
@@ -538,11 +543,10 @@
 
 def totals_over(grads, axes):
     scattered, axis = axes
-    leaving, kept = [], []
-    for pieces in grads:
-        one, terms = nearer_sums([after(piece, *leaving[:1]) for piece in pieces], scattered)
-        leaving.append(one)
-        kept.append(terms)
+    first, later = grads[0], grads[1:]
+    first_leaving, first_kept = nearer_sums(first, scattered)
+    first_leaving, *tied = together(first_leaving, *later)
+    leaving, kept = zip((first_leaving, first_kept), *(nearer_sums(pieces, scattered) for pieces in tied))
     if lax.axis_size(axis) == 4:
         return totals_over_line(leaving, kept, axes)
     last = lax.axis_size(scattered) // 2
@@ -617,10 +621,19 @@
         1,
         room=56 * 1024 * 1024,
     )
-    first_rows, first_unit = call(pick_kernel, "pick", info, (images,), (), (rows_wide, rows_wide), [], 1)
+    first_rows, first_unit, own_mix = call(
+        pick_kernel,
+        "pick",
+        info,
+        (images,),
+        (mix,),
+        (rows_wide, rows_wide, shape(mix.shape, BF)),
+        [pltpu.SemaphoreType.DMA(())],
+        1,
+    )
     farthest = shards // 2
     up_far = swapped(up_half, "fsdp", farthest)
-    mix_pieces = gather_pieces(mix, "fsdp", up_far, first_rows)
+    mix_pieces = [own_mix, *gather_pieces(mix, "fsdp", up_far, first_rows)[1:]]
     up_other = swapped(after(up_far, mix_pieces[-1]), "dp", 1)
     up_near = gather_nearer([up_weight[0]], "fsdp")
     up_halves = (gather_nearer([one], "fsdp") for one in (up_far, up_other))

time: 109 us -> 106 us (0.972)
  waiting for transfers between devices: 44.3 us -> 42.1 us
    ppermute x32, waiting for transfers between devices: 37.1 us -> 34.9 us  [swapped(): lax.ppermute(block, axis, [(i, i ^ bit) for i in range(lax.axis_size(axis...]
  transfers between devices with their start and end apart: 34 -> 34, of which waited for: 15 -> 18; matrix products, arithmetic and copies ran while one was open for 8% -> 8% of each run, Pallas kernels for 4% -> 4%
where the time goes in v6:
time: 106 us
  waiting for transfers between devices  42.1 us (40%)
  starting transfers between devices  35.4 us (33%)
  Pallas kernels  16.6 us (16%)
  other arithmetic  6.46 us (6%)
  local copies, waits for them, and re-layouts  4.59 us (4%)
    ppermute x32, waiting for transfers between devices, swapped(): lax.ppermute(block, axis, [(i, i ^ bit) for i in range(lax.axis_size(axis...  34.9 us
    ppermute x32, starting transfers between devices, swapped(): lax.ppermute(block, axis, [(i, i ^ bit) for i in range(lax.axis_size(axis...  30.9 us
    pallas_call x8, Pallas kernels, call(): pl.pallas_call(lambda *refs: kernel(*refs[:used], *refs[used + len(earlie...  16.6 us
    ppermute x1, waiting for transfers between devices, local(): returned = lax.ppermute(sent, 'section', [(1, 0)])  5.16 us
    unnamed x12, local copies, waits for them, and re-layouts  3.41 us
    ppermute x1, starting transfers between devices, local(): arrived = lax.ppermute(first_out, 'section', [(0, 1)])  2.99 us
    convert_element_type x7, other arithmetic, added(): return sum((term.astype(F32) for term in terms)).astype(BF)  2.28 us
  transfers between devices with their start and end apart: 34, of which 18 were waited for; matrix products, arithmetic and copies ran while one was open for 8% of the time, Pallas kernels for 4%

profile of v6, /device:TPU:0, one launch (start us, length us, event | category | flops | bytes accessed | tf_op | source)
XLA Modules:
  0.0 106.0 jit_solution(7656241093391393791)
XLA Ops:
  0.7 2.0 %pack.1 = (bf16[112,1536]{1,0:T(8,128)(2,1)}, bf16[96,768]{1,0:T(8,128)(2,1)}) custom-call(s32[1]{0:T(128)} %bitcast.3.refs_0_, bf16[96,1152]{1,0:T(8,128)(2,1)} %bitcast.33, bf16[96,384]{1,0:T(8,128)(2,1)} %bitcast.34, bf16[96,1536]{1,0:T(8,128)(2,1)} %bitcast.25, bf16[1,96]{1,0:T(2,128)(2,1)} %refs_4_.1, bf16[1,96]{1,0:T(2,128)(2,1)} %refs_5_.1, ...), custom_call_target="tpu_custom_call" | custom-call | flops 1 | bytes 1083648 | tf_op jit(solution)/shard_map/pack/pallas_call | solution.py:438
  2.7 3.0 %collective-permute-start.1 = (bf16[112,1536]{1,0:T(8,128)(2,1)}, bf16[112,1536]{1,0:T(8,128)(2,1)S(1)}, u32[]{:S(2)}, u32[]{:S(2)}) collective-permute-start(bf16[112,1536]{1,0:T(8,128)(2,1)} %get-tuple-element.88.refs_2_), channel_id=1, source_target_pairs={{0,8},{4,12},{8,0},{12,4},{1,9},{5,13},{9,1},{13,5},{2,10},{6,14},... | collective-permute-start | bytes 1032200 | tf_op jit(solution)/shard_map/ppermute | solution.py:455
  9.3 7.8 %collective-permute-done.2.refs_7_ = bf16[96,768]{1,0:T(8,128)(2,1)S(1)} collective-permute-done((bf16[96,768]{1,0:T(8,128)(2,1)}, bf16[96,768]{1,0:T(8,128)(2,1)S(1)}, u32[]{:S(2)}, u32[]{:S(2)}) %collective-permute-start.2) | collective-permute-done | bytes 147488 | tf_op jit(solution)/shard_map/ppermute | solution.py:455
  17.6 1.7 %collective-permute-start.9 = (bf16[384,384]{1,0:T(8,128)(2,1)S(1)}, bf16[384,384]{1,0:T(8,128)(2,1)S(1)}, u32[]{:S(2)}, u32[]{:S(2)}) collective-permute-start(bf16[384,384]{1,0:T(8,128)(2,1)S(1)} %bitcast.28), channel_id=1, source_target_pairs={{0,8},{4,12},{8,0},{12,4},{1,9},{5,13},{9,1},{13,5},{2,10},{6,14},... | collective-permute-start | bytes 884744 | tf_op jit(solution)/shard_map/ppermute | solution.py:455
  21.5 2.4 %attend.1 = (f32[160,384]{1,0:T(8,128)S(1)}, bf16[160,384]{1,0:T(8,128)(2,1)S(1)}, bf16[384,1152]{1,0:T(8,128)(2,1)S(1)}, bf16[384,384]{1,0:T(8,128)(2,1)S(1)}, ...) custom-call(s32[5]{0:T(128)S(1)} %pad_add_fusion.refs_0_, f32[160,384]{1,0:T(8,128)S(1)} %get-tuple-element.89.refs_1_, ...), custom_call_target="tpu_custom_call" | custom-call | flops 188743680 | bytes 3434496 | tf_op jit(solution)/shard_map/attend/pallas_call | solution.py:438
  23.9 2.7 %collective-permute-done.9.refs_13_ = bf16[384,384]{1,0:T(8,128)(2,1)S(1)} collective-permute-done((bf16[384,384]{1,0:T(8,128)(2,1)S(1)}, bf16[384,384]{1,0:T(8,128)(2,1)S(1)}, u32[]{:S(2)}, u32[]{:S(2)}) %collective-permute-start.9) | collective-permute-done | bytes 294944 | tf_op jit(solution)/shard_map/ppermute | solution.py:455
  28.6 1.8 %feed_forward.1 = (bf16[2,65,384]{2,1,0:T(8,128)(2,1)S(1)}, bf16[384,1536]{1,0:T(8,128)(2,1)S(1)}, bf16[1536,384]{1,0:T(8,128)(2,1)S(1)}) custom-call(s32[5]{0:T(128)S(1)} %pad_add_fusion.refs_0_, bf16[160,384]{1,0:T(8,128)(2,1)S(1)} %get-tuple-element.94.refs_1_, f32[160,384]{1,0:T(8,128)S(1)} %get-tuple-element.95.refs_2_, ...), custom_call_target="tpu_custom_call" | custom-call | flops 377487360 | bytes 5205504 | tf_op jit(solution)/shard_map/feed_forward/pallas_call | solution.py:438
  30.4 3.0 %collective-permute-start.11 = (bf16[2,65,384]{2,1,0:T(8,128)(2,1)S(1)}, bf16[2,65,384]{2,1,0:T(8,128)(2,1)S(1)}, u32[]{:S(2)}, u32[]{:S(2)}) collective-permute-start(bf16[2,65,384]{2,1,0:T(8,128)(2,1)S(1)} %get-tuple-element.100), channel_id=1, source_target_pairs={{0,16},{1,17},{2,18},{3,19},{4,20},{5,21},{6,22},{7,23},{8,24},{9,... | collective-permute-start | bytes 299528 | tf_op jit(solution)/shard_map/ppermute | solution.py:667
  34.0 2.0 %collective-permute-done.11.refs_2_ = bf16[2,65,384]{2,1,0:T(8,128)(2,1)S(1)} collective-permute-done((bf16[2,65,384]{2,1,0:T(8,128)(2,1)S(1)}, bf16[2,65,384]{2,1,0:T(8,128)(2,1)S(1)}, u32[]{:S(2)}, u32[]{:S(2)}) %collective-permute-start.11) | collective-permute-done | bytes 99872 | tf_op jit(solution)/shard_map/ppermute | solution.py:667
  36.0 4.7 %both_ways.1 = (bf16[2,65,384]{2,1,0:T(8,128)(2,1)S(1)}, bf16[2,65,384]{2,1,0:T(8,128)(2,1)S(1)}, bf16[160,1152]{1,0:T(8,128)(2,1)S(1)}, f32[960,80]{1,0:T(8,128...) custom-call(s32[5]{0:T(128)S(1)} %pad_add_fusion.refs_0_, ...), custom_call_target="tpu_custom_call" | custom-call | flops 1132462080 | bytes 8197376 | tf_op jit(solution)/shard_map/both_ways/pallas_call | solution.py:438
  42.2 5.2 %collective-permute-done.12.refs_1_ = bf16[2,65,384]{2,1,0:T(8,128)(2,1)S(1)} collective-permute-done((bf16[2,65,384]{2,1,0:T(8,128)(2,1)S(1)}, bf16[2,65,384]{2,1,0:T(8,128)(2,1)S(1)}, u32[]{:S(2)}, u32[]{:S(2)}) %collective-permute-start.12) | collective-permute-done | bytes 99872 | tf_op jit(solution)/shard_map/ppermute | solution.py:704
  47.3 4.1 %rest_grad.1 = (bf16[400,384]{1,0:T(8,128)(2,1)S(1)}, bf16[400,384]{1,0:T(8,128)(2,1)S(1)}, bf16[400,384]{1,0:T(8,128)(2,1)S(1)}, bf16[400,384]{1,0:T(8,128)(2,1...) custom-call(s32[5]{0:T(128)S(1)} %pad_add_fusion.refs_0_, ...), custom_call_target="tpu_custom_call" | custom-call | flops 1132462080 | bytes 10550528 | tf_op jit(solution)/shard_map/rest_grad/pallas_call | solution.py:438
  57.6 6.4 %collective-permute-done.15 = bf16[400,384]{1,0:T(8,128)(2,1)S(1)} collective-permute-done((bf16[400,384]{1,0:T(8,128)(2,1)}, bf16[400,384]{1,0:T(8,128)(2,1)S(1)}, u32[]{:S(2)}, u32[]{:S(2)}) %collective-permute-start.15) | collective-permute-done | bytes 307232 | tf_op jit(solution)/shard_map/ppermute | solution.py:455
  64.1 1.6 %collective-permute-start.20 = (bf16[200,384]{1,0:T(8,128)(2,1)S(1)}, bf16[200,384]{1,0:T(8,128)(2,1)S(1)}, u32[]{:S(2)}, u32[]{:S(2)}) collective-permute-start(bf16[200,384]{1,0:T(8,128)(2,1)S(1)} %broadcast_select_fusion.2), channel_id=1, source_target_pairs={{0,1},{1,0},{2,3},{3,2},{4,5},{5,4},{6,7},{7,6},{8,9},{9,8},{10,11... | collective-permute-start | bytes 460808 | tf_op jit(solution)/shard_map/ppermute | solution.py:455
  67.3 2.1 %collective-permute-done.20 = bf16[200,384]{1,0:T(8,128)(2,1)S(1)} collective-permute-done((bf16[200,384]{1,0:T(8,128)(2,1)S(1)}, bf16[200,384]{1,0:T(8,128)(2,1)S(1)}, u32[]{:S(2)}, u32[]{:S(2)}) %collective-permute-start.20) | collective-permute-done | bytes 153632 | tf_op jit(solution)/shard_map/ppermute | solution.py:455
  71.0 2.6 %collective-permute-start.23 = (bf16[200,384]{1,0:T(8,128)(2,1)S(1)}, bf16[200,384]{1,0:T(8,128)(2,1)S(1)}, u32[]{:S(2)}, u32[]{:S(2)}) collective-permute-start(bf16[200,384]{1,0:T(8,128)(2,1)S(1)} %add_convert_fusion.5), channel_id=1, source_target_pairs={{0,2},{1,3},{2,0},{3,1},{4,6},{5,7},{6,4},{7,5},{8,10},{9,11},{10,... | collective-permute-start | bytes 460808 | tf_op jit(solution)/shard_map/ppermute | solution.py:455
  73.6 2.1 %collective-permute-done.18 = bf16[96,1536]{1,0:T(8,128)(2,1)S(1)} collective-permute-done((bf16[96,1536]{1,0:T(8,128)(2,1)S(1)}, bf16[96,1536]{1,0:T(8,128)(2,1)S(1)}, u32[]{:S(2)}, u32[]{:S(2)}) %collective-permute-start.18) | collective-permute-done | bytes 294944 | tf_op jit(solution)/shard_map/ppermute | solution.py:455
  76.4 2.0 %collective-permute-done.23 = bf16[200,384]{1,0:T(8,128)(2,1)S(1)} collective-permute-done((bf16[200,384]{1,0:T(8,128)(2,1)S(1)}, bf16[200,384]{1,0:T(8,128)(2,1)S(1)}, u32[]{:S(2)}, u32[]{:S(2)}) %collective-permute-start.23) | collective-permute-done | bytes 153632 | tf_op jit(solution)/shard_map/ppermute | solution.py:455
  78.4 2.6 %collective-permute-done.22 = bf16[48,1536]{1,0:T(8,128)(2,1)S(1)} collective-permute-done((bf16[48,1536]{1,0:T(8,128)(2,1)S(1)}, bf16[48,1536]{1,0:T(8,128)(2,1)S(1)}, u32[]{:S(2)}, u32[]{:S(2)}) %collective-permute-start.22) | collective-permute-done | bytes 147488 | tf_op jit(solution)/shard_map/ppermute | solution.py:455
  81.2 3.8 %collective-permute-start.26 = (bf16[48,1536]{1,0:T(8,128)(2,1)S(1)}, bf16[48,1536]{1,0:T(8,128)(2,1)S(1)}, u32[]{:S(2)}, u32[]{:S(2)}) collective-permute-start(bf16[48,1536]{1,0:T(8,128)(2,1)S(1)} %add_convert_fusion.6), channel_id=1, source_target_pairs={{0,2},{1,3},{2,0},{3,1},{4,6},{5,7},{6,4},{7,5},{8,10},{9,11},{10,... | collective-permute-start | bytes 442376 | tf_op jit(solution)/shard_map/ppermute | solution.py:455
  85.2 4.3 %collective-permute-start.29 = (bf16[96,384]{1,0:T(8,128)(2,1)S(1)}, bf16[96,384]{1,0:T(8,128)(2,1)S(1)}, u32[]{:S(2)}, u32[]{:S(2)}) collective-permute-start(bf16[96,384]{1,0:T(8,128)(2,1)S(1)} %get-tuple-element.153), channel_id=1, source_target_pairs={{0,3},{1,2},{2,1},{3,0},{4,7},{5,6},{6,5},{7,4},{8,11},{9,10},{10,... | collective-permute-start | bytes 221192 | tf_op jit(solution)/shard_map/ppermute | solution.py:455
  91.8 2.2 %collective-permute-done.28 = bf16[96,384]{1,0:T(8,128)(2,1)S(1)} collective-permute-done((bf16[96,384]{1,0:T(8,128)(2,1)S(1)}, bf16[96,384]{1,0:T(8,128)(2,1)S(1)}, u32[]{:S(2)}, u32[]{:S(2)}) %collective-permute-start.28) | collective-permute-done | bytes 73760 | tf_op jit(solution)/shard_map/ppermute | solution.py:455
  95.4 2.0 %collective-permute-start.31 = (bf16[96,384]{1,0:T(8,128)(2,1)S(1)}, bf16[96,384]{1,0:T(8,128)(2,1)S(1)}, u32[]{:S(2)}, u32[]{:S(2)}) collective-permute-start(bf16[96,384]{1,0:T(8,128)(2,1)S(1)} %reduce-precision_convert_fusion.2), channel_id=1, source_target_pairs={{0,2},{1,3},{2,0},{3,1},{4,6},{5,7},{6,4},{7,5},{8,10},{9,11},{10,... | collective-permute-start | bytes 221192 | tf_op jit(solution)/shard_map/ppermute | solution.py:455
  101.7 2.0 %collective-permute-done.32 = bf16[96,384]{1,0:T(8,128)(2,1)S(1)} collective-permute-done((bf16[96,384]{1,0:T(8,128)(2,1)S(1)}, bf16[96,384]{1,0:T(8,128)(2,1)S(1)}, u32[]{:S(2)}, u32[]{:S(2)}) %collective-permute-start.32) | collective-permute-done | bytes 73760 | tf_op jit(solution)/shard_map/ppermute | solution.py:455
  (87 shorter events, 30.9 us)
Async XLA Ops:
  2.7 14.4 %collective-permute-start.1 = (bf16[112,1536]{1,0:T(8,128)(2,1)}, bf16[112,1536]{1,0:T(8,128)(2,1)S(1)}, u32[]{:S(2)}, u32[]{:S(2)}) collective-permute-start(bf16[112,1536]{1,0:T(8,128)(2,1)} %get-tuple-element.88.refs_2_), channel_id=1, source_target_pairs={{0,8},{4,12},{8,0},{12,4},{1,9},{5,13},{9,1},{13,5},{2,10},{6,14},... | collective-permute-start | bytes 1032200 | tf_op jit(solution)/shard_map/ppermute | solution.py:455
  5.7 11.4 %collective-permute-start.2 = (bf16[96,768]{1,0:T(8,128)(2,1)}, bf16[96,768]{1,0:T(8,128)(2,1)S(1)}, u32[]{:S(2)}, u32[]{:S(2)}) collective-permute-start(bf16[96,768]{1,0:T(8,128)(2,1)} %get-tuple-element.92), channel_id=1, source_target_pairs={{0,8},{4,12},{8,0},{12,4},{1,9},{5,13},{9,1},{13,5},{2,10},{6,14},... | collective-permute-start | bytes 442376 | tf_op jit(solution)/shard_map/ppermute | solution.py:455
  17.6 8.9 %collective-permute-start.9 = (bf16[384,384]{1,0:T(8,128)(2,1)S(1)}, bf16[384,384]{1,0:T(8,128)(2,1)S(1)}, u32[]{:S(2)}, u32[]{:S(2)}) collective-permute-start(bf16[384,384]{1,0:T(8,128)(2,1)S(1)} %bitcast.28), channel_id=1, source_target_pairs={{0,8},{4,12},{8,0},{12,4},{1,9},{5,13},{9,1},{13,5},{2,10},{6,14},... | collective-permute-start | bytes 884744 | tf_op jit(solution)/shard_map/ppermute | solution.py:455
  19.4 7.7 %collective-permute-start.4 = (bf16[96,1536]{1,0:T(8,128)(2,1)S(1)}, bf16[96,1536]{1,0:T(8,128)(2,1)S(1)}, u32[]{:S(2)}, u32[]{:S(2)}) collective-permute-start(bf16[96,1536]{1,0:T(8,128)(2,1)S(1)} %bitcast.26), channel_id=1, source_target_pairs={{0,4},{4,0},{8,12},{12,8},{1,5},{5,1},{9,13},{13,9},{2,6},{6,2},{1... | collective-permute-start | bytes 884744 | tf_op jit(solution)/shard_map/ppermute | solution.py:455
  19.4 9.0 %collective-permute-start.8 = (bf16[384,384]{1,0:T(8,128)(2,1)S(1)}, bf16[384,384]{1,0:T(8,128)(2,1)S(1)}, u32[]{:S(2)}, u32[]{:S(2)}) collective-permute-start(bf16[384,384]{1,0:T(8,128)(2,1)S(1)} %bitcast.29), channel_id=1, source_target_pairs={{0,4},{4,0},{8,12},{12,8},{1,5},{5,1},{9,13},{13,9},{2,6},{6,2},{1... | collective-permute-start | bytes 884744 | tf_op jit(solution)/shard_map/ppermute | solution.py:455
  19.9 7.2 %collective-permute-start.5 = (bf16[96,768]{1,0:T(8,128)(2,1)S(1)}, bf16[96,768]{1,0:T(8,128)(2,1)S(1)}, u32[]{:S(2)}, u32[]{:S(2)}) collective-permute-start(bf16[96,768]{1,0:T(8,128)(2,1)S(1)} %collective-permute-done.2.refs_7_), channel_id=1, source_target_pairs={{0,1},{1,0},{2,3},{3,2},{4,5},{5,4},{6,7},{7,6},{8,9},{9,8},{10,11... | collective-permute-start | bytes 442376 | tf_op jit(solution)/shard_map/ppermute | solution.py:455
  30.4 5.6 %collective-permute-start.11 = (bf16[2,65,384]{2,1,0:T(8,128)(2,1)S(1)}, bf16[2,65,384]{2,1,0:T(8,128)(2,1)S(1)}, u32[]{:S(2)}, u32[]{:S(2)}) collective-permute-start(bf16[2,65,384]{2,1,0:T(8,128)(2,1)S(1)} %get-tuple-element.100), channel_id=1, source_target_pairs={{0,16},{1,17},{2,18},{3,19},{4,20},{5,21},{6,22},{7,23},{8,24},{9,... | collective-permute-start | bytes 299528 | tf_op jit(solution)/shard_map/ppermute | solution.py:667
  40.7 6.6 %collective-permute-start.12 = (bf16[2,65,384]{2,1,0:T(8,128)(2,1)S(1)}, bf16[2,65,384]{2,1,0:T(8,128)(2,1)S(1)}, u32[]{:S(2)}, u32[]{:S(2)}) collective-permute-start(bf16[2,65,384]{2,1,0:T(8,128)(2,1)S(1)} %get-tuple-element.106), channel_id=1, source_target_pairs={{16,0},{17,1},{18,2},{19,3},{20,4},{21,5},{22,6},{23,7},{24,8},{25... | collective-permute-start | bytes 299528 | tf_op jit(solution)/shard_map/ppermute | solution.py:704
  54.1 9.9 %collective-permute-start.19 = (bf16[400,384]{1,0:T(8,128)(2,1)S(1)}, bf16[400,384]{1,0:T(8,128)(2,1)S(1)}, u32[]{:S(2)}, u32[]{:S(2)}) collective-permute-start(bf16[400,384]{1,0:T(8,128)(2,1)S(1)} %get-tuple-element.137), channel_id=1, source_target_pairs={{0,4},{4,0},{8,12},{12,8},{1,5},{5,1},{9,13},{13,9},{2,6},{6,2},{1... | collective-permute-start | bytes 921608 | tf_op jit(solution)/shard_map/ppermute | solution.py:455
  54.5 9.5 %collective-permute-start.15 = (bf16[400,384]{1,0:T(8,128)(2,1)}, bf16[400,384]{1,0:T(8,128)(2,1)S(1)}, u32[]{:S(2)}, u32[]{:S(2)}) collective-permute-start(bf16[400,384]{1,0:T(8,128)(2,1)} %add_convert_fusion.1), channel_id=1, source_target_pairs={{0,8},{4,12},{8,0},{12,4},{1,9},{5,13},{9,1},{13,5},{2,10},{6,14},... | collective-permute-start | bytes 921608 | tf_op jit(solution)/shard_map/ppermute | solution.py:455
  65.8 9.9 %collective-permute-start.18 = (bf16[96,1536]{1,0:T(8,128)(2,1)S(1)}, bf16[96,1536]{1,0:T(8,128)(2,1)S(1)}, u32[]{:S(2)}, u32[]{:S(2)}) collective-permute-start(bf16[96,1536]{1,0:T(8,128)(2,1)S(1)} %add_convert_fusion.4), channel_id=1, source_target_pairs={{0,8},{4,12},{8,0},{12,4},{1,9},{5,13},{9,1},{13,5},{2,10},{6,14},... | collective-permute-start | bytes 884744 | tf_op jit(solution)/shard_map/ppermute | solution.py:455
  67.3 8.5 %collective-permute-start.14 = (bf16[96,1536]{1,0:T(8,128)(2,1)S(1)}, bf16[96,1536]{1,0:T(8,128)(2,1)S(1)}, u32[]{:S(2)}, u32[]{:S(2)}) collective-permute-start(bf16[96,1536]{1,0:T(8,128)(2,1)S(1)} %get-tuple-element.129), channel_id=1, source_target_pairs={{0,4},{4,0},{8,12},{12,8},{1,5},{5,1},{9,13},{13,9},{2,6},{6,2},{1... | collective-permute-start | bytes 884744 | tf_op jit(solution)/shard_map/ppermute | solution.py:455
  69.4 11.7 %collective-permute-start.21 = (bf16[96,1536]{1,0:T(8,128)(2,1)S(1)}, bf16[96,1536]{1,0:T(8,128)(2,1)S(1)}, u32[]{:S(2)}, u32[]{:S(2)}) collective-permute-start(bf16[96,1536]{1,0:T(8,128)(2,1)S(1)} %add_convert_fusion.3), channel_id=1, source_target_pairs={{0,8},{4,12},{8,0},{12,4},{1,9},{5,13},{9,1},{13,5},{2,10},{6,14},... | collective-permute-start | bytes 884744 | tf_op jit(solution)/shard_map/ppermute | solution.py:455
  71.0 7.5 %collective-permute-start.23 = (bf16[200,384]{1,0:T(8,128)(2,1)S(1)}, bf16[200,384]{1,0:T(8,128)(2,1)S(1)}, u32[]{:S(2)}, u32[]{:S(2)}) collective-permute-start(bf16[200,384]{1,0:T(8,128)(2,1)S(1)} %add_convert_fusion.5), channel_id=1, source_target_pairs={{0,2},{1,3},{2,0},{3,1},{4,6},{5,7},{6,4},{7,5},{8,10},{9,11},{10,... | collective-permute-start | bytes 460808 | tf_op jit(solution)/shard_map/ppermute | solution.py:455
  76.4 8.5 %collective-permute-start.25 = (bf16[96,1536]{1,0:T(8,128)(2,1)S(1)}, bf16[96,1536]{1,0:T(8,128)(2,1)S(1)}, u32[]{:S(2)}, u32[]{:S(2)}) collective-permute-start(bf16[96,1536]{1,0:T(8,128)(2,1)S(1)} %get-tuple-element.148), channel_id=1, source_target_pairs={{0,4},{4,0},{8,12},{12,8},{1,5},{5,1},{9,13},{13,9},{2,6},{6,2},{1... | collective-permute-start | bytes 884744 | tf_op jit(solution)/shard_map/ppermute | solution.py:455
  81.2 12.9 %collective-permute-start.26 = (bf16[48,1536]{1,0:T(8,128)(2,1)S(1)}, bf16[48,1536]{1,0:T(8,128)(2,1)S(1)}, u32[]{:S(2)}, u32[]{:S(2)}) collective-permute-start(bf16[48,1536]{1,0:T(8,128)(2,1)S(1)} %add_convert_fusion.6), channel_id=1, source_target_pairs={{0,2},{1,3},{2,0},{3,1},{4,6},{5,7},{6,4},{7,5},{8,10},{9,11},{10,... | collective-permute-start | bytes 442376 | tf_op jit(solution)/shard_map/ppermute | solution.py:455
  85.0 6.8 %collective-permute-start.27 = (bf16[96,384]{1,0:T(8,128)(2,1)S(1)}, bf16[96,384]{1,0:T(8,128)(2,1)S(1)}, u32[]{:S(2)}, u32[]{:S(2)}) collective-permute-start(bf16[96,384]{1,0:T(8,128)(2,1)S(1)} %get-tuple-element.151), channel_id=1, source_target_pairs={{0,1},{1,0},{2,3},{3,2},{4,5},{5,4},{6,7},{7,6},{8,9},{9,8},{10,11... | collective-permute-start | bytes 221192 | tf_op jit(solution)/shard_map/ppermute | solution.py:455
  85.1 8.9 %collective-permute-start.28 = (bf16[96,384]{1,0:T(8,128)(2,1)S(1)}, bf16[96,384]{1,0:T(8,128)(2,1)S(1)}, u32[]{:S(2)}, u32[]{:S(2)}) collective-permute-start(bf16[96,384]{1,0:T(8,128)(2,1)S(1)} %get-tuple-element.152), channel_id=1, source_target_pairs={{0,2},{1,3},{2,0},{3,1},{4,6},{5,7},{6,4},{7,5},{8,10},{9,11},{10,... | collective-permute-start | bytes 221192 | tf_op jit(solution)/shard_map/ppermute | solution.py:455
  85.2 8.8 %collective-permute-start.29 = (bf16[96,384]{1,0:T(8,128)(2,1)S(1)}, bf16[96,384]{1,0:T(8,128)(2,1)S(1)}, u32[]{:S(2)}, u32[]{:S(2)}) collective-permute-start(bf16[96,384]{1,0:T(8,128)(2,1)S(1)} %get-tuple-element.153), channel_id=1, source_target_pairs={{0,3},{1,2},{2,1},{3,0},{4,7},{5,6},{6,5},{7,4},{8,11},{9,10},{10,... | collective-permute-start | bytes 221192 | tf_op jit(solution)/shard_map/ppermute | solution.py:455
  91.0 8.3 %collective-permute-start.24 = (bf16[200,384]{1,0:T(8,128)(2,1)S(1)}, bf16[200,384]{1,0:T(8,128)(2,1)S(1)}, u32[]{:S(2)}, u32[]{:S(2)}) collective-permute-start(bf16[200,384]{1,0:T(8,128)(2,1)S(1)} %reduce-precision_convert_fusion), channel_id=1, source_target_pairs={{0,1},{1,0},{2,3},{3,2},{4,5},{5,4},{6,7},{7,6},{8,9},{9,8},{10,11... | collective-permute-start | bytes 460808 | tf_op jit(solution)/shard_map/ppermute | solution.py:455
  94.1 7.6 %collective-permute-start.30 = (bf16[96,384]{1,0:T(8,128)(2,1)S(1)}, bf16[96,384]{1,0:T(8,128)(2,1)S(1)}, u32[]{:S(2)}, u32[]{:S(2)}) collective-permute-start(bf16[96,384]{1,0:T(8,128)(2,1)S(1)} %reduce-precision_convert_fusion.2), channel_id=1, source_target_pairs={{0,1},{1,0},{2,3},{3,2},{4,5},{5,4},{6,7},{7,6},{8,9},{9,8},{10,11... | collective-permute-start | bytes 221192 | tf_op jit(solution)/shard_map/ppermute | solution.py:455
  95.4 6.2 %collective-permute-start.31 = (bf16[96,384]{1,0:T(8,128)(2,1)S(1)}, bf16[96,384]{1,0:T(8,128)(2,1)S(1)}, u32[]{:S(2)}, u32[]{:S(2)}) collective-permute-start(bf16[96,384]{1,0:T(8,128)(2,1)S(1)} %reduce-precision_convert_fusion.2), channel_id=1, source_target_pairs={{0,2},{1,3},{2,0},{3,1},{4,6},{5,7},{6,4},{7,5},{8,10},{9,11},{10,... | collective-permute-start | bytes 221192 | tf_op jit(solution)/shard_map/ppermute | solution.py:455
  97.4 6.3 %collective-permute-start.32 = (bf16[96,384]{1,0:T(8,128)(2,1)S(1)}, bf16[96,384]{1,0:T(8,128)(2,1)S(1)}, u32[]{:S(2)}, u32[]{:S(2)}) collective-permute-start(bf16[96,384]{1,0:T(8,128)(2,1)S(1)} %reduce-precision_convert_fusion.2), channel_id=1, source_target_pairs={{0,3},{1,2},{2,1},{3,0},{4,7},{5,6},{6,5},{7,4},{8,11},{9,10},{10,... | collective-permute-start | bytes 221192 | tf_op jit(solution)/shard_map/ppermute | solution.py:455
  98.6 6.6 %collective-permute-start.33 = (bf16[48,1536]{1,0:T(8,128)(2,1)S(1)}, bf16[48,1536]{1,0:T(8,128)(2,1)S(1)}, u32[]{:S(2)}, u32[]{:S(2)}) collective-permute-start(bf16[48,1536]{1,0:T(8,128)(2,1)S(1)} %reduce-precision_convert_fusion.1), channel_id=1, source_target_pairs={{0,1},{1,0},{2,3},{3,2},{4,5},{5,4},{6,7},{7,6},{8,9},{9,8},{10,11... | collective-permute-start | bytes 442376 | tf_op jit(solution)/shard_map/ppermute | solution.py:455
  (14 other events, 69.7 us)

commit v7 on v6

--- a/solution.py
+++ b/solution.py
@@ -636,7 +636,7 @@
     mix_pieces = [own_mix, *gather_pieces(mix, "fsdp", up_far, first_rows)[1:]]
     up_other = swapped(after(up_far, mix_pieces[-1]), "dp", 1)
     up_near = gather_nearer([up_weight[0]], "fsdp")
-    up_halves = (gather_nearer([one], "fsdp") for one in (up_far, up_other))
+    up_halves = [gather_nearer([one], "fsdp") for one in (up_far, up_other)]
 
     middle, mid, heads, merge, small, wide_bias = call(
         functools.partial(attend_kernel, shards, count, length),
@@ -653,7 +653,7 @@
         ],
         work * (wide + width),
     )
-    down_pieces = gather_pieces(down_weight[0], "fsdp", mid)
+    down_pieces = gather_pieces(down_weight[0], "fsdp", mid, *(one for two in up_halves for one in two))
     first_out, up, down = call(
         bind(feed_forward_kernel),
         "feed_forward",

time: 106 us -> 106 us (level)
  starting transfers between devices: 35.4 us -> 34.2 us
  waiting for transfers between devices: 42.1 us -> 43.3 us
    ppermute x1, starting transfers between devices: 2.99 us -> 1.55 us  [local(): arrived = lax.ppermute(first_out, 'section', [(0, 1)])]
  transfers between devices with their start and end apart: 34 -> 34, of which waited for: 18 -> 17; matrix products, arithmetic and copies ran while one was open for 8% -> 8% of each run, Pallas kernels for 4% -> 4%
where the time goes in v7:
time: 106 us
  waiting for transfers between devices  43.3 us (41%)
  starting transfers between devices  34.2 us (32%)
  Pallas kernels  16.6 us (16%)
  other arithmetic  6.46 us (6%)
  local copies, waits for them, and re-layouts  4.59 us (4%)
    ppermute x32, waiting for transfers between devices, swapped(): lax.ppermute(block, axis, [(i, i ^ bit) for i in range(lax.axis_size(axis...  35.8 us
    ppermute x32, starting transfers between devices, swapped(): lax.ppermute(block, axis, [(i, i ^ bit) for i in range(lax.axis_size(axis...  31.2 us
    pallas_call x8, Pallas kernels, call(): pl.pallas_call(lambda *refs: kernel(*refs[:used], *refs[used + len(earlie...  16.6 us
    ppermute x1, waiting for transfers between devices, local(): returned = lax.ppermute(sent, 'section', [(1, 0)])  5.16 us
    unnamed x12, local copies, waits for them, and re-layouts  3.41 us
    ppermute x1, waiting for transfers between devices, local(): arrived = lax.ppermute(first_out, 'section', [(0, 1)])  2.29 us
    convert_element_type x7, other arithmetic, added(): return sum((term.astype(F32) for term in terms)).astype(BF)  2.28 us
  transfers between devices with their start and end apart: 34, of which 17 were waited for; matrix products, arithmetic and copies ran while one was open for 8% of the time, Pallas kernels for 4%

profile of v7, /device:TPU:0, one launch (start us, length us, event | category | flops | bytes accessed | tf_op | source)
XLA Modules:
  0.0 106.0 jit_solution(2035985409687797861)
XLA Ops:
  0.7 2.0 %pack.1 = (bf16[112,1536]{1,0:T(8,128)(2,1)}, bf16[96,768]{1,0:T(8,128)(2,1)}) custom-call(s32[1]{0:T(128)} %bitcast.3.refs_0_, bf16[96,1152]{1,0:T(8,128)(2,1)} %bitcast.33, bf16[96,384]{1,0:T(8,128)(2,1)} %bitcast.34, bf16[96,1536]{1,0:T(8,128)(2,1)} %bitcast.25, bf16[1,96]{1,0:T(2,128)(2,1)} %refs_4_.1, bf16[1,96]{1,0:T(2,128)(2,1)} %refs_5_.1, ...), custom_call_target="tpu_custom_call" | custom-call | flops 1 | bytes 1083648 | tf_op jit(solution)/shard_map/pack/pallas_call | solution.py:438
  2.7 3.0 %collective-permute-start.1 = (bf16[112,1536]{1,0:T(8,128)(2,1)}, bf16[112,1536]{1,0:T(8,128)(2,1)S(1)}, u32[]{:S(2)}, u32[]{:S(2)}) collective-permute-start(bf16[112,1536]{1,0:T(8,128)(2,1)} %get-tuple-element.88.refs_2_), channel_id=1, source_target_pairs={{0,8},{4,12},{8,0},{12,4},{1,9},{5,13},{9,1},{13,5},{2,10},{6,14},... | collective-permute-start | bytes 1032200 | tf_op jit(solution)/shard_map/ppermute | solution.py:455
  9.3 7.8 %collective-permute-done.2.refs_7_ = bf16[96,768]{1,0:T(8,128)(2,1)S(1)} collective-permute-done((bf16[96,768]{1,0:T(8,128)(2,1)}, bf16[96,768]{1,0:T(8,128)(2,1)S(1)}, u32[]{:S(2)}, u32[]{:S(2)}) %collective-permute-start.2) | collective-permute-done | bytes 147488 | tf_op jit(solution)/shard_map/ppermute | solution.py:455
  17.6 1.7 %collective-permute-start.9 = (bf16[384,384]{1,0:T(8,128)(2,1)S(1)}, bf16[384,384]{1,0:T(8,128)(2,1)S(1)}, u32[]{:S(2)}, u32[]{:S(2)}) collective-permute-start(bf16[384,384]{1,0:T(8,128)(2,1)S(1)} %bitcast.28), channel_id=1, source_target_pairs={{0,8},{4,12},{8,0},{12,4},{1,9},{5,13},{9,1},{13,5},{2,10},{6,14},... | collective-permute-start | bytes 884744 | tf_op jit(solution)/shard_map/ppermute | solution.py:455
  21.0 3.9 %collective-permute-done.5.refs_8_ = bf16[96,768]{1,0:T(8,128)(2,1)S(1)} collective-permute-done((bf16[96,768]{1,0:T(8,128)(2,1)S(1)}, bf16[96,768]{1,0:T(8,128)(2,1)S(1)}, u32[]{:S(2)}, u32[]{:S(2)}) %collective-permute-start.5) | collective-permute-done | bytes 147488 | tf_op jit(solution)/shard_map/ppermute | solution.py:455
  25.4 2.4 %attend.1 = (f32[160,384]{1,0:T(8,128)S(1)}, bf16[160,384]{1,0:T(8,128)(2,1)S(1)}, bf16[384,1152]{1,0:T(8,128)(2,1)S(1)}, bf16[384,384]{1,0:T(8,128)(2,1)S(1)}, ...) custom-call(s32[5]{0:T(128)S(1)} %pad_add_fusion.refs_0_, f32[160,384]{1,0:T(8,128)S(1)} %get-tuple-element.89.refs_1_, ...), custom_call_target="tpu_custom_call" | custom-call | flops 188743680 | bytes 3434496 | tf_op jit(solution)/shard_map/attend/pallas_call | solution.py:438
  29.6 1.8 %feed_forward.1 = (bf16[2,65,384]{2,1,0:T(8,128)(2,1)S(1)}, bf16[384,1536]{1,0:T(8,128)(2,1)S(1)}, bf16[1536,384]{1,0:T(8,128)(2,1)S(1)}) custom-call(s32[5]{0:T(128)S(1)} %pad_add_fusion.refs_0_, bf16[160,384]{1,0:T(8,128)(2,1)S(1)} %get-tuple-element.94.refs_1_, f32[160,384]{1,0:T(8,128)S(1)} %get-tuple-element.95.refs_2_, ...), custom_call_target="tpu_custom_call" | custom-call | flops 377487360 | bytes 5205504 | tf_op jit(solution)/shard_map/feed_forward/pallas_call | solution.py:438
  33.6 2.3 %collective-permute-done.11.refs_2_ = bf16[2,65,384]{2,1,0:T(8,128)(2,1)S(1)} collective-permute-done((bf16[2,65,384]{2,1,0:T(8,128)(2,1)S(1)}, bf16[2,65,384]{2,1,0:T(8,128)(2,1)S(1)}, u32[]{:S(2)}, u32[]{:S(2)}) %collective-permute-start.11) | collective-permute-done | bytes 99872 | tf_op jit(solution)/shard_map/ppermute | solution.py:667
  35.9 4.7 %both_ways.1 = (bf16[2,65,384]{2,1,0:T(8,128)(2,1)S(1)}, bf16[2,65,384]{2,1,0:T(8,128)(2,1)S(1)}, bf16[160,1152]{1,0:T(8,128)(2,1)S(1)}, f32[960,80]{1,0:T(8,128...) custom-call(s32[5]{0:T(128)S(1)} %pad_add_fusion.refs_0_, ...), custom_call_target="tpu_custom_call" | custom-call | flops 1132462080 | bytes 8197376 | tf_op jit(solution)/shard_map/both_ways/pallas_call | solution.py:438
  42.0 5.2 %collective-permute-done.12.refs_1_ = bf16[2,65,384]{2,1,0:T(8,128)(2,1)S(1)} collective-permute-done((bf16[2,65,384]{2,1,0:T(8,128)(2,1)S(1)}, bf16[2,65,384]{2,1,0:T(8,128)(2,1)S(1)}, u32[]{:S(2)}, u32[]{:S(2)}) %collective-permute-start.12) | collective-permute-done | bytes 99872 | tf_op jit(solution)/shard_map/ppermute | solution.py:704
  47.2 4.1 %rest_grad.1 = (bf16[400,384]{1,0:T(8,128)(2,1)S(1)}, bf16[400,384]{1,0:T(8,128)(2,1)S(1)}, bf16[400,384]{1,0:T(8,128)(2,1)S(1)}, bf16[400,384]{1,0:T(8,128)(2,1...) custom-call(s32[5]{0:T(128)S(1)} %pad_add_fusion.refs_0_, ...), custom_call_target="tpu_custom_call" | custom-call | flops 1132462080 | bytes 10550528 | tf_op jit(solution)/shard_map/rest_grad/pallas_call | solution.py:438
  51.4 1.6 %collective-permute-done.13 = bf16[400,384]{1,0:T(8,128)(2,1)S(1)} collective-permute-done((bf16[400,384]{1,0:T(8,128)(2,1)S(1)}, bf16[400,384]{1,0:T(8,128)(2,1)S(1)}, u32[]{:S(2)}, u32[]{:S(2)}) %collective-permute-start.13) | collective-permute-done | bytes 307232 | tf_op jit(solution)/shard_map/ppermute | solution.py:455
  57.5 6.3 %collective-permute-done.15 = bf16[400,384]{1,0:T(8,128)(2,1)S(1)} collective-permute-done((bf16[400,384]{1,0:T(8,128)(2,1)}, bf16[400,384]{1,0:T(8,128)(2,1)S(1)}, u32[]{:S(2)}, u32[]{:S(2)}) %collective-permute-start.15) | collective-permute-done | bytes 307232 | tf_op jit(solution)/shard_map/ppermute | solution.py:455
  64.0 1.7 %collective-permute-start.20 = (bf16[200,384]{1,0:T(8,128)(2,1)S(1)}, bf16[200,384]{1,0:T(8,128)(2,1)S(1)}, u32[]{:S(2)}, u32[]{:S(2)}) collective-permute-start(bf16[200,384]{1,0:T(8,128)(2,1)S(1)} %broadcast_select_fusion.2), channel_id=1, source_target_pairs={{0,1},{1,0},{2,3},{3,2},{4,5},{5,4},{6,7},{7,6},{8,9},{9,8},{10,11... | collective-permute-start | bytes 460808 | tf_op jit(solution)/shard_map/ppermute | solution.py:455
  67.2 2.1 %collective-permute-done.20 = bf16[200,384]{1,0:T(8,128)(2,1)S(1)} collective-permute-done((bf16[200,384]{1,0:T(8,128)(2,1)S(1)}, bf16[200,384]{1,0:T(8,128)(2,1)S(1)}, u32[]{:S(2)}, u32[]{:S(2)}) %collective-permute-start.20) | collective-permute-done | bytes 153632 | tf_op jit(solution)/shard_map/ppermute | solution.py:455
  70.9 2.6 %collective-permute-start.23 = (bf16[200,384]{1,0:T(8,128)(2,1)S(1)}, bf16[200,384]{1,0:T(8,128)(2,1)S(1)}, u32[]{:S(2)}, u32[]{:S(2)}) collective-permute-start(bf16[200,384]{1,0:T(8,128)(2,1)S(1)} %add_convert_fusion.5), channel_id=1, source_target_pairs={{0,2},{1,3},{2,0},{3,1},{4,6},{5,7},{6,4},{7,5},{8,10},{9,11},{10,... | collective-permute-start | bytes 460808 | tf_op jit(solution)/shard_map/ppermute | solution.py:455
  73.5 2.1 %collective-permute-done.18 = bf16[96,1536]{1,0:T(8,128)(2,1)S(1)} collective-permute-done((bf16[96,1536]{1,0:T(8,128)(2,1)S(1)}, bf16[96,1536]{1,0:T(8,128)(2,1)S(1)}, u32[]{:S(2)}, u32[]{:S(2)}) %collective-permute-start.18) | collective-permute-done | bytes 294944 | tf_op jit(solution)/shard_map/ppermute | solution.py:455
  76.2 2.1 %collective-permute-done.23 = bf16[200,384]{1,0:T(8,128)(2,1)S(1)} collective-permute-done((bf16[200,384]{1,0:T(8,128)(2,1)S(1)}, bf16[200,384]{1,0:T(8,128)(2,1)S(1)}, u32[]{:S(2)}, u32[]{:S(2)}) %collective-permute-start.23) | collective-permute-done | bytes 153632 | tf_op jit(solution)/shard_map/ppermute | solution.py:455
  78.3 2.6 %collective-permute-done.22 = bf16[48,1536]{1,0:T(8,128)(2,1)S(1)} collective-permute-done((bf16[48,1536]{1,0:T(8,128)(2,1)S(1)}, bf16[48,1536]{1,0:T(8,128)(2,1)S(1)}, u32[]{:S(2)}, u32[]{:S(2)}) %collective-permute-start.22) | collective-permute-done | bytes 147488 | tf_op jit(solution)/shard_map/ppermute | solution.py:455
  81.1 3.8 %collective-permute-start.26 = (bf16[48,1536]{1,0:T(8,128)(2,1)S(1)}, bf16[48,1536]{1,0:T(8,128)(2,1)S(1)}, u32[]{:S(2)}, u32[]{:S(2)}) collective-permute-start(bf16[48,1536]{1,0:T(8,128)(2,1)S(1)} %add_convert_fusion.6), channel_id=1, source_target_pairs={{0,2},{1,3},{2,0},{3,1},{4,6},{5,7},{6,4},{7,5},{8,10},{9,11},{10,... | collective-permute-start | bytes 442376 | tf_op jit(solution)/shard_map/ppermute | solution.py:455
  85.1 4.3 %collective-permute-start.29 = (bf16[96,384]{1,0:T(8,128)(2,1)S(1)}, bf16[96,384]{1,0:T(8,128)(2,1)S(1)}, u32[]{:S(2)}, u32[]{:S(2)}) collective-permute-start(bf16[96,384]{1,0:T(8,128)(2,1)S(1)} %get-tuple-element.153), channel_id=1, source_target_pairs={{0,3},{1,2},{2,1},{3,0},{4,7},{5,6},{6,5},{7,4},{8,11},{9,10},{10,... | collective-permute-start | bytes 221192 | tf_op jit(solution)/shard_map/ppermute | solution.py:455
  91.7 2.2 %collective-permute-done.28 = bf16[96,384]{1,0:T(8,128)(2,1)S(1)} collective-permute-done((bf16[96,384]{1,0:T(8,128)(2,1)S(1)}, bf16[96,384]{1,0:T(8,128)(2,1)S(1)}, u32[]{:S(2)}, u32[]{:S(2)}) %collective-permute-start.28) | collective-permute-done | bytes 73760 | tf_op jit(solution)/shard_map/ppermute | solution.py:455
  95.3 2.0 %collective-permute-start.31 = (bf16[96,384]{1,0:T(8,128)(2,1)S(1)}, bf16[96,384]{1,0:T(8,128)(2,1)S(1)}, u32[]{:S(2)}, u32[]{:S(2)}) collective-permute-start(bf16[96,384]{1,0:T(8,128)(2,1)S(1)} %reduce-precision_convert_fusion.2), channel_id=1, source_target_pairs={{0,2},{1,3},{2,0},{3,1},{4,6},{5,7},{6,4},{7,5},{8,10},{9,11},{10,... | collective-permute-start | bytes 221192 | tf_op jit(solution)/shard_map/ppermute | solution.py:455
  101.6 2.0 %collective-permute-done.32 = bf16[96,384]{1,0:T(8,128)(2,1)S(1)} collective-permute-done((bf16[96,384]{1,0:T(8,128)(2,1)S(1)}, bf16[96,384]{1,0:T(8,128)(2,1)S(1)}, u32[]{:S(2)}, u32[]{:S(2)}) %collective-permute-start.32) | collective-permute-done | bytes 73760 | tf_op jit(solution)/shard_map/ppermute | solution.py:455
  (87 shorter events, 30.7 us)
Async XLA Ops:
  2.7 14.4 %collective-permute-start.1 = (bf16[112,1536]{1,0:T(8,128)(2,1)}, bf16[112,1536]{1,0:T(8,128)(2,1)S(1)}, u32[]{:S(2)}, u32[]{:S(2)}) collective-permute-start(bf16[112,1536]{1,0:T(8,128)(2,1)} %get-tuple-element.88.refs_2_), channel_id=1, source_target_pairs={{0,8},{4,12},{8,0},{12,4},{1,9},{5,13},{9,1},{13,5},{2,10},{6,14},... | collective-permute-start | bytes 1032200 | tf_op jit(solution)/shard_map/ppermute | solution.py:455
  5.7 11.4 %collective-permute-start.2 = (bf16[96,768]{1,0:T(8,128)(2,1)}, bf16[96,768]{1,0:T(8,128)(2,1)S(1)}, u32[]{:S(2)}, u32[]{:S(2)}) collective-permute-start(bf16[96,768]{1,0:T(8,128)(2,1)} %get-tuple-element.92), channel_id=1, source_target_pairs={{0,8},{4,12},{8,0},{12,4},{1,9},{5,13},{9,1},{13,5},{2,10},{6,14},... | collective-permute-start | bytes 442376 | tf_op jit(solution)/shard_map/ppermute | solution.py:455
  17.1 8.2 %collective-permute-start = (bf16[112,1536]{1,0:T(8,128)(2,1)S(1)}, bf16[112,1536]{1,0:T(8,128)(2,1)S(1)}, u32[]{:S(2)}, u32[]{:S(2)}) collective-permute-start(bf16[112,1536]{1,0:T(8,128)(2,1)S(1)} %copy-done.1), channel_id=1, source_target_pairs={{0,4},{4,0},{8,12},{12,8},{1,5},{5,1},{9,13},{13,9},{2,6},{6,2},{1... | collective-permute-start | bytes 1032200 | tf_op jit(solution)/shard_map/ppermute | solution.py:455
  17.6 10.2 %collective-permute-start.9 = (bf16[384,384]{1,0:T(8,128)(2,1)S(1)}, bf16[384,384]{1,0:T(8,128)(2,1)S(1)}, u32[]{:S(2)}, u32[]{:S(2)}) collective-permute-start(bf16[384,384]{1,0:T(8,128)(2,1)S(1)} %bitcast.28), channel_id=1, source_target_pairs={{0,8},{4,12},{8,0},{12,4},{1,9},{5,13},{9,1},{13,5},{2,10},{6,14},... | collective-permute-start | bytes 884744 | tf_op jit(solution)/shard_map/ppermute | solution.py:455
  19.4 5.5 %collective-permute-start.5 = (bf16[96,768]{1,0:T(8,128)(2,1)S(1)}, bf16[96,768]{1,0:T(8,128)(2,1)S(1)}, u32[]{:S(2)}, u32[]{:S(2)}) collective-permute-start(bf16[96,768]{1,0:T(8,128)(2,1)S(1)} %collective-permute-done.2.refs_7_), channel_id=1, source_target_pairs={{0,1},{1,0},{2,3},{3,2},{4,5},{5,4},{6,7},{7,6},{8,9},{9,8},{10,11... | collective-permute-start | bytes 442376 | tf_op jit(solution)/shard_map/ppermute | solution.py:455
  21.0 6.9 %collective-permute-start.6 = (bf16[96,768]{1,0:T(8,128)(2,1)S(1)}, bf16[96,768]{1,0:T(8,128)(2,1)S(1)}, u32[]{:S(2)}, u32[]{:S(2)}) collective-permute-start(bf16[96,768]{1,0:T(8,128)(2,1)S(1)} %collective-permute-done.2.refs_7_), channel_id=1, source_target_pairs={{0,4},{4,0},{8,12},{12,8},{1,5},{5,1},{9,13},{13,9},{2,6},{6,2},{1... | collective-permute-start | bytes 442376 | tf_op jit(solution)/shard_map/ppermute | solution.py:455
  40.6 6.6 %collective-permute-start.12 = (bf16[2,65,384]{2,1,0:T(8,128)(2,1)S(1)}, bf16[2,65,384]{2,1,0:T(8,128)(2,1)S(1)}, u32[]{:S(2)}, u32[]{:S(2)}) collective-permute-start(bf16[2,65,384]{2,1,0:T(8,128)(2,1)S(1)} %get-tuple-element.106), channel_id=1, source_target_pairs={{16,0},{17,1},{18,2},{19,3},{20,4},{21,5},{22,6},{23,7},{24,8},{25... | collective-permute-start | bytes 299528 | tf_op jit(solution)/shard_map/ppermute | solution.py:704
  53.9 9.9 %collective-permute-start.19 = (bf16[400,384]{1,0:T(8,128)(2,1)S(1)}, bf16[400,384]{1,0:T(8,128)(2,1)S(1)}, u32[]{:S(2)}, u32[]{:S(2)}) collective-permute-start(bf16[400,384]{1,0:T(8,128)(2,1)S(1)} %get-tuple-element.137), channel_id=1, source_target_pairs={{0,4},{4,0},{8,12},{12,8},{1,5},{5,1},{9,13},{13,9},{2,6},{6,2},{1... | collective-permute-start | bytes 921608 | tf_op jit(solution)/shard_map/ppermute | solution.py:455
  54.3 9.5 %collective-permute-start.15 = (bf16[400,384]{1,0:T(8,128)(2,1)}, bf16[400,384]{1,0:T(8,128)(2,1)S(1)}, u32[]{:S(2)}, u32[]{:S(2)}) collective-permute-start(bf16[400,384]{1,0:T(8,128)(2,1)} %add_convert_fusion.1), channel_id=1, source_target_pairs={{0,8},{4,12},{8,0},{12,4},{1,9},{5,13},{9,1},{13,5},{2,10},{6,14},... | collective-permute-start | bytes 921608 | tf_op jit(solution)/shard_map/ppermute | solution.py:455
  64.0 5.3 %collective-permute-start.20 = (bf16[200,384]{1,0:T(8,128)(2,1)S(1)}, bf16[200,384]{1,0:T(8,128)(2,1)S(1)}, u32[]{:S(2)}, u32[]{:S(2)}) collective-permute-start(bf16[200,384]{1,0:T(8,128)(2,1)S(1)} %broadcast_select_fusion.2), channel_id=1, source_target_pairs={{0,1},{1,0},{2,3},{3,2},{4,5},{5,4},{6,7},{7,6},{8,9},{9,8},{10,11... | collective-permute-start | bytes 460808 | tf_op jit(solution)/shard_map/ppermute | solution.py:455
  65.7 9.9 %collective-permute-start.18 = (bf16[96,1536]{1,0:T(8,128)(2,1)S(1)}, bf16[96,1536]{1,0:T(8,128)(2,1)S(1)}, u32[]{:S(2)}, u32[]{:S(2)}) collective-permute-start(bf16[96,1536]{1,0:T(8,128)(2,1)S(1)} %add_convert_fusion.4), channel_id=1, source_target_pairs={{0,8},{4,12},{8,0},{12,4},{1,9},{5,13},{9,1},{13,5},{2,10},{6,14},... | collective-permute-start | bytes 884744 | tf_op jit(solution)/shard_map/ppermute | solution.py:455
  67.2 8.4 %collective-permute-start.14 = (bf16[96,1536]{1,0:T(8,128)(2,1)S(1)}, bf16[96,1536]{1,0:T(8,128)(2,1)S(1)}, u32[]{:S(2)}, u32[]{:S(2)}) collective-permute-start(bf16[96,1536]{1,0:T(8,128)(2,1)S(1)} %get-tuple-element.129), channel_id=1, source_target_pairs={{0,4},{4,0},{8,12},{12,8},{1,5},{5,1},{9,13},{13,9},{2,6},{6,2},{1... | collective-permute-start | bytes 884744 | tf_op jit(solution)/shard_map/ppermute | solution.py:455
  69.2 11.7 %collective-permute-start.21 = (bf16[96,1536]{1,0:T(8,128)(2,1)S(1)}, bf16[96,1536]{1,0:T(8,128)(2,1)S(1)}, u32[]{:S(2)}, u32[]{:S(2)}) collective-permute-start(bf16[96,1536]{1,0:T(8,128)(2,1)S(1)} %add_convert_fusion.3), channel_id=1, source_target_pairs={{0,8},{4,12},{8,0},{12,4},{1,9},{5,13},{9,1},{13,5},{2,10},{6,14},... | collective-permute-start | bytes 884744 | tf_op jit(solution)/shard_map/ppermute | solution.py:455
  70.9 7.5 %collective-permute-start.23 = (bf16[200,384]{1,0:T(8,128)(2,1)S(1)}, bf16[200,384]{1,0:T(8,128)(2,1)S(1)}, u32[]{:S(2)}, u32[]{:S(2)}) collective-permute-start(bf16[200,384]{1,0:T(8,128)(2,1)S(1)} %add_convert_fusion.5), channel_id=1, source_target_pairs={{0,2},{1,3},{2,0},{3,1},{4,6},{5,7},{6,4},{7,5},{8,10},{9,11},{10,... | collective-permute-start | bytes 460808 | tf_op jit(solution)/shard_map/ppermute | solution.py:455
  76.2 8.6 %collective-permute-start.25 = (bf16[96,1536]{1,0:T(8,128)(2,1)S(1)}, bf16[96,1536]{1,0:T(8,128)(2,1)S(1)}, u32[]{:S(2)}, u32[]{:S(2)}) collective-permute-start(bf16[96,1536]{1,0:T(8,128)(2,1)S(1)} %get-tuple-element.148), channel_id=1, source_target_pairs={{0,4},{4,0},{8,12},{12,8},{1,5},{5,1},{9,13},{13,9},{2,6},{6,2},{1... | collective-permute-start | bytes 884744 | tf_op jit(solution)/shard_map/ppermute | solution.py:455
  81.1 12.9 %collective-permute-start.26 = (bf16[48,1536]{1,0:T(8,128)(2,1)S(1)}, bf16[48,1536]{1,0:T(8,128)(2,1)S(1)}, u32[]{:S(2)}, u32[]{:S(2)}) collective-permute-start(bf16[48,1536]{1,0:T(8,128)(2,1)S(1)} %add_convert_fusion.6), channel_id=1, source_target_pairs={{0,2},{1,3},{2,0},{3,1},{4,6},{5,7},{6,4},{7,5},{8,10},{9,11},{10,... | collective-permute-start | bytes 442376 | tf_op jit(solution)/shard_map/ppermute | solution.py:455
  85.0 6.8 %collective-permute-start.27 = (bf16[96,384]{1,0:T(8,128)(2,1)S(1)}, bf16[96,384]{1,0:T(8,128)(2,1)S(1)}, u32[]{:S(2)}, u32[]{:S(2)}) collective-permute-start(bf16[96,384]{1,0:T(8,128)(2,1)S(1)} %get-tuple-element.151), channel_id=1, source_target_pairs={{0,1},{1,0},{2,3},{3,2},{4,5},{5,4},{6,7},{7,6},{8,9},{9,8},{10,11... | collective-permute-start | bytes 221192 | tf_op jit(solution)/shard_map/ppermute | solution.py:455
  85.0 8.9 %collective-permute-start.28 = (bf16[96,384]{1,0:T(8,128)(2,1)S(1)}, bf16[96,384]{1,0:T(8,128)(2,1)S(1)}, u32[]{:S(2)}, u32[]{:S(2)}) collective-permute-start(bf16[96,384]{1,0:T(8,128)(2,1)S(1)} %get-tuple-element.152), channel_id=1, source_target_pairs={{0,2},{1,3},{2,0},{3,1},{4,6},{5,7},{6,4},{7,5},{8,10},{9,11},{10,... | collective-permute-start | bytes 221192 | tf_op jit(solution)/shard_map/ppermute | solution.py:455
  85.1 8.8 %collective-permute-start.29 = (bf16[96,384]{1,0:T(8,128)(2,1)S(1)}, bf16[96,384]{1,0:T(8,128)(2,1)S(1)}, u32[]{:S(2)}, u32[]{:S(2)}) collective-permute-start(bf16[96,384]{1,0:T(8,128)(2,1)S(1)} %get-tuple-element.153), channel_id=1, source_target_pairs={{0,3},{1,2},{2,1},{3,0},{4,7},{5,6},{6,5},{7,4},{8,11},{9,10},{10,... | collective-permute-start | bytes 221192 | tf_op jit(solution)/shard_map/ppermute | solution.py:455
  91.0 8.3 %collective-permute-start.24 = (bf16[200,384]{1,0:T(8,128)(2,1)S(1)}, bf16[200,384]{1,0:T(8,128)(2,1)S(1)}, u32[]{:S(2)}, u32[]{:S(2)}) collective-permute-start(bf16[200,384]{1,0:T(8,128)(2,1)S(1)} %reduce-precision_convert_fusion), channel_id=1, source_target_pairs={{0,1},{1,0},{2,3},{3,2},{4,5},{5,4},{6,7},{7,6},{8,9},{9,8},{10,11... | collective-permute-start | bytes 460808 | tf_op jit(solution)/shard_map/ppermute | solution.py:455
  94.0 7.6 %collective-permute-start.30 = (bf16[96,384]{1,0:T(8,128)(2,1)S(1)}, bf16[96,384]{1,0:T(8,128)(2,1)S(1)}, u32[]{:S(2)}, u32[]{:S(2)}) collective-permute-start(bf16[96,384]{1,0:T(8,128)(2,1)S(1)} %reduce-precision_convert_fusion.2), channel_id=1, source_target_pairs={{0,1},{1,0},{2,3},{3,2},{4,5},{5,4},{6,7},{7,6},{8,9},{9,8},{10,11... | collective-permute-start | bytes 221192 | tf_op jit(solution)/shard_map/ppermute | solution.py:455
  95.3 6.2 %collective-permute-start.31 = (bf16[96,384]{1,0:T(8,128)(2,1)S(1)}, bf16[96,384]{1,0:T(8,128)(2,1)S(1)}, u32[]{:S(2)}, u32[]{:S(2)}) collective-permute-start(bf16[96,384]{1,0:T(8,128)(2,1)S(1)} %reduce-precision_convert_fusion.2), channel_id=1, source_target_pairs={{0,2},{1,3},{2,0},{3,1},{4,6},{5,7},{6,4},{7,5},{8,10},{9,11},{10,... | collective-permute-start | bytes 221192 | tf_op jit(solution)/shard_map/ppermute | solution.py:455
  97.3 6.3 %collective-permute-start.32 = (bf16[96,384]{1,0:T(8,128)(2,1)S(1)}, bf16[96,384]{1,0:T(8,128)(2,1)S(1)}, u32[]{:S(2)}, u32[]{:S(2)}) collective-permute-start(bf16[96,384]{1,0:T(8,128)(2,1)S(1)} %reduce-precision_convert_fusion.2), channel_id=1, source_target_pairs={{0,3},{1,2},{2,1},{3,0},{4,7},{5,6},{6,5},{7,4},{8,11},{9,10},{10,... | collective-permute-start | bytes 221192 | tf_op jit(solution)/shard_map/ppermute | solution.py:455
  98.5 6.6 %collective-permute-start.33 = (bf16[48,1536]{1,0:T(8,128)(2,1)S(1)}, bf16[48,1536]{1,0:T(8,128)(2,1)S(1)}, u32[]{:S(2)}, u32[]{:S(2)}) collective-permute-start(bf16[48,1536]{1,0:T(8,128)(2,1)S(1)} %reduce-precision_convert_fusion.1), channel_id=1, source_target_pairs={{0,1},{1,0},{2,3},{3,2},{4,5},{5,4},{6,7},{7,6},{8,9},{9,8},{10,11... | collective-permute-start | bytes 442376 | tf_op jit(solution)/shard_map/ppermute | solution.py:455
  (14 other events, 74.1 us)
